TPU v7x, 32 devices: a whole 2x2x4 slice. The times are simulated.
32 devices in a mesh: dp: 8 (over y, x, core), tensor: 4 (over z).
Axes of the slice: x: 2, y: 2, z: 4, core: 2. Of those that a mesh axis runs over, the one named last changes fastest.
Arguments:
- tokens: bfloat16 [11664, 1152], P('dp', 'tensor'), may hold values from -6 to 6
- cotangent: bfloat16 [11664, 1152], P('dp', 'tensor'), may hold values from -6 to 6
- adapter_index: int32 [16], P('dp'), may hold values from 0 to 7
- valid_image: int32 [16], P('dp'), may hold values 0 or 1
- first_gain: bfloat16 [1152], replicated, may hold values from 0.5 to 1.5
- first_shift: bfloat16 [1152], replicated, may hold values from -1.5 to 1.5
- triple_weight: bfloat16 [3, 1152, 1152], P(None, None, 'tensor'), may hold values from -0.1875 to 0.1875
- triple_bias: bfloat16 [3, 1152], P(None, 'tensor'), may hold values from -1.5 to 1.5
- triple_down: bfloat16 [3, 8, 1152, 16], replicated, may hold values from -0.1875 to 0.1875
- triple_up: bfloat16 [3, 8, 16, 1152], P(None, None, None, 'tensor'), may hold values from -1.5 to 1.5
- merge_weight: bfloat16 [1152, 1152], P('tensor'), may hold values from -0.75 to 0.75
- merge_bias: bfloat16 [1152], replicated, may hold values from -1.5 to 1.5
- merge_down: bfloat16 [8, 1152, 16], P(None, 'tensor'), may hold values from -0.75 to 0.75
- merge_up: bfloat16 [8, 16, 1152], replicated, may hold values from -1.5 to 1.5
- second_gain: bfloat16 [1152], replicated, may hold values from 0.4 to 8.5
- second_shift: bfloat16 [1152], replicated, may hold values from -1.5 to 1.5
- expand_weight: bfloat16 [1152, 4304], P(None, 'tensor'), may hold values from -0.1875 to 0.1875
- expand_bias: bfloat16 [4304], P('tensor'), may hold values from -1.5 to 1.5
- expand_down: bfloat16 [8, 1152, 16], replicated, may hold values from -0.1875 to 0.1875
- expand_up: bfloat16 [8, 16, 4304], P(None, None, 'tensor'), may hold values from -1.5 to 1.5
- reduce_weight: bfloat16 [4304, 1152], P('tensor'), may hold values from -0.09375 to 0.09375
- reduce_bias: bfloat16 [1152], replicated, may hold values from -1.5 to 1.5
- reduce_down: bfloat16 [8, 4304, 16], P(None, 'tensor'), may hold values from -0.09375 to 0.09375
- reduce_up: bfloat16 [8, 16, 1152], replicated, may hold values from -1.5 to 1.5
Outputs:
- layer_out: bfloat16 [11664, 1152], P('dp', 'tensor')
- tokens_grad: float32 [11664, 1152], P('dp', 'tensor')
- triple_down_grad: float32 [3, 8, 1152, 16], replicated
- triple_up_grad: float32 [3, 8, 16, 1152], P(None, None, None, 'tensor')
- merge_down_grad: float32 [8, 1152, 16], P(None, 'tensor')
- merge_up_grad: float32 [8, 16, 1152], replicated
- expand_down_grad: float32 [8, 1152, 16], replicated
- expand_up_grad: float32 [8, 16, 4304], P(None, None, 'tensor')
- reduce_down_grad: float32 [8, 4304, 16], P(None, 'tensor')
- reduce_up_grad: float32 [8, 16, 1152], replicated
Inputs may be any that keep to these rules, and one draw needn't show every extreme that they name: `valid_image`: padding images carry 0.
All inputs are finite; a program needn't handle non-finite values. No bound on the sum of `valid_image` on one device may be relied on, other than what follows from the above.
Results may differ from a plain program's by a relative error of at most 0.017.
Values may be sent and summed in bfloat16 or wider, within the bound.
No kernel may reach another device: no remote copies, remote signals or barrier semaphores. Data moves between devices by JAX's collectives and lax.ppermute only.
A program may use at most 256 MiB of HBM per device.

v0:
```python
from functools import partial
import math

import jax
import jax.numpy as jnp
from jax import lax
from jax.sharding import PartitionSpec as P

D = 1152
HEAD_DIM = 72
ADAPTERS = 8
SEQ = 729


eps = 1e-06
adapter_scale = 0.5
highest = lax.Precision.HIGHEST


def norm_rows(rows, gain, shift):
    center = rows - jnp.mean(rows, -1, keepdims=True)
    scaled = lax.rsqrt(jnp.mean(center * center, -1, keepdims=True) + eps)
    unit = center * scaled
    return (unit * gain.astype(jnp.float32) + shift.astype(jnp.float32), unit, scaled)


def pick_table(one_hot, table):
    flat = table.reshape(table.shape[0], -1).astype(jnp.float32)
    chosen = jnp.dot(one_hot, flat, precision=highest)
    return chosen.astype(jnp.bfloat16).reshape((one_hot.shape[0],) + table.shape[1:])


def spread_table(one_hot, terms):
    flat = terms.reshape(terms.shape[0], -1)
    summed = jnp.dot(one_hot.T, flat, precision=highest)
    return summed.reshape((one_hot.shape[1],) + terms.shape[1:])


def rank_forward(inputs, down_sel, up_sel):
    inner = jnp.einsum("isd,idr->isr", inputs, down_sel, preferred_element_type=jnp.float32)
    extra = jnp.einsum("isr,iro->iso", inner, up_sel.astype(jnp.float32), precision=highest)
    return (inner, extra)


def rank_backward(inputs, inner, grads, down_sel, up_sel):
    through = jnp.einsum("iso,iro->isr", grads, up_sel, preferred_element_type=jnp.float32)
    up_terms = adapter_scale * jnp.einsum(
        "isr,iso->iro", inner, grads.astype(jnp.float32), precision=highest
    )
    down_terms = adapter_scale * jnp.einsum(
        "isd,isr->idr", inputs.astype(jnp.float32), through, precision=highest
    )
    back = adapter_scale * jnp.einsum(
        "isr,idr->isd", through, down_sel.astype(jnp.float32), precision=highest
    )
    return (back, down_terms, up_terms)


def attend(element):
    query, keys, values = element
    scores = jnp.einsum(
        "qhd,khd->hqk", query, keys, preferred_element_type=jnp.float32
    ) / math.sqrt(HEAD_DIM)
    top = jnp.max(scores, -1, keepdims=True)
    raised = jnp.exp(scores - top)
    total = jnp.sum(raised, -1, keepdims=True)
    attn_weights = (raised / total).astype(jnp.bfloat16)
    heads = jnp.einsum("hqk,khd->qhd", attn_weights, values, preferred_element_type=jnp.float32)
    return (heads.astype(jnp.bfloat16), top + jnp.log(total))


def attend_back(element):
    query, keys, values, log_total, grad_heads = element
    scores = jnp.einsum(
        "qhd,khd->hqk", query, keys, preferred_element_type=jnp.float32
    ) / math.sqrt(HEAD_DIM)
    attn_weights = jnp.exp(scores - log_total)
    grad_weights = jnp.einsum(
        "qhd,khd->hqk", grad_heads, values, preferred_element_type=jnp.float32
    )
    grad_values = jnp.einsum(
        "hqk,qhd->khd",
        attn_weights.astype(jnp.bfloat16),
        grad_heads,
        preferred_element_type=jnp.float32,
    )
    delta = jnp.sum(attn_weights * grad_weights, -1, keepdims=True)
    grad_scores = (attn_weights * (grad_weights - delta)).astype(jnp.bfloat16)
    grad_query = jnp.einsum(
        "hqk,khd->qhd", grad_scores, keys, preferred_element_type=jnp.float32
    ) / math.sqrt(HEAD_DIM)
    grad_keys = jnp.einsum(
        "hqk,qhd->khd", grad_scores, query, preferred_element_type=jnp.float32
    ) / math.sqrt(HEAD_DIM)
    return (
        grad_query.astype(jnp.bfloat16),
        grad_keys.astype(jnp.bfloat16),
        grad_values.astype(jnp.bfloat16),
    )


def sum_pair(shard_first, shard_second, whole_first, whole_second):
    shard_first, shard_second = (
        lax.psum(shard_first.astype(jnp.bfloat16), "dp").astype(jnp.float32),
        lax.psum(shard_second.astype(jnp.bfloat16), "dp").astype(jnp.float32),
    )
    whole_first, whole_second = lax.psum((whole_first, whole_second), ("dp", "tensor"))
    return (shard_first, shard_second, whole_first, whole_second)


def shards(
    tokens,
    cotangent,
    adapter_index,
    valid_image,
    first_gain,
    first_shift,
    triple_weight,
    triple_bias,
    triple_down,
    triple_up,
    merge_weight,
    merge_bias,
    merge_down,
    merge_up,
    second_gain,
    second_shift,
    expand_weight,
    expand_bias,
    expand_down,
    expand_up,
    reduce_weight,
    reduce_bias,
    reduce_down,
    reduce_up,
):
    images = adapter_index.shape[0]
    count = tokens.shape[0]
    width = tokens.shape[1]
    head_width = triple_weight.shape[2]
    heads_here = head_width // HEAD_DIM
    start = lax.axis_index("tensor") * width
    one_hot = (adapter_index[:, None] == jnp.arange(ADAPTERS, dtype=jnp.int32)[None, :]).astype(
        jnp.float32
    )
    keep = valid_image.astype(jnp.float32)

    def local_cols(full):
        return lax.dynamic_slice_in_dim(full, start, width, full.ndim - 1)

    def as_images(flat):
        return flat.reshape(images, SEQ, flat.shape[-1])

    rows = lax.all_gather(tokens, "tensor", axis=1, tiled=True).astype(jnp.float32)
    normed, unit_one, scale_one = norm_rows(rows, first_gain, first_shift)
    act_one = normed.astype(jnp.bfloat16)
    triple_down_sel = [pick_table(one_hot, triple_down[which]) for which in range(3)]
    triple_up_sel = [pick_table(one_hot, triple_up[which]) for which in range(3)]
    projected = []
    inners = []
    for which in range(3):
        inner, extra = rank_forward(
            as_images(act_one), triple_down_sel[which], triple_up_sel[which]
        )
        full_proj = (
            jnp.dot(act_one, triple_weight[which], preferred_element_type=jnp.float32)
            + adapter_scale * extra.reshape(count, head_width)
            + triple_bias[which].astype(jnp.float32)
        )
        projected.append(full_proj.astype(jnp.bfloat16).reshape(images, SEQ, heads_here, HEAD_DIM))
        inners.append(inner)
    heads, log_total = lax.map(attend, (projected[0], projected[1], projected[2]))
    heads_flat = heads.reshape(count, head_width)
    merge_down_sel = pick_table(one_hot, merge_down)
    merge_up_sel = pick_table(one_hot, merge_up)
    inner_merge, extra_merge = rank_forward(as_images(heads_flat), merge_down_sel, merge_up_sel)
    partial_merge = jnp.dot(
        heads_flat, merge_weight, preferred_element_type=jnp.float32
    ) + adapter_scale * extra_merge.reshape(count, D)
    branch = lax.psum(partial_merge, "tensor")
    hidden = rows + branch + merge_bias.astype(jnp.float32)
    hidden_local = local_cols(hidden)
    normed_two, unit_two, scale_two = norm_rows(hidden, second_gain, second_shift)
    act_two = normed_two.astype(jnp.bfloat16)
    expand_down_sel = pick_table(one_hot, expand_down)
    expand_up_sel = pick_table(one_hot, expand_up)
    inner_expand, extra_expand = rank_forward(as_images(act_two), expand_down_sel, expand_up_sel)
    pre_act = (
        jnp.dot(act_two, expand_weight, preferred_element_type=jnp.float32)
        + adapter_scale * extra_expand.reshape(count, -1)
        + expand_bias.astype(jnp.float32)
    )
    gelu_value, gelu_pull = jax.vjp(partial(jax.nn.gelu, approximate=True), pre_act)
    act_three = gelu_value.astype(jnp.bfloat16)
    reduce_down_sel = pick_table(one_hot, reduce_down)
    reduce_up_sel = pick_table(one_hot, reduce_up)
    inner_reduce, extra_reduce = rank_forward(as_images(act_three), reduce_down_sel, reduce_up_sel)
    partial_reduce = jnp.dot(
        act_three, reduce_weight, preferred_element_type=jnp.float32
    ) + adapter_scale * extra_reduce.reshape(count, D)
    share_reduce = lax.psum_scatter(
        partial_reduce.astype(jnp.bfloat16), "tensor", scatter_dimension=1, tiled=True
    ).astype(jnp.float32)
    layer_out = (hidden_local + share_reduce + local_cols(reduce_bias.astype(jnp.float32))).astype(
        jnp.bfloat16
    )
    grad_full = lax.all_gather(cotangent, "tensor", axis=1, tiled=True)
    grad_low = (as_images(grad_full) * keep.astype(jnp.bfloat16)[:, None, None]).reshape(count, D)
    grad_local = (as_images(cotangent.astype(jnp.float32)) * keep[:, None, None]).reshape(
        count, width
    )
    back_reduce, down_terms_reduce, up_terms_reduce = rank_backward(
        as_images(act_three), inner_reduce, as_images(grad_low), reduce_down_sel, reduce_up_sel
    )
    grad_act = jnp.dot(
        grad_low, reduce_weight.T, preferred_element_type=jnp.float32
    ) + back_reduce.reshape(count, -1)
    grad_pre = gelu_pull(grad_act)[0].astype(jnp.bfloat16)
    back_expand, down_terms_expand, up_terms_expand = rank_backward(
        as_images(act_two), inner_expand, as_images(grad_pre), expand_down_sel, expand_up_sel
    )
    grad_normed_two = jnp.dot(
        grad_pre, expand_weight.T, preferred_element_type=jnp.float32
    ) + back_expand.reshape(count, D)
    expand_up_grad = spread_table(one_hot, up_terms_expand)
    reduce_down_grad = spread_table(one_hot, down_terms_reduce)
    expand_down_grad = spread_table(one_hot, down_terms_expand)
    reduce_up_grad = spread_table(one_hot, up_terms_reduce)
    grad_share_two = lax.psum_scatter(
        grad_normed_two.astype(jnp.bfloat16), "tensor", scatter_dimension=1, tiled=True
    ).astype(jnp.float32)
    gain_two = local_cols(second_gain.astype(jnp.float32))
    unit_two_local = local_cols(unit_two)
    scaled_two = grad_share_two * gain_two
    first_sum, second_sum = lax.psum(
        (jnp.sum(scaled_two, -1), jnp.sum(scaled_two * unit_two_local, -1)), "tensor"
    )
    grad_hidden_local = grad_local + scale_two * (
        scaled_two - first_sum[:, None] / D - unit_two_local * second_sum[:, None] / D
    )
    grad_branch = lax.all_gather(
        grad_hidden_local.astype(jnp.bfloat16), "tensor", axis=1, tiled=True
    )
    back_merge, down_terms_merge, up_terms_merge = rank_backward(
        as_images(heads_flat), inner_merge, as_images(grad_branch), merge_down_sel, merge_up_sel
    )
    grad_heads = (
        jnp.dot(grad_branch, merge_weight.T, preferred_element_type=jnp.float32)
        + back_merge.reshape(count, head_width)
    ).astype(jnp.bfloat16)
    grad_triple = lax.map(
        attend_back,
        (
            projected[0],
            projected[1],
            projected[2],
            log_total,
            grad_heads.reshape(images, SEQ, heads_here, HEAD_DIM),
        ),
    )
    grad_normed_one = jnp.zeros((count, D), jnp.float32)
    down_list = []
    up_list = []
    for which in range(3):
        grad_flat = grad_triple[which].reshape(count, head_width)
        back_part, down_part, up_part = rank_backward(
            as_images(act_one),
            inners[which],
            as_images(grad_flat),
            triple_down_sel[which],
            triple_up_sel[which],
        )
        grad_normed_one = (
            grad_normed_one
            + jnp.dot(grad_flat, triple_weight[which].T, preferred_element_type=jnp.float32)
            + back_part.reshape(count, D)
        )
        down_list.append(spread_table(one_hot, down_part))
        up_list.append(spread_table(one_hot, up_part))
    grad_share_one = lax.psum_scatter(
        grad_normed_one.astype(jnp.bfloat16), "tensor", scatter_dimension=1, tiled=True
    ).astype(jnp.float32)
    gain_one = local_cols(first_gain.astype(jnp.float32))
    unit_one_local = local_cols(unit_one)
    scaled_one = grad_share_one * gain_one
    third_sum, fourth_sum = lax.psum(
        (jnp.sum(scaled_one, -1), jnp.sum(scaled_one * unit_one_local, -1)), "tensor"
    )
    tokens_grad = grad_hidden_local + scale_one * (
        scaled_one - third_sum[:, None] / D - unit_one_local * fourth_sum[:, None] / D
    )
    triple_up_grad, merge_down_grad, triple_down_grad, merge_up_grad = sum_pair(
        jnp.stack(up_list),
        spread_table(one_hot, down_terms_merge),
        jnp.stack(down_list),
        spread_table(one_hot, up_terms_merge),
    )
    expand_up_grad, reduce_down_grad, expand_down_grad, reduce_up_grad = sum_pair(
        expand_up_grad, reduce_down_grad, expand_down_grad, reduce_up_grad
    )
    return (
        layer_out,
        tokens_grad,
        triple_down_grad,
        triple_up_grad,
        merge_down_grad,
        merge_up_grad,
        expand_down_grad,
        expand_up_grad,
        reduce_down_grad,
        reduce_up_grad,
    )


def solution(mesh):
    in_specs = (
        P("dp", "tensor"),
        P("dp", "tensor"),
        P("dp"),
        P("dp"),
        P(),
        P(),
        P(None, None, "tensor"),
        P(None, "tensor"),
        P(),
        P(None, None, None, "tensor"),
        P("tensor", None),
        P(),
        P(None, "tensor", None),
        P(),
        P(),
        P(),
        P(None, "tensor"),
        P("tensor"),
        P(),
        P(None, None, "tensor"),
        P("tensor", None),
        P(),
        P(None, "tensor", None),
        P(),
    )
    out_specs = (
        P("dp", "tensor"),
        P("dp", "tensor"),
        P(),
        P(None, None, None, "tensor"),
        P(None, "tensor", None),
        P(),
        P(),
        P(None, None, "tensor"),
        P(None, "tensor", None),
        P(),
    )
    return jax.shard_map(shards, mesh=mesh, in_specs=in_specs, out_specs=out_specs, check_vma=False)
```

profile of v0, /device:TPU:0, one launch (start us, length us, event | category | flops | bytes accessed | tf_op | source)
XLA Modules:
  0.0 1211.1 jit_solution(5400152676511726444)
XLA Ops:
  15.1 5.9 reshape_squeeze.18
  30.4 6.7 reshape_squeeze.20
  45.0 5.9 reshape_squeeze.22
  59.1 23.2 %all-gather.4.cloned.1.call-done = bf16[1458,1152]{0,1:T(8,128)(2,1)} async-done(((bf16[1458,288]{0,1:T(8,128)(2,1)}), bf16[1458,1152]{0,1:T(8,128)(2,1)}) %all-gather.4.cloned.1.call-update) | async-done | bytes 3359248 | tf_op jit(solution)/shard_map/all_gather | solution.py:154
  82.3 5.7 copy.245
  92.7 5.0 fusion.60
  97.7 4.5 reshape.311
  112.4 5.0 fusion.91
  151.7 5.0 fusion.93
  163.4 14.6 %while.26 = (s32[]{:T(128)}, bf16[2,729,4,72]{1,3,2,0:T(8,128)(2,1)}, f32[2,4,729,1]{2,1,3,0:T(4,128)}, bf16[2,729,4,72]{1,3,2,0:T(8,128)(2,1)}, bf16[2,729,4,72...) while((s32[]{:T(128)}, bf16[2,729,4,72]{1,3,2,0:T(8,128)(2,1)}, ...), condition=%wide.region_5.6_spmd, body=%wide.region_2.5_spmd.sunk | while | flops 631558912 | bytes 37994652 | solution.py:172
  183.4 5.8 convolution_multiply_fusion.9
  189.2 6.4 mul.288
  198.3 8.1 convolution_add_fusion
  217.5 5.9 reshape.327
  231.8 9.4 reshape.365
  241.2 10.6 copy.339
  257.8 19.0 %copy.271 = f32[2,729,1076]{1,0,2:T(2,128)} copy(f32[2,729,1076]{1,2,0:T(8,128)S(1)} %convolution_multiply_fusion.2) | data formatting | bytes 12550464 | tf_op jit(solution)/shard_map/mul | solution.py:53
  276.7 9.7 reshape.337
  286.5 156.0 %all-reduce.8.cloned.1.call-done = f32[1458,1152]{1,0:T(8,128)} async-done(((f32[1458,1152]{1,0:T(8,128)}), f32[1458,1152]{1,0:T(8,128)}) %all-reduce.8.cloned.1.call-update) | async-done | bytes 6718480 | tf_op jit(solution)/shard_map/psum | solution.py:180
  442.5 4.9 fusion.181
  450.1 4.8 add_convert_fusion
  465.2 19.0 %copy.263 = f32[2,729,1076]{1,0,2:T(2,128)} copy(f32[2,729,1076]{1,2,0:T(8,128)S(1)} %convolution_multiply_fusion.3) | data formatting | bytes 12550464 | tf_op jit(solution)/shard_map/mul | solution.py:190
  484.1 9.7 mul.296
  493.8 10.6 multiply_convert_fusion.1
  504.4 11.8 fusion.73
  516.2 8.9 reshape.338
  527.6 5.2 convolution_multiply_fusion.7
  532.8 6.4 reshape.339
  539.2 10.3 fusion.63
  549.5 5.8 copy.343
  557.9 62.8 %reduce-scatter.12.cloned.1.call-done = bf16[288,1458]{1,0:T(8,128)(2,1)} async-done(((bf16[1152,1458]{1,0:T(8,128)(2,1)}), bf16[288,1458]{1,0:T(8,128)(2,1)}) %reduce-scatter.12.cloned.1.call-update) | async-done | bytes 839824
  625.9 17.8 %all-reduce.2 = (f32[1458]{0:T(1024)S(1)}, f32[1458]{0:T(1024)S(1)}) all-reduce(f32[1458]{0:T(1024)S(1)} %get-tuple-element.200, f32[1458]{0:T(1024)S(1)} %get-tuple-element.199), channel_id=1, replica_groups=mesh['dp'=8,'tensor'=4] {'tensor'}, use_global_device_ids=true, to_apply=%region_14.15 | all-reduce | flops 2916 | bytes 23328 | tf_op jit(solution)/shard_map/psum | solution.py:235
  650.6 9.0 reshape.331
  662.2 4.8 convolution_multiply_fusion.8
  666.9 6.6 mul.302
  673.5 10.2 fusion.62
  683.8 5.9 copy.341
  695.0 4.6 fusion.98
  700.0 4.6 fusion.95
  719.0 9.9 reshape.366
  729.0 10.4 copy.340
  758.0 58.3 %while.27 = (s32[]{:T(128)}, bf16[2,729,4,72]{1,3,2,0:T(8,128)(2,1)}, bf16[2,729,4,72]{1,3,2,0:T(8,128)(2,1)}, bf16[2,729,4,72]{1,3,2,0:T(8,128)(2,1)}, bf16[2,7...) while((s32[]{:T(128)}, ...), condition=%wide.region_17.18_spmd, body=%wide.region_15.17_spmd.sunk | while | flops 1557106048 | bytes 148009760 | solution.py:251
  759.6 5.2 multiply_reduce_fusion.8
  765.7 10.2 multiply_convert_fusion.3
  780.0 4.7 fusion.325
  788.7 5.2 multiply_reduce_fusion.8
  794.8 10.2 multiply_convert_fusion.3
  809.1 4.6 fusion.325
  819.8 5.3 convolution_multiply_fusion.6
  825.0 6.4 reshape.344
  831.4 8.2 copy.285
  893.7 8.2 convolution_add_fusion.3
  904.3 5.3 convolution_multiply_fusion.4
  910.6 5.4 convolution_multiply_fusion.5
  917.9 6.4 reshape.348
  924.3 7.9 copy.291
  932.2 6.4 reshape.346
  938.6 8.0 copy.288
  948.0 7.7 fusion.57
  955.7 7.6 fusion.74
  978.8 126.3 %all-reduce.10.cloned.1.call-done = (f32[3,8,1152,16]{2,1,3,0:T(8,128)}, f32[8,16,1152]{2,0,1:T(8,128)}, f32[8,1152,16]{1,0,2:T(8,128)}, f32[8,16,1152]{2,0,1:T(8,128)}) async-done(((f32[3,8,1152,16]{2,1,3,0:T(8,128)}, f32[8,16,1152]{2,0,1:T(8,128)}, f32[8,1152,16]{1,0,2:T(8,128)}, f32[8,16,1152]{2,0,1:T(8,128)}), (f32[3,8,1152,16]{2,1,3,0:T(8,128)}, f32[8,16,1152]{2,0,1:T(8,128)}, ...) | async-done | bytes 3538960 | tf_op jit(solution)/shard_map/psum | solution.py:107
  1111.0 61.9 %reduce-scatter.14.cloned.1.call-done = bf16[288,1458]{1,0:T(8,128)(2,1)} async-done(((bf16[1152,1458]{1,0:T(8,128)(2,1)}), bf16[288,1458]{1,0:T(8,128)(2,1)}) %reduce-scatter.14.cloned.1.call-update) | async-done | bytes 839824
  1179.1 17.5 %all-reduce.1 = (f32[1458]{0:T(1024)S(1)}, f32[1458]{0:T(1024)S(1)}) all-reduce(f32[1458]{0:T(1024)S(1)} %get-tuple-element.198, f32[1458]{0:T(1024)S(1)} %get-tuple-element.197), channel_id=1, replica_groups=mesh['dp'=8,'tensor'=4] {'tensor'}, use_global_device_ids=true, to_apply=%region_22.23 | all-reduce | flops 2916 | bytes 23328 | tf_op jit(solution)/shard_map/psum | solution.py:286
  1196.7 4.8 multiply_add_fusion
  (413 shorter events, 319.9 us)
Async XLA Ops:
  7.2 486.6 %copy-start = (bf16[1152,1076]{0,1:T(8,128)(2,1)S(1)}, bf16[1152,1076]{0,1:T(8,128)(2,1)}, u32[]{:S(2)}) copy-start(bf16[1152,1076]{0,1:T(8,128)(2,1)} %param.44) | copy-start | bytes 7437316
  7.2 75.1 %all-gather.4.cloned.1.call-start = ((), (), s32[]{:S(2)}) async-start(), calls=%async_computation.3 | async-start | bytes 4423680 | tf_op jit(solution)/shard_map/all_gather | solution.py:154
  7.9 223.8 %all-gather.6.cloned.1.call-start = ((), (), s32[]{:S(2)}) async-start(), calls=%async_computation.5 | async-start | bytes 4423680 | tf_op jit(solution)/shard_map/all_gather | solution.py:207
  8.7 433.8 %all-reduce.8.cloned.1.call-start = ((), (), s32[]{:S(2)}) async-start(), calls=%async_computation.4 | async-start | bytes 13492224 | tf_op jit(solution)/shard_map/psum | solution.py:180
  11.3 9.7 copy-start.60
  13.2 13.7 %copy-start.72 = (bf16[3,288]{1,0:T(4,128)(2,1)S(1)}, bf16[3,288]{1,0:T(4,128)(2,1)}, u32[]{:S(2)}) copy-start(bf16[3,288]{1,0:T(4,128)(2,1)} %param.35) | copy-start | bytes 5188
  21.7 80.4 %copy-start.20 = (bf16[2,1152,16]{2,1,0:T(8,128)(2,1)}, bf16[2,1152,16]{2,1,0:T(8,128)(2,1)S(1)}, u32[]{:S(2)}) copy-start(bf16[2,1152,16]{2,1,0:T(8,128)(2,1)S(1)} %reshape.312) | copy-start | bytes 221188
  52.9 90.9 %copy-start.56 = (bf16[2,16,288]{2,1,0:T(8,128)(2,1)}, bf16[2,16,288]{2,1,0:T(8,128)(2,1)S(1)}, u32[]{:S(2)}) copy-start(bf16[2,16,288]{2,1,0:T(8,128)(2,1)S(1)} %reshape.319) | copy-start | bytes 55300
  105.2 7.2 copy-start.37
  106.1 6.3 copy-start.81
  117.3 5.9 copy-start.23
  117.3 8.8 copy-start.58
  126.2 7.4 copy-start.39
  127.1 6.4 copy-start.80
  145.4 6.3 copy-start.79
  178.0 11.1 copy-start.6
  206.5 8.4 copy-start.75
  206.5 9.0 copy-start.76
  206.5 9.0 copy-start.68
  206.5 9.0 copy-start.77
  206.6 9.0 copy-start.51
  206.6 414.1 %reduce-scatter.12.cloned.1.call-start = ((), (), s32[]{:S(2)}) async-start(), calls=%async_computation.8 | async-start | bytes 4423680
  215.6 13.4 %copy-start.85 = (s32[2]{0:T(128)S(1)}, s32[2]{0:T(128)}, u32[]{:S(2)}) copy-start(s32[2]{0:T(128)} %param.31) | copy-start | bytes 28
  241.2 10.6 copy-start.52
  241.2 10.6 copy-start.74
  484.1 9.7 copy-start.71
  493.8 10.6 copy-start.25
  493.8 10.6 copy-start.78
  493.8 10.6 copy-start.83
  555.3 163.8 %all-gather.8.cloned.1.call-start = ((), (), s32[]{:S(2)}) async-start(), calls=%async_computation.6 | async-start | bytes 4423680 | tf_op jit(solution)/shard_map/all_gather | solution.py:241
  650.5 9.1 copy-start.30
  650.6 314.3 %reduce-scatter.10.cloned.1.call-start = ((), (), s32[]{:S(2)}) async-start(), calls=%async_computation.7 | async-start | bytes 4423680
  666.9 6.6 copy-start.84
  683.8 6.0 copy-start.49
  694.2 5.9 copy-start.63
  715.2 256.5 %all-reduce.12.cloned.1.call-start = ((), (), s32[]{:S(2)}) async-start(), calls=%async_computation.11 | async-start | bytes 1966080 | tf_op jit(solution)/shard_map/psum | solution.py:104
  729.0 10.4 copy-start.44
  751.9 6.1 copy-start.7
  751.9 6.1 copy-start.8
  751.9 6.1 copy-start.61
  757.9 60.4 %copy-start.59 = (bf16[2,16,288]{2,1,0:T(8,128)(2,1)S(1)}, bf16[2,16,288]{2,1,0:T(8,128)(2,1)}, u32[]{:S(2)}) copy-start(bf16[2,16,288]{2,1,0:T(8,128)(2,1)} %reshape.316) | copy-start | bytes 55300
  758.0 61.8 %copy-start.24 = (bf16[2,1152,16]{2,1,0:T(8,128)(2,1)S(1)}, bf16[2,1152,16]{2,1,0:T(8,128)(2,1)}, u32[]{:S(2)}) copy-start(bf16[2,1152,16]{2,1,0:T(8,128)(2,1)} %reshape.315) | copy-start | bytes 221188
  759.6 6.2 copy-start.2
  775.9 8.8 copy-start.3
  788.7 6.1 copy-start.2
  805.0 8.7 copy-start.3
  831.4 9.8 copy-start.13
  831.4 9.8 copy-start.55
  841.4 8.2 copy-start.35
  844.9 7.0 copy-start.10
  844.9 7.0 copy-start.57
  866.0 7.1 copy-start.38
  866.1 8.1 copy-start.42
  867.5 7.8 copy-start.9
  867.5 7.8 copy-start.40
  869.4 6.9 copy-start.34
  875.2 12.8 %copy-start.32 = (f32[2,729,16]{1,2,0:T(8,128)S(1)}, f32[2,729,16]{1,2,0:T(8,128)}, u32[]{:S(2)}) copy-start(f32[2,729,16]{1,2,0:T(8,128)} %copy-done.31) | copy-start | bytes 279940
  888.1 5.7 copy-start.19
  893.7 10.5 copy-start.21
  893.7 10.5 copy-start.36
  901.9 203.2 %all-reduce.10.cloned.1.call-start = ((), (), s32[]{:S(2)}) async-start(), calls=%async_computation.10 | async-start | bytes 7077888 | tf_op jit(solution)/shard_map/psum | solution.py:107
  909.6 263.4 %reduce-scatter.14.cloned.1.call-start = ((), (), s32[]{:S(2)}) async-start(), calls=%async_computation.9 | async-start | bytes 4423680
  1110.1 86.6 %copy-start.65 = (f32[1458]{0:T(1024)S(1)}, f32[1458]{0:T(1024)}, u32[]{:S(2)}) copy-start(f32[1458]{0:T(1024)} %copy-done.64) | copy-start | bytes 17500
  1196.6 7.7 copy-start.1
  (39 other events, 96.9 us)
Sparse Core Ops, SparseCore 0:
  9.6 72.6 all-gather.3
  83.9 68.5 all-gather.5
  206.6 235.7 all-reduce.7
  555.4 65.2 reduce-scatter.11
  650.7 68.3 all-gather.7
  721.3 64.9 reduce-scatter.9
  902.1 55.0 all-reduce.11
  965.3 139.7 all-reduce.9
  1107.4 65.4 reduce-scatter.13
where the time goes:
time: 1220 us; the launch traced here: 1210 us
  waiting for transfers between devices  436 us (36%)
  local copies, waits for them, and re-layouts  393 us (32%)
  matrix products  261 us (21%)
  other arithmetic  69.1 us (6%)
  blocking collectives  35.4 us (3%)
  between operations  15.2 us (1%)
    psum x1, waiting for transfers between devices, shards(): branch = lax.psum(partial_merge, 'tensor')  156 us
    psum x1, waiting for transfers between devices, sum_pair(): lax.psum((whole_first, whole_second), ('dp', 'tensor'))  126 us
    unnamed x12, waiting for transfers between devices  126 us
    reshape x8, local copies, waits for them, and re-layouts, as_images(): return flat.reshape(images, SEQ, flat.shape[-1])  67.1 us
    unnamed x177, local copies, waits for them, and re-layouts  55.4 us
    reshape x6, local copies, waits for them, and re-layouts, shards(): back_part.reshape(count, D)  43.3 us
    mul x2, local copies, waits for them, and re-layouts, shards(): adapter_scale * extra_expand.reshape(count, -1)  28.6 us
    dot_general x6, matrix products, rank_backward(): jnp.einsum('isr,idr->isd', through, down_sel.astype(jnp.float32), precisi...  24.9 us
  transfers between devices with their start and end apart: 9, of which 6 were waited for; matrix products, arithmetic and copies ran while one was open for 47% of the time, Pallas kernels for 0%

commit v1 on v0

v1 whole, which is shorter than its diff:
```python
import math
from functools import partial

import jax
import jax.numpy as jnp
from jax import lax
from jax.experimental import pallas as pl
from jax.experimental.pallas import tpu as pltpu
from jax.sharding import PartitionSpec as P

HEAD_DIM = 72
HEAD_PAD = 80
LANES = 128
CHUNK = 256
EPS = 1e-06
BF = jnp.bfloat16
F32 = jnp.float32
SCALE = 1.0 / math.sqrt(HEAD_DIM)
LOG2E = 1.4426950408889634
MIB = 1024 * 1024

NN = (((1,), (0,)), ((), ()))
NT = (((1,), (1,)), ((), ()))
TN = (((0,), (0,)), ((), ()))


def mm(a, b, dims=NN):
    return lax.dot_general(a, b, dims, preferred_element_type=F32)


def up_to(value, step):
    return -(-value // step) * step


def attend_kernel(seq, slots, groups, tok_ref, norm_ref, down_ref, upx_ref, *rest):
    weights = rest[:slots]
    qkv_ref, n1_ref, stats_ref, lse_ref, inner_ref, heads_ref, rows_ref = rest[slots : slots + 7]
    (scr,) = rest[slots + 7 :]
    parts, width, span = tok_ref.shape
    dim = parts * width
    head_rows = upx_ref.shape[2] // 3
    heads_here = head_rows // HEAD_DIM
    block = span // groups

    def norm_step(c, carry):
        cols = pl.ds(pl.multiple_of(c * LANES, LANES), LANES)
        x = tok_ref[:, :, cols].reshape(dim, LANES).astype(F32)
        mean = jnp.mean(x, 0, keepdims=True)
        center = x - mean
        rstd = lax.rsqrt(jnp.mean(center * center, 0, keepdims=True) + EPS)
        n1 = center * rstd * norm_ref[:, 0:1] + norm_ref[:, 1:2]
        n1_ref[:, cols] = n1.astype(BF)
        stats_ref[0:1, cols] = mean
        stats_ref[1:2, cols] = rstd
        return carry

    lax.fori_loop(0, span // LANES, norm_step, 0)
    stats_ref[2:8, :] = jnp.zeros((6, span), F32)

    def proj_step(c, carry):
        start = pl.multiple_of(c * CHUNK, CHUNK)
        cols = pl.ds(start, CHUNK)
        n1 = n1_ref[:, cols]
        rank = down_ref.shape[0]
        inner = mm(down_ref[...], n1)
        line = lax.broadcasted_iota(jnp.int32, (rank, CHUNK), 0)
        inner_x = jnp.where(line == 48, 1.0, 0.5 * inner).astype(BF)
        inner_ref[:, cols] = inner_x
        spot = lax.broadcasted_iota(jnp.int32, (HEAD_PAD - HEAD_DIM, CHUNK), 0)
        place = start + lax.broadcasted_iota(jnp.int32, (HEAD_PAD - HEAD_DIM, CHUNK), 1)
        tails = (
            jnp.where(spot == 0, 1.0, 0.0),
            jnp.where((spot == 0) & (place >= seq), -1e30, 0.0),
            jnp.zeros((HEAD_PAD - HEAD_DIM, CHUNK), F32),
        )
        for k in range(slots):
            proj = mm(weights[k][0 : 3 * head_rows, :], n1) + mm(upx_ref[k], inner_x, TN)
            for j in range(3):
                for h in range(heads_here):
                    at = j * head_rows + h * HEAD_DIM
                    piece = jnp.concatenate([proj[at : at + HEAD_DIM, :], tails[j]], 0)
                    qkv_ref[j, k * heads_here + h, :, cols] = piece.astype(BF)
        return carry

    lax.fori_loop(0, span // CHUNK, proj_step, 0)

    def head_step(h, carry):
        keys = qkv_ref[1, h].T
        vals = qkv_ref[2, h]
        row = pl.multiple_of(h * HEAD_DIM, 8)
        for c in range(span // CHUNK):
            cols = slice(c * CHUNK, (c + 1) * CHUNK)
            scores = mm(keys, qkv_ref[0, h, :, cols]) * (SCALE * LOG2E)
            top = jnp.max(scores, 0, keepdims=True)
            raised = jnp.exp2(scores - top)
            total = jnp.sum(raised, 0, keepdims=True)
            out = mm(vals, raised.astype(BF)) / total
            scr[pl.ds(row, HEAD_DIM), cols] = out[0:HEAD_DIM, :]
            lse_ref[pl.ds(h, 1), 0:1, cols] = (top + jnp.log2(total)).reshape(1, 1, CHUNK)
        return carry

    lax.fori_loop(0, slots * heads_here, head_step, 0)
    for g in range(groups):
        cols = slice(g * block, (g + 1) * block)
        rows_ref[g] = tok_ref[:, :, cols].reshape(dim, block)
        for k in range(slots):
            heads_ref[g, k] = scr[k * head_rows : (k + 1) * head_rows, cols].astype(BF)


def attend(seq, groups, tok, norm, down, upx, weights):
    parts, width, span = tok.shape
    slots = len(weights)
    head_rows = upx.shape[2] // 3
    heads = slots * head_rows // HEAD_DIM
    dim = parts * width
    out = (
        jax.ShapeDtypeStruct((3, heads, HEAD_PAD, span), BF),
        jax.ShapeDtypeStruct((dim, span), BF),
        jax.ShapeDtypeStruct((8, span), F32),
        jax.ShapeDtypeStruct((heads, 1, span), F32),
        jax.ShapeDtypeStruct((down.shape[0], span), BF),
        jax.ShapeDtypeStruct((groups, slots, head_rows, span // groups), BF),
        jax.ShapeDtypeStruct((groups, dim, span // groups), BF),
    )
    return pl.pallas_call(
        partial(attend_kernel, seq, slots, groups),
        out_shape=out,
        in_specs=[pl.BlockSpec(memory_space=pltpu.VMEM)] * (4 + slots),
        out_specs=tuple(pl.BlockSpec(memory_space=pltpu.VMEM) for _ in out),
        scratch_shapes=[pltpu.VMEM((slots * head_rows, span), F32)],
        compiler_params=pltpu.CompilerParams(vmem_limit_bytes=48 * MIB),
        cost_estimate=pl.CostEstimate(flops=8 * 10**9, bytes_accessed=16 * 10**6, transcendentals=5 * 10**6),
        name="attend",
    )(tok, norm, down, upx, *weights)


def middle_kernel(
    sc,
    heads_ref,
    rows_ref,
    cot_ref,
    fac_ref,
    vec_ref,
    tab_ref,
    merge_hbm,
    mlp_hbm,
    pair_ref,
    back_ref,
    gm_ref,
    we,
    wr,
    wm,
    heads_in,
    acc_out,
    acc_back,
    n2x,
    gx,
    eug,
    rdg,
    sem,
):
    groups, slots, head_rows, block = heads_ref.shape
    parts = cot_ref.shape[0]
    dim = parts * head_rows
    hidden_rows = fac_ref.shape[3]
    full = parts * hidden_rows
    tail = slice(dim, dim + LANES)
    mine, member, valid = sc[0], sc[1], sc[2]

    copies = []
    for t in range(parts):
        copies.append(
            pltpu.make_async_copy(
                merge_hbm.at[t, pl.ds(0, head_rows), :],
                wm.at[pl.ds(t * head_rows, head_rows), pl.ds(0, dim)],
                sem.at[0, t],
            )
        )
    for t in range(parts):
        for which, dest in ((0, we), (1, wr)):
            copies.append(
                pltpu.make_async_copy(
                    mlp_hbm.at[t, pl.ds(which * hidden_rows, hidden_rows), :],
                    dest.at[pl.ds(t * hidden_rows, hidden_rows), pl.ds(0, dim)],
                    sem.at[1 + which, t],
                )
            )
    for copy in copies:
        copy.start()

    for s in range(groups):
        for k in range(slots):
            heads_in[s + groups * lax.rem(mine + k, slots)] = heads_ref[s, k]
    heads_t = heads_in[...].reshape(dim, block)
    heads = heads_t.T
    grads = cot_ref[...].reshape(dim, block).T * valid.astype(F32).astype(BF)

    for t in range(parts):
        fac = fac_ref[t, mine]
        spread = jnp.concatenate(
            [fac[0:16, :], fac[48:64, :], jnp.zeros((LANES - 32, hidden_rows), BF)], 0
        )
        we[t * hidden_rows : (t + 1) * hidden_rows, tail] = spread.T
        spread = jnp.concatenate([fac[16:32, :], jnp.zeros((LANES - 16, hidden_rows), BF)], 0)
        wr[t * hidden_rows : (t + 1) * hidden_rows, tail] = spread.T
        spread = jnp.concatenate(
            [fac[32:48, 0:head_rows], jnp.zeros((LANES - 16, head_rows), BF)], 0
        )
        wm[t * head_rows : (t + 1) * head_rows, tail] = spread.T

    for copy in copies[:parts]:
        copy.wait()
    merged = mm(heads, wm[...])
    inner_m = (0.5 * merged[:, tail]).astype(BF)
    x = rows_ref[member].T.astype(F32)
    hidden = x + merged[:, :dim] + mm(inner_m, tab_ref[0]) + vec_ref[0:1, :]
    mean = jnp.mean(hidden, 1, keepdims=True)
    center = hidden - mean
    rstd = lax.rsqrt(jnp.mean(center * center, 1, keepdims=True) + EPS)
    unit = center * rstd
    n2 = (unit * vec_ref[2:3, :] + vec_ref[3:4, :]).astype(BF)
    n2x[:, 0:dim] = n2
    lane = lax.broadcasted_iota(jnp.int32, (block, LANES), 1)
    inner_e = jnp.where(lane == 16, 1.0, 0.5 * mm(n2, tab_ref[1], NT)).astype(BF)
    n2x[:, tail] = inner_e
    gx[:, 0:dim] = grads
    thr_r = (0.5 * mm(grads, tab_ref[2], NT)).astype(BF)
    gx[:, tail] = thr_r
    inner_et = inner_e.T
    thr_rt = thr_r.T
    acc_out[...] = jnp.zeros_like(acc_out)
    acc_back[...] = jnp.zeros_like(acc_back)
    for copy in copies[parts:]:
        copy.wait()

    def step(c, carry):
        at = pl.ds(pl.multiple_of(c * CHUNK, CHUNK), CHUNK)
        we_c = we[at, :]
        wr_c = wr[at, :]
        pre = mm(n2x[...], we_c, NT)
        grad_act = mm(gx[...], wr_c, NT)
        square = pre * pre
        th = jnp.tanh(pre * (0.7978845608028654 + 0.035677408136300125 * square))
        half = 0.5 * (1.0 + th)
        act = (pre * half).astype(BF)
        slope = half + pre * (0.5 * (1.0 - th * th)) * (
            0.7978845608028654 + 0.10703222440890037 * square
        )
        grad_pre = (grad_act * slope).astype(BF)
        acc_out[...] += mm(act, wr_c)
        acc_back[...] += mm(grad_pre, we_c)
        eug[:, at] = mm(inner_et[0:16, :], grad_pre)
        rdg[:, at] = mm(thr_rt[0:16, :], act)
        return carry

    lax.fori_loop(0, full // CHUNK, step, 0)

    inner_r = (0.5 * acc_out[:, tail]).astype(BF)
    layer = hidden + acc_out[:, 0:dim] + mm(inner_r, tab_ref[2]) + vec_ref[1:2, :]
    thr_e = (0.5 * acc_back[:, tail]).astype(BF)
    scaled = (acc_back[:, 0:dim] + mm(thr_e, tab_ref[1])) * vec_ref[2:3, :]
    first = jnp.mean(scaled, 1, keepdims=True)
    second = jnp.mean(scaled * unit, 1, keepdims=True)
    grad_hidden = grads.astype(F32) + rstd * (scaled - first - unit * second)
    branch = grad_hidden.astype(BF)
    thr_m = (0.5 * mm(branch, tab_ref[0], NT)).astype(BF)
    grad_heads = mm(branch, wm[:, 0:dim], NT) + mm(thr_m, wm[:, tail], NT)
    grad_heads_t = grad_heads.T.astype(BF)
    layer_t = layer.T.astype(BF)
    hidden_t = grad_hidden.T.astype(BF)
    for t in range(parts):
        at = slice(t * head_rows, (t + 1) * head_rows)
        pair_ref[t, 0] = layer_t[at, :]
        pair_ref[t, 1] = hidden_t[at, :]
        back_ref[t % groups, lax.rem(t // groups - mine + slots, slots)] = grad_heads_t[at, :]

    whole = (
        mm(thr_m, heads, TN)[0:16, :],
        mm(inner_m, branch, TN)[0:16, :],
        mm(thr_e, n2, TN)[0:16, :],
        mm(inner_r, grads, TN)[0:16, :],
    )
    for t in range(parts):
        at = slice(t * hidden_rows, (t + 1) * hidden_rows)
        gm_ref[t, :, 0:hidden_rows] = eug[:, at].astype(BF)
        gm_ref[t, :, hidden_rows : 2 * hidden_rows] = rdg[:, at].astype(BF)
        for n in range(4):
            off = 2 * hidden_rows + n * head_rows
            gm_ref[t, :, off : off + head_rows] = whole[n][
                :, t * head_rows : (t + 1) * head_rows
            ].astype(BF)


def middle(scalars, heads, rows, cot, fac, vec, tab, merge, mlp):
    groups, slots, head_rows, block = heads.shape
    parts = cot.shape[0]
    dim = parts * head_rows
    hidden_rows = fac.shape[3]
    full = parts * hidden_rows
    out = (
        jax.ShapeDtypeStruct((parts, 2, head_rows, block), BF),
        jax.ShapeDtypeStruct((groups, slots, head_rows, block), BF),
        jax.ShapeDtypeStruct((parts, 16, 2 * hidden_rows + 4 * head_rows), BF),
    )
    vmem = pl.BlockSpec(memory_space=pltpu.VMEM)
    return pl.pallas_call(
        middle_kernel,
        out_shape=out,
        in_specs=[pl.BlockSpec(memory_space=pltpu.SMEM)]
        + [vmem] * 6
        + [pl.BlockSpec(memory_space=pl.ANY)] * 2,
        out_specs=tuple(vmem for _ in out),
        scratch_shapes=[
            pltpu.VMEM((full, dim + LANES), BF),
            pltpu.VMEM((full, dim + LANES), BF),
            pltpu.VMEM((dim, dim + LANES), BF),
            pltpu.VMEM((parts, head_rows, block), BF),
            pltpu.VMEM((block, dim + LANES), F32),
            pltpu.VMEM((block, dim + LANES), F32),
            pltpu.VMEM((block, dim + LANES), BF),
            pltpu.VMEM((block, dim + LANES), BF),
            pltpu.VMEM((16, full), F32),
            pltpu.VMEM((16, full), F32),
            pltpu.SemaphoreType.DMA((3, parts)),
        ],
        compiler_params=pltpu.CompilerParams(vmem_limit_bytes=60 * MIB),
        cost_estimate=pl.CostEstimate(flops=20 * 10**9, bytes_accessed=30 * 10**6, transcendentals=2 * 10**6),
        name="middle",
    )(scalars, heads, rows, cot, fac, vec, tab, merge, mlp)


def back_kernel(
    slots, sc, tok_ref, norm_ref, down_ref, upx_ref, qkv_ref, n1_ref, stats_ref, lse_ref,
    inner_ref, dout_ref, *rest,
):
    weights = rest[:slots]
    (out_ref,) = rest[slots : slots + 1]
    dot_scr, grad_scr, gb_scr, e1_scr, tu_scr = rest[slots + 1 :]
    parts, width, span = tok_ref.shape
    dim = parts * width
    groups, _, head_rows, block = dout_ref.shape
    heads_here = head_rows // HEAD_DIM
    mine, member = sc[0], sc[1]
    rank = down_ref.shape[0]

    pad = jnp.zeros((HEAD_PAD - HEAD_DIM, block), F32)
    for g in range(groups):
        cols = slice(g * block, (g + 1) * block)
        for k in range(slots):
            piece = dout_ref[g, k].astype(F32)
            for h in range(heads_here):
                one = jnp.concatenate([piece[h * HEAD_DIM : (h + 1) * HEAD_DIM, :], pad], 0)
                dot_scr[k * heads_here + h, :, cols] = one.astype(BF)

    def head_step(h, carry):
        query_t = qkv_ref[0, h]
        keys_t = qkv_ref[1, h]
        query = query_t.T
        keys = keys_t.T
        vals = qkv_ref[2, h].T
        dout_t = dot_scr[h]
        dout = dout_t.T
        dvals = jnp.zeros((span, HEAD_PAD), F32)
        dkeys = jnp.zeros((span, HEAD_PAD), F32)
        slot = h // heads_here
        row = pl.multiple_of(lax.rem(h, heads_here) * HEAD_DIM, 8)
        for c in range(span // CHUNK):
            cols = slice(c * CHUNK, (c + 1) * CHUNK)
            scores = mm(keys, query_t[:, cols]) * (SCALE * LOG2E)
            probs = jnp.exp2(scores - lse_ref[h, 0:1, cols])
            dprobs = mm(vals, dout_t[:, cols])
            delta = jnp.sum(probs * dprobs, 0, keepdims=True)
            dscores = (probs * (dprobs - delta)).astype(BF)
            dvals += mm(probs.astype(BF), dout[cols, :])
            dkeys += mm(dscores, query[cols, :])
            dquery = mm(keys_t, dscores) * SCALE
            grad_scr[slot, pl.ds(row, HEAD_DIM), cols] = dquery[0:HEAD_DIM, :]
        row = pl.multiple_of(row + head_rows, 8)
        grad_scr[slot, pl.ds(row, HEAD_DIM), :] = (dkeys * SCALE).T[0:HEAD_DIM, :]
        row = pl.multiple_of(row + head_rows, 8)
        grad_scr[slot, pl.ds(row, HEAD_DIM), :] = dvals.T[0:HEAD_DIM, :]
        return carry

    lax.fori_loop(0, slots * heads_here, head_step, 0)

    thr = jnp.zeros((rank, span), F32)
    spread = 3 * head_rows
    row_of = lax.broadcasted_iota(jnp.int32, (rank, spread), 0) // 16
    part_of = lax.broadcasted_iota(jnp.int32, (rank, spread), 1) // head_rows
    for k in range(slots):
        gb_scr[k] = grad_scr[k].astype(BF)
        thr = thr + mm(upx_ref[k], gb_scr[k])
        ups = mm(inner_ref[...], gb_scr[k], NT)
        ups = jnp.where(row_of == part_of, ups, 0.0)
        tu_scr[k] = ups[0:16, :] + ups[16:32, :] + ups[32:48, :]
    line = lax.broadcasted_iota(jnp.int32, (rank, span), 0)
    thr_b = jnp.where(line < 48, 0.5 * thr, 0.0).astype(BF)
    downs = mm(thr_b, n1_ref[...], NT)

    def final_step(c, carry):
        cols = pl.ds(pl.multiple_of(c * CHUNK, CHUNK), CHUNK)
        total = mm(weights[0][0:spread, :], gb_scr[0, :, cols], TN)
        for k in range(1, slots):
            total = total + mm(weights[k][0:spread, :], gb_scr[k, :, cols], TN)
        e1_scr[:, cols] = total
        return carry

    lax.fori_loop(0, span // CHUNK, final_step, 0)
    e1 = (e1_scr[...] + mm(down_ref[...], thr_b, TN)) * norm_ref[:, 0:1]
    first = jnp.sum(e1, 0, keepdims=True)
    mean, rstd = stats_ref[0:1, :], stats_ref[1:2, :]
    unit = (tok_ref[...].reshape(dim, span).astype(F32) - mean) * rstd
    second = jnp.sum(e1 * unit, 0, keepdims=True)
    lines = []
    for value in (first, second, mean, rstd):
        high = value.astype(BF).astype(F32)
        lines += [high, value - high]
    lines = jnp.concatenate(lines + [jnp.zeros((8, span), F32)], 0).astype(BF)
    for t in range(parts):
        out_ref[t, 0:width, :] = e1[t * width : (t + 1) * width, :].astype(BF)
        out_ref[t, width : width + 16, :] = lines
        own = jnp.where(member == t % groups, 1.0, 0.0)
        ups = tu_scr[lax.rem(t // groups - mine + slots, slots)] * own
        ups = jnp.concatenate([ups[:, j * head_rows : (j + 1) * head_rows] for j in range(3)], 0)
        down_part = downs[0:48, t * width : (t + 1) * width]
        rest_cols = span - width - head_rows
        out_ref[t, width + 16 : width + 64, :] = jnp.concatenate(
            [down_part, ups, jnp.zeros((48, rest_cols), F32)], 1
        ).astype(BF)


def attend_back(scalars, tok, norm, down, upx, qkv, n1, stats, lse, inner, dout, weights):
    parts, width, span = tok.shape
    slots = len(weights)
    head_rows = upx.shape[2] // 3
    heads = slots * head_rows // HEAD_DIM
    dim = parts * width
    return pl.pallas_call(
        partial(back_kernel, slots),
        out_shape=jax.ShapeDtypeStruct((parts, width + 64, span), BF),
        in_specs=[pl.BlockSpec(memory_space=pltpu.SMEM)]
        + [pl.BlockSpec(memory_space=pltpu.VMEM)] * (10 + slots),
        out_specs=pl.BlockSpec(memory_space=pltpu.VMEM),
        scratch_shapes=[
            pltpu.VMEM((heads, HEAD_PAD, span), BF),
            pltpu.VMEM((slots, 3 * head_rows, span), F32),
            pltpu.VMEM((slots, 3 * head_rows, span), BF),
            pltpu.VMEM((dim, span), F32),
            pltpu.VMEM((slots, 16, 3 * head_rows), F32),
        ],
        compiler_params=pltpu.CompilerParams(vmem_limit_bytes=56 * MIB),
        cost_estimate=pl.CostEstimate(flops=12 * 10**9, bytes_accessed=20 * 10**6, transcendentals=5 * 10**6),
        name="attend_back",
    )(scalars, tok, norm, down, upx, qkv, n1, stats, lse, inner, dout, *weights)


def shards(
    tokens,
    cotangent,
    adapter_index,
    valid_image,
    first_gain,
    first_shift,
    triple_weight,
    triple_bias,
    triple_down,
    triple_up,
    merge_weight,
    merge_bias,
    merge_down,
    merge_up,
    second_gain,
    second_shift,
    expand_weight,
    expand_bias,
    expand_down,
    expand_up,
    reduce_weight,
    reduce_bias,
    reduce_down,
    reduce_up,
    *,
    parts,
    copies,
):
    slots = adapter_index.shape[0]
    groups = parts // slots
    seq = tokens.shape[0] // slots
    width = tokens.shape[1]
    dim = width * parts
    head_rows = triple_weight.shape[2]
    adapters = triple_down.shape[1]
    span = up_to(seq, CHUNK)
    block = span // groups
    place = lax.axis_index("tensor")
    row = lax.axis_index("dp")
    mine, member = place // groups, place % groups
    index = lax.dynamic_index_in_dim(adapter_index, mine, 0, False)
    valid = lax.dynamic_index_in_dim(valid_image, mine, 0, False)
    all_index = lax.all_gather(adapter_index, "dp", tiled=True)
    scalars = jnp.stack([mine, member, valid]).astype(jnp.int32)

    def hop(x, step):
        return lax.ppermute(x, "tensor", [(s, (s + step) % parts) for s in range(parts)])

    def swap(x):
        pieces = [lax.dynamic_index_in_dim(x, place, 0, False)]
        for k in range(1, parts):
            pieces.append(hop(lax.dynamic_index_in_dim(x, (place + k) % parts, 0, False), k))
        stacked = jnp.stack(pieces)
        return jnp.stack(
            [lax.dynamic_index_in_dim(stacked, (place - s) % parts, 0, False) for s in range(parts)]
        )

    def images_of(x):
        flat = x.T
        return jnp.stack(
            [
                jnp.pad(flat[:, n * seq : (n + 1) * seq], ((0, 0), (0, span - seq)))
                for n in range(slots)
            ]
        )

    def pick(table, axis=0):
        return lax.dynamic_index_in_dim(table, index, axis, False)

    tok = lax.all_to_all(jnp.repeat(images_of(tokens), groups, 0), "tensor", 0, 0)

    flat_triple = triple_weight.transpose(0, 2, 1).reshape(3 * head_rows, dim)
    piece_rows = up_to(3 * head_rows, 16 * copies) // copies
    padded = jnp.pad(flat_triple, ((0, piece_rows * copies - 3 * head_rows), (0, 0)))
    my_piece = lax.dynamic_slice_in_dim(padded, row * piece_rows, piece_rows, 0)
    weights = [flat_triple]
    for k in range(1, slots):
        got = hop(my_piece, -groups * k)
        weights.append(lax.all_gather(got, "dp", tiled=True))

    def up_pack(which):
        table = lax.dynamic_index_in_dim(triple_up, which, 1, False)
        lines = [
            jnp.pad(table[j], ((0, 0), (j * head_rows, (2 - j) * head_rows))) for j in range(3)
        ]
        bias = jnp.pad(triple_bias.reshape(1, 3 * head_rows), ((0, 15), (0, 0)))
        return jnp.concatenate(lines + [bias], 0)

    ups = [up_pack(index)]
    for k in range(1, slots):
        there = lax.dynamic_index_in_dim(adapter_index, (mine - k) % slots, 0, False)
        ups.append(hop(up_pack(there), -groups * k))
    upx = jnp.stack(ups)
    down = jnp.pad(pick(triple_down, 1).transpose(0, 2, 1).reshape(48, dim), ((0, 16), (0, 0)))
    norm = jnp.pad(jnp.stack([first_gain, first_shift], 1).astype(F32), ((0, 0), (0, 6)))

    merge_rows = up_to(width, 16 * copies) // copies
    merge_piece = lax.dynamic_slice_in_dim(
        jnp.pad(merge_weight, ((0, merge_rows * copies - width), (0, 0))), row * merge_rows, merge_rows, 0
    )
    merge_all = lax.all_gather(merge_piece, ("tensor", "dp")).reshape(parts, merge_rows * copies, dim)
    hidden_here = reduce_weight.shape[0]
    hidden_rows = up_to(hidden_here, 8 * copies)
    extra = ((0, hidden_rows - hidden_here), (0, 0))
    both = jnp.concatenate([jnp.pad(expand_weight.T, extra), jnp.pad(reduce_weight, extra)], 0)
    mlp_rows = 2 * hidden_rows // copies
    mlp_piece = lax.dynamic_slice_in_dim(both, row * mlp_rows, mlp_rows, 0)
    mlp_all = lax.all_gather(mlp_piece, ("tensor", "dp")).reshape(parts, 2 * hidden_rows, dim)

    def factor_pack(which):
        def lanes(x):
            return jnp.pad(x, ((0, 16 - x.shape[0]), (0, hidden_rows - x.shape[1])))

        return jnp.concatenate(
            [
                lanes(lax.dynamic_index_in_dim(expand_up, which, 0, False)),
                lanes(lax.dynamic_index_in_dim(reduce_down, which, 0, False).T),
                lanes(lax.dynamic_index_in_dim(merge_down, which, 0, False).T),
                lanes(expand_bias[None, :]),
            ],
            0,
        )

    fac = lax.all_gather(jnp.stack([factor_pack(adapter_index[n]) for n in range(slots)]), "tensor")
    tab = jnp.stack(
        [
            jnp.pad(x, ((0, LANES - 16), (0, 0)))
            for x in (pick(merge_up), pick(expand_down).T, pick(reduce_up))
        ]
    )
    vec = jnp.pad(
        jnp.stack([merge_bias, reduce_bias, second_gain, second_shift]).astype(F32), ((0, 4), (0, 0))
    )

    cot = images_of(cotangent).reshape(slots, width, groups, block).transpose(0, 2, 1, 3)
    cot = swap(cot.reshape(parts, width, block))

    group_list = [[n * groups + g for g in range(groups)] for n in range(slots)]

    def trade(x):
        return lax.all_to_all(x, "tensor", 0, 0, axis_index_groups=group_list)

    qkv, n1, stats, lse, inner, heads, rows = attend(seq, groups, tok, norm, down, upx, weights)
    heads = trade(heads)
    pair, back, gm = middle(scalars, heads, rows, cot, fac, vec, tab, merge_all, mlp_all)
    dout = trade(back)
    pair = swap(pair)
    gm = swap(gm)
    last = attend_back(scalars, tok, norm, down, upx, qkv, n1, stats, lse, inner, dout, weights)
    last = lax.all_to_all(last, "tensor", 0, 0)

    def to_rows(image_parts):
        return jnp.concatenate([x[:, :seq] for x in image_parts], 1).T

    def whole_image(x):
        return x.reshape(slots, groups, width, block).transpose(0, 2, 1, 3).reshape(slots, width, span)

    layer = to_rows(whole_image(pair[:, 0])).astype(BF)
    residual = whole_image(pair[:, 1]).astype(F32)
    last = last.reshape(slots, groups, width + 64, span).astype(F32)
    summed = jnp.sum(last, 1)
    mine_t = images_of(tokens).astype(F32)
    one = last[:, 0]

    def line(source, n):
        at = width + 2 * n
        return source[:, at : at + 1, :] + source[:, at + 1 : at + 2, :]

    first, second = line(summed, 0), line(summed, 1)
    mean, rstd = line(one, 2), line(one, 3)
    unit = (mine_t - mean) * rstd
    grad = residual + rstd * (summed[:, :width] - first / dim - unit * (second / dim))
    tokens_grad = to_rows(grad)

    one_hot = (all_index[:, None] == jnp.arange(adapters, dtype=jnp.int32)[None, :]).astype(BF)

    def by_adapter(terms):
        gathered = lax.all_gather(terms.astype(BF), "dp", tiled=True)
        flat = gathered.reshape(gathered.shape[0], -1)
        summed = lax.dot_general(one_hot, flat, TN, preferred_element_type=F32)
        return summed.reshape((adapters,) + terms.shape[1:])

    gm = jnp.sum(gm.reshape(slots, groups, 16, gm.shape[2]).astype(F32), 1)
    gm = by_adapter(gm)
    off = 2 * hidden_rows
    expand_up_grad = gm[:, :, :hidden_here]
    reduce_down_grad = gm[:, :, hidden_rows : hidden_rows + hidden_here].transpose(0, 2, 1)
    merge_down_grad = gm[:, :, off : off + width].transpose(0, 2, 1)
    held = lax.all_gather(gm[:, :, off + width :].astype(BF), "tensor").astype(F32)
    held = held.reshape(parts, adapters, 16, 3, width).transpose(3, 1, 2, 0, 4)
    held = held.reshape(3, adapters, 16, dim)
    merge_up_grad = held[0]
    expand_down_grad = held[1].transpose(0, 2, 1)
    reduce_up_grad = held[2]

    gt = by_adapter(summed[:, width + 16 : width + 64, : width + head_rows])
    triple_up_grad = gt[:, :, width:].reshape(adapters, 3, 16, head_rows).transpose(1, 0, 2, 3)
    held = lax.all_gather(gt[:, :, :width].astype(BF), "tensor").astype(F32)
    held = held.reshape(parts, adapters, 3, 16, width).transpose(2, 1, 0, 4, 3)
    triple_down_grad = held.reshape(3, adapters, dim, 16)

    return (
        layer,
        tokens_grad,
        triple_down_grad,
        triple_up_grad,
        merge_down_grad,
        merge_up_grad,
        expand_down_grad,
        expand_up_grad,
        reduce_down_grad,
        reduce_up_grad,
    )


def solution(mesh):
    in_specs = (
        P("dp", "tensor"),
        P("dp", "tensor"),
        P("dp"),
        P("dp"),
        P(),
        P(),
        P(None, None, "tensor"),
        P(None, "tensor"),
        P(),
        P(None, None, None, "tensor"),
        P("tensor", None),
        P(),
        P(None, "tensor", None),
        P(),
        P(),
        P(),
        P(None, "tensor"),
        P("tensor"),
        P(),
        P(None, None, "tensor"),
        P("tensor", None),
        P(),
        P(None, "tensor", None),
        P(),
    )
    out_specs = (
        P("dp", "tensor"),
        P("dp", "tensor"),
        P(),
        P(None, None, None, "tensor"),
        P(None, "tensor", None),
        P(),
        P(),
        P(None, None, "tensor"),
        P(None, "tensor", None),
        P(),
    )
    return jax.shard_map(
        partial(shards, parts=mesh.shape["tensor"], copies=mesh.shape["dp"]),
        mesh=mesh,
        in_specs=in_specs,
        out_specs=out_specs,
        check_vma=False,
    )
```

time: 1220 us -> 573 us (0.47)
  local copies, waits for them, and re-layouts: 393 us -> 73.3 us
  matrix products: 261 us -> 3.85 us
  waiting for transfers between devices: 436 us -> 219 us
  Pallas kernels: 0 us -> 97.6 us
  blocking collectives: 35.4 us -> 95.6 us
  other arithmetic: 69.1 us -> 18.1 us
  starting transfers between devices: 0.36 us -> 35.1 us
    psum x3 -> x0, waiting for transfers between devices: 282 us -> none  [the longest x1 156 us: shards(): branch = lax.psum(partial_merge, 'tensor')]
    dot_general x86 -> x2, matrix products: 261 us -> 3.85 us  [by_adapter(): summed = lax.dot_general(one_hot, flat, TN, preferred_element_type=F32)]
    reshape x49 -> x5, local copies, waits for them, and re-layouts: 176 us -> 8.54 us  [the longest x2 5.42 us: shards(): triple_down_grad = held.reshape(3, adapters, dim, 16)]
    unnamed x12 -> x5, waiting for transfers between devices: 126 us -> 0.08 us
    all_gather x3 -> x5, waiting for transfers between devices: 27 us -> 138 us  [the longest x1 132 us: shards(): lax.all_gather(mlp_piece, ('tensor', 'dp'))]
    pallas_call x0 -> x3, Pallas kernels: none -> 97.6 us  [the longest x1 40 us: middle(): pl.pallas_call(middle_kernel, out_shape=out, in_specs=[pl.BlockSpec(memor...]
    all_gather x0 -> x3, blocking collectives: none -> 88.2 us  [the longest x1 51.8 us: shards(): lax.all_gather(gm[:, :, off + width:].astype(BF), 'tensor').astype(F32)]
    mul x22 -> x0, local copies, waits for them, and re-layouts: 86.9 us -> none  [the longest x2 28.6 us: shards(): adapter_scale * extra_expand.reshape(count, -1)]
  transfers between devices with their start and end apart: 9 -> 20, of which waited for: 6 -> 7; matrix products, arithmetic and copies ran while one was open for 47% -> 12% of each run, Pallas kernels for 0% -> 10%
where the time goes in v1:
time: 573 us; the launch traced here: 566 us
  waiting for transfers between devices  219 us (38%)
  Pallas kernels  97.6 us (17%)
  blocking collectives  95.6 us (17%)
  local copies, waits for them, and re-layouts  73.3 us (13%)
  starting transfers between devices  35.1 us (6%)
  between operations  23.6 us (4%)
  other arithmetic  18.1 us (3%)
    all_gather x1, waiting for transfers between devices, shards(): lax.all_gather(mlp_piece, ('tensor', 'dp'))  132 us
    ppermute x11, waiting for transfers between devices, hop(): lax.ppermute(x, 'tensor', [(s, (s + step) % parts) for s in range(parts)])  68.7 us
    all_gather x1, blocking collectives, shards(): lax.all_gather(gm[:, :, off + width:].astype(BF), 'tensor').astype(F32)  51.8 us
    pallas_call x1, Pallas kernels, middle(): pl.pallas_call(middle_kernel, out_shape=out, in_specs=[pl.BlockSpec(memor...  40 us
    pallas_call x1, Pallas kernels, attend_back(): pl.pallas_call(partial(back_kernel, slots), out_shape=jax.ShapeDtypeStruc...  31.6 us
    pallas_call x1, Pallas kernels, attend(): pl.pallas_call(partial(attend_kernel, seq, slots, groups), out_shape=out,...  25.9 us
    all_gather x1, blocking collectives, shards(): held = lax.all_gather(gt[:, :, :width].astype(BF), 'tensor').astype(F32)  24.7 us
    ppermute x11, starting transfers between devices, hop(): lax.ppermute(x, 'tensor', [(s, (s + step) % parts) for s in range(parts)])  18.1 us
  transfers between devices with their start and end apart: 20, of which 7 were waited for; matrix products, arithmetic and copies ran while one was open for 12% of the time, Pallas kernels for 10%

profile of v1, /device:TPU:0, one launch (start us, length us, event | category | flops | bytes accessed | tf_op | source)
XLA Modules:
  0.0 566.1 jit_solution(7602394394270630434)
XLA Ops:
  7.3 1.1 pad_dynamic-slice_fusion.2
  8.4 4.1 collective-permute-start.1
  12.5 11.7 %collective-permute-done.1 = bf16[112,1152]{1,0:T(8,128)(2,1)S(1)} collective-permute-done((bf16[112,1152]{1,0:T(8,128)(2,1)S(1)}, bf16[112,1152]{1,0:T(8,128)(2,1)S(1)}, u32[]{:S(2)}, u32[]{:S(2)}) %collective-permute-start.1) | collective-permute-done | bytes 258080 | tf_op jit(solution)/shard_map/ppermute | solution.py:504
  33.5 3.0 fusion.13
  38.6 1.3 broadcast_in_dim.4
  39.9 4.9 all-to-all-start
  50.4 2.9 collective-permute-start
  53.3 2.0 slice.181
  55.3 1.1 pad_bitcast_fusion
  56.6 1.0 constant_dynamic-slice_fusion.14
  57.6 1.5 collective-permute-start.4
  59.0 1.5 collective-permute-start.3
  66.6 1.1 pad_add_fusion.sc
  67.7 53.0 %collective-permute-done = bf16[64,864]{1,0:T(8,128)(2,1)} collective-permute-done((bf16[64,864]{1,0:T(8,128)(2,1)}, bf16[64,864]{1,0:T(8,128)(2,1)}, u32[]{:S(2)}, u32[]{:S(2)}) %collective-permute-start) | collective-permute-done | bytes 110624 | tf_op jit(solution)/shard_map/ppermute | solution.py:504
  120.7 0.9 pad_maximum_fusion.10.upx_ref
  121.7 1.2 copy-done.15
  122.9 25.9 %attend.1 = (bf16[3,8,80,768]{3,2,1,0:T(8,128)(2,1)}, bf16[1152,768]{1,0:T(8,128)(2,1)S(1)}, f32[8,768]{1,0:T(8,128)S(1)}, f32[8,1,768]{2,1,0:T(1,128)S(1)}, bf1...) custom-call(bf16[4,288,768]{2,1,0:T(8,128)(2,1)} %copy-done.15, ...), custom_call_target="tpu_custom_call" | custom-call | flops 8000000000 | bytes 16000000 | tf_op jit(solution)/shard_map/attend/pallas_call | solution.py:125
  148.8 1.2 copy-done.5
  150.0 1.2 copy-done.6
  153.1 3.9 all-to-all-start.1
  157.0 1.1 pad_maximum_fusion.6.tab_ref
  158.7 1.3 pad_maximum_fusion.4
  160.1 1.1 pad_maximum_fusion.5.cot_ref
  161.2 12.4 %all-to-all-done.1.heads_ref = bf16[2,2,288,384]{3,2,1,0:T(8,128)(2,1)S(1)} async-done(((bf16[2,2,288,384]{3,2,1,0:T(8,128)(2,1)}), bf16[2,2,288,384]{3,2,1,0:T(8,128)(2,1)S(1)}, u32[]{:S(2)}, u32[]{:S(2)}) %all-to-all-start.1) | async-done | bytes 884768 | tf_op jit(solution)/shard_map/all_to_all | solution.py:598
  173.6 6.0 %all-gather.17.cloned.1.call-done = bf16[1536,1152]{1,0:T(8,128)(2,1)} async-done(((bf16[48,1152]{1,0:T(8,128)(2,1)}), bf16[1536,1152]{1,0:T(8,128)(2,1)}) %all-gather.17.cloned.1.call-update) | async-done | bytes 3538960 | tf_op jit(solution)/shard_map/all_gather | solution.py:558
  179.6 131.7 %all-gather.19.cloned.1.call-done = bf16[8704,1152]{1,0:T(8,128)(2,1)} async-done(((bf16[272,1152]{1,0:T(8,128)(2,1)}), bf16[8704,1152]{1,0:T(8,128)(2,1)}) %all-gather.19.cloned.1.call-update) | async-done | bytes 20054032 | tf_op jit(solution)/shard_map/all_gather | solution.py:565
  311.4 40.0 %middle.1 = (bf16[4,2,288,384]{3,2,1,0:T(8,128)(2,1)}, bf16[2,2,288,384]{3,2,1,0:T(8,128)(2,1)}, bf16[4,16,3328]{2,1,0:T(8,128)(2,1)}) custom-call(s32[3]{0:T(128)} %pad_add_fusion.sc, bf16[2,2,288,384]{3,2,1,0:T(8,128)(2,1)} %copy-done.22, bf16[2,1152,384]{2,1,0:T(8,128)(2,1)} %copy-done.6, bf16[4,288,384]{2,1,0:T(8,128)(2,1)} %pad_maximum_fusion.5.cot_ref, ...), custom_call_target="tpu_custom_call" | custom-call | flops 20000000000 | bytes 30000000 | tf_op jit(solution)/shard_map/middle/pallas_call | solution.py:306
  351.4 1.1 constant_dynamic-slice_fusion.4
  352.5 1.4 collective-permute-start.10
  354.0 1.9 collective-permute-start.8
  356.0 4.5 all-to-all-start.2
  360.5 3.8 collective-permute-done.9
  366.9 7.3 %all-reduce.26 = s32[16]{0:T(128)S(1)} all-reduce(s32[16]{0:T(128)S(1)} %dynamic-update-slice), channel_id=1, replica_groups=mesh['dp'=8,'tensor'=4] {'dp'}, use_global_device_ids=true, to_apply=%add.26 | all-reduce | flops 16 | bytes 128
  374.2 1.1 constant_dynamic-slice_fusion.9
  375.3 1.2 collective-permute-start.7
  376.5 1.3 collective-permute-start.6
  377.7 2.2 collective-permute-start.5
  379.9 31.6 %attend_back.1 = bf16[4,352,768]{2,1,0:T(8,128)(2,1)} custom-call(s32[3]{0:T(128)} %pad_add_fusion.sc, bf16[4,288,768]{2,1,0:T(8,128)(2,1)} %copy-done.15, f32[1152,8]{1,0:T(8,128)} %copy-done.2, bf16[64,1152]{1,0:T(8,128)(2,1)} %copy-done.4, bf16[2,64,864]{2,1,0:T(8,128)(2,1)} %copy-done.3, bf16[3,8,80,768]{3,2,1,0:T(8,128)(2,1)} %get-tuple-element.23.qkv_ref, ...), custom_call_target="tpu_custom_call" | custom-call | flops 12000000000 | bytes 20000000 | tf_op jit(solution)/shard_map/attend_back/pallas_call | solution.py:438
  411.6 3.6 all-to-all-start.3
  415.3 1.6 pad_maximum_fusion
  418.6 1.3 copy.94
  419.9 1.2 maximum_bitcast_fusion.1
  421.1 2.4 fusion.3
  424.6 0.9 copy.88
  426.4 51.8 %all-gather.4 = bf16[32,16,864]{2,0,1:T(8,128)(2,1)S(1)} all-gather(bf16[8,16,864]{2,0,1:T(8,128)(2,1)S(1)} %slice.248), channel_id=6, replica_groups=mesh['dp'=8,'tensor'=4] {'tensor'}, dimensions={0}, use_global_device_ids=true | all-gather | bytes 1105920 | tf_op jit(solution)/shard_map/all_gather | solution.py:646
  478.3 1.6 copy.82
  479.9 4.6 reshape.126
  484.4 7.3 %fusion.66 = (f32[1,8,16,4,288]{4,0,2,1,3:T(1,128)S(1)}, f32[1,8,16,4,288]{4,0,2,1,3:T(1,128)}, f32[1,8,16,4,288]{4,0,2,1,3:T(1,128)S(1)}) fusion(f32[3,8,16,4,288]{4,0,2,1,3:T(4,128)} %bitcast.195), kind=kLoop, calls=%fused_computation.170 | loop fusion | bytes 3538944 | tf_op jit(solution)/shard_map/slice | solution.py:651
  491.7 1.4 copy.85
  493.1 2.3 squeeze.160
  495.4 2.5 copy.84
  497.9 2.3 squeeze.159
  500.2 1.4 copy.83
  501.6 2.3 squeeze.158
  504.3 1.3 copy-done.10
  505.7 11.7 %all_gather.50 = bf16[16,48,576]{2,1,0:T(8,128)(2,1)} all-gather(bf16[2,48,576]{2,1,0:T(8,128)(2,1)S(1)} %slice.249), channel_id=1, replica_groups=mesh['dp'=8,'tensor'=4] {'dp'}, dimensions={0}, use_global_device_ids=true | all-gather | bytes 995328 | tf_op jit(solution)/shard_map/all_gather | solution.py:635
  517.4 2.1 reshape.113
  519.5 1.8 dot_general.15
  521.3 1.5 fusion.10
  523.9 24.7 %all-gather.3 = bf16[32,48,288]{2,0,1:T(8,128)(2,1)S(1)} all-gather(bf16[8,48,288]{2,0,1:T(8,128)(2,1)S(1)} %slice.247), channel_id=5, replica_groups=mesh['dp'=8,'tensor'=4] {'tensor'}, dimensions={0}, use_global_device_ids=true | all-gather | bytes 1105920 | tf_op jit(solution)/shard_map/all_gather | solution.py:655
  548.9 2.1 copy.79
  551.0 3.3 reshape.124
  554.9 1.4 copy-done.11
  557.5 1.6 maximum_bitcast_fusion
  (177 shorter events, 27.1 us)
Async XLA Ops:
  7.2 55.5 %copy-start = (bf16[3,8,1152,16]{2,3,1,0:T(8,128)(2,1)S(1)}, bf16[3,8,1152,16]{2,3,1,0:T(8,128)(2,1)}, u32[]{:S(2)}) copy-start(bf16[3,8,1152,16]{2,3,1,0:T(8,128)(2,1)} %param.32) | copy-start | bytes 2654212
  7.2 17.8 %copy-start.29 = (s32[2]{0:T(128)S(1)}, s32[2]{0:T(128)}, u32[]{:S(2)}) copy-start(s32[2]{0:T(128)} %param.26) | copy-start | bytes 28
  7.2 21.0 %copy-start.31 = (bf16[1076]{0:T(1024)(128)(2,1)S(1)}, bf16[1076]{0:T(1024)(128)(2,1)}, u32[]{:S(2)}) copy-start(bf16[1076]{0:T(1024)(128)(2,1)} %param.41) | copy-start | bytes 6460
  7.2 114.4 %all-gather.11.cloned.1.call-start = ((), (), s32[]{:S(2)}) async-start(), calls=%async_computation.4 | async-start | bytes 2322432 | tf_op jit(solution)/shard_map/all_gather | solution.py:536
  7.3 25.5 %copy-start.24 = (bf16[288,1152]{1,0:T(8,128)(2,1)S(1)}, bf16[288,1152]{1,0:T(8,128)(2,1)}, u32[]{:S(2)}) copy-start(bf16[288,1152]{1,0:T(8,128)(2,1)} %param.34) | copy-start | bytes 1990660
  8.4 15.8 %collective-permute-start.1 = (bf16[112,1152]{1,0:T(8,128)(2,1)S(1)}, bf16[112,1152]{1,0:T(8,128)(2,1)S(1)}, u32[]{:S(2)}, u32[]{:S(2)}) collective-permute-start(bf16[112,1152]{1,0:T(8,128)(2,1)S(1)} %pad_dynamic-slice_fusion.2), channel_id=1, source_target_pairs={{0,2},{1,3},{2,0},{3,1},{4,6},{5,7},{6,4},{7,5},{8,10},{9,11},{10,... | collective-permute-start | bytes 774152 | tf_op jit(solution)/shard_map/ppermute | solution.py:504
  24.2 0.7 copy-start.26
  24.9 136.3 %all-gather.15.cloned.1.call-start = ((), (), s32[]{:S(2)}) async-start(), calls=%async_computation.6 | async-start | bytes 1474560 | tf_op jit(solution)/shard_map/all_gather | solution.py:581
  32.7 146.9 %all-gather.17.cloned.1.call-start = ((), (), s32[]{:S(2)}) async-start(), calls=%async_computation.7 | async-start | bytes 3649536 | tf_op jit(solution)/shard_map/all_gather | solution.py:558
  33.4 277.9 %all-gather.19.cloned.1.call-start = ((), (), s32[]{:S(2)}) async-start(), calls=%async_computation.8 | async-start | bytes 20680704 | tf_op jit(solution)/shard_map/all_gather | solution.py:565
  33.5 3.0 copy-start.20
  36.5 1.2 copy-start.21
  36.5 1.2 copy-start.39
  37.7 0.8 copy-start.13
  39.9 7.5 %copy-start.38 = (bf16[3,288]{1,0:T(4,128)(2,1)S(1)}, bf16[3,288]{1,0:T(4,128)(2,1)}, u32[]{:S(2)}) copy-start(bf16[3,288]{1,0:T(4,128)(2,1)} %param.31) | copy-start | bytes 5188
  39.9 81.7 %all-to-all-start = ((bf16[4,288,768]{2,1,0:T(8,128)(2,1)}), bf16[4,288,768]{2,1,0:T(8,128)(2,1)S(1)}, u32[]{:S(2)}, u32[]{:S(2)}) async-start(bf16[4,288,768]{2,1,0:T(8,128)(2,1)} %bitcast.5), calls=%async_computation | async-start | bytes 3538944 | tf_op jit(solution)/shard_map/all_to_all | solution.py:527
  50.4 70.2 %collective-permute-start = (bf16[64,864]{1,0:T(8,128)(2,1)}, bf16[64,864]{1,0:T(8,128)(2,1)}, u32[]{:S(2)}, u32[]{:S(2)}) collective-permute-start(bf16[64,864]{1,0:T(8,128)(2,1)} %get-tuple-element.124), channel_id=1, source_target_pairs={{0,2},{1,3},{2,0},{3,1},{4,6},{5,7},{6,4},{7,5},{8,10},{9,11},{10,... | collective-permute-start | bytes 331784 | tf_op jit(solution)/shard_map/ppermute | solution.py:504
  56.4 4.1 copy-start.40
  56.5 4.6 copy-start.32
  56.5 4.6 copy-start.33
  56.5 4.6 copy-start.34
  56.6 4.5 copy-start.35
  56.6 4.5 copy-start.36
  56.6 5.1 copy-start.37
  57.6 63.1 %copy-start.25 = (bf16[1,64,864]{2,1,0:T(8,128)(2,1)S(1)}, bf16[1,64,864]{2,1,0:T(8,128)(2,1)}, u32[]{:S(2)}) copy-start(bf16[1,64,864]{2,1,0:T(8,128)(2,1)} %get-tuple-element.123) | copy-start | bytes 331780
  57.6 101.1 %collective-permute-start.4 = (bf16[288,384]{1,0:T(8,128)(2,1)}, bf16[288,384]{1,0:T(8,128)(2,1)}, u32[]{:S(2)}, u32[]{:S(2)}) collective-permute-start(bf16[288,384]{1,0:T(8,128)(2,1)} %get-tuple-element.98), channel_id=1, source_target_pairs={{0,3},{1,0},{2,1},{3,2},{4,7},{5,4},{6,5},{7,6},{8,11},{9,8},{10,9... | collective-permute-start | bytes 663560 | tf_op jit(solution)/shard_map/ppermute | solution.py:504
  59.0 99.7 %collective-permute-start.3 = (bf16[288,384]{1,0:T(8,128)(2,1)}, bf16[288,384]{1,0:T(8,128)(2,1)}, u32[]{:S(2)}, u32[]{:S(2)}) collective-permute-start(bf16[288,384]{1,0:T(8,128)(2,1)} %get-tuple-element.99), channel_id=1, source_target_pairs={{0,2},{1,3},{2,0},{3,1},{4,6},{5,7},{6,4},{7,5},{8,10},{9,11},{10,... | collective-permute-start | bytes 663560 | tf_op jit(solution)/shard_map/ppermute | solution.py:504
  60.5 98.2 %collective-permute-start.2 = (bf16[288,384]{1,0:T(8,128)(2,1)}, bf16[288,384]{1,0:T(8,128)(2,1)}, u32[]{:S(2)}, u32[]{:S(2)}) collective-permute-start(bf16[288,384]{1,0:T(8,128)(2,1)} %get-tuple-element.100), channel_id=1, source_target_pairs={{0,1},{1,2},{2,3},{3,0},{4,5},{5,6},{6,7},{7,4},{8,9},{9,10},{10,1... | collective-permute-start | bytes 663560 | tf_op jit(solution)/shard_map/ppermute | solution.py:504
  62.7 86.1 %copy-start.4 = (bf16[64,1152]{1,0:T(8,128)(2,1)}, bf16[64,1152]{1,0:T(8,128)(2,1)S(1)}, u32[]{:S(2)}) copy-start(bf16[64,1152]{1,0:T(8,128)(2,1)S(1)} %pad.111.down_ref) | copy-start | bytes 442372
  66.6 82.2 %copy-start.2 = (f32[1152,8]{1,0:T(8,128)}, f32[1152,8]{1,0:T(8,128)S(1)}, u32[]{:S(2)}) copy-start(f32[1152,8]{1,0:T(8,128)S(1)} %pad_convert_fusion.norm_ref) | copy-start | bytes 110596
  121.6 27.2 %copy-start.3 = (bf16[2,64,864]{2,1,0:T(8,128)(2,1)}, bf16[2,64,864]{2,1,0:T(8,128)(2,1)S(1)}, u32[]{:S(2)}) copy-start(bf16[2,64,864]{2,1,0:T(8,128)(2,1)S(1)} %pad_maximum_fusion.10.upx_ref) | copy-start | bytes 663556
  121.6 1.2 copy-start.15
  148.8 1.2 copy-start.5
  150.0 1.2 copy-start.6
  151.2 0.6 copy-start.7
  151.9 0.6 copy-start.8
  152.5 0.6 copy-start.9
  153.1 3.9 copy-start.17
  153.1 3.9 copy-start.18
  153.1 3.9 copy-start.19
  153.1 5.0 copy-start.27
  153.1 5.0 copy-start.28
  153.1 5.7 copy-start.23
  153.1 20.5 %all-to-all-start.1 = ((bf16[2,2,288,384]{3,2,1,0:T(8,128)(2,1)}), bf16[2,2,288,384]{3,2,1,0:T(8,128)(2,1)S(1)}, u32[]{:S(2)}, u32[]{:S(2)}) async-start(bf16[2,2,288,384]{3,2,1,0:T(8,128)(2,1)} %get-tuple-element.20), calls=%async_computation.1 | async-start | bytes 1769472 | tf_op jit(solution)/shard_map/all_to_all | solution.py:598
  173.6 137.8 %copy-start.22 = (bf16[2,2,288,384]{3,2,1,0:T(8,128)(2,1)}, bf16[2,2,288,384]{3,2,1,0:T(8,128)(2,1)S(1)}, u32[]{:S(2)}) copy-start(bf16[2,2,288,384]{3,2,1,0:T(8,128)(2,1)S(1)} %all-to-all-done.1.heads_ref) | copy-start | bytes 2654212
  352.5 8.0 %collective-permute-start.10 = (bf16[16,3328]{1,0:T(8,128)(2,1)S(1)}, bf16[16,3328]{1,0:T(8,128)(2,1)S(1)}, u32[]{:S(2)}, u32[]{:S(2)}) collective-permute-start(bf16[16,3328]{1,0:T(8,128)(2,1)S(1)} %get-tuple-element.106), channel_id=1, source_target_pairs={{0,3},{1,0},{2,1},{3,2},{4,7},{5,4},{6,5},{7,6},{8,11},{9,8},{10,9... | collective-permute-start | bytes 319496 | tf_op jit(solution)/shard_map/ppermute | solution.py:504
  353.9 10.4 %collective-permute-start.9 = (bf16[16,3328]{1,0:T(8,128)(2,1)S(1)}, bf16[16,3328]{1,0:T(8,128)(2,1)S(1)}, u32[]{:S(2)}, u32[]{:S(2)}) collective-permute-start(bf16[16,3328]{1,0:T(8,128)(2,1)S(1)} %get-tuple-element.107), channel_id=1, source_target_pairs={{0,2},{1,3},{2,0},{3,1},{4,6},{5,7},{6,4},{7,5},{8,10},{9,11},{10,... | collective-permute-start | bytes 319496 | tf_op jit(solution)/shard_map/ppermute | solution.py:504
  354.0 10.3 %collective-permute-start.8 = (bf16[16,3328]{1,0:T(8,128)(2,1)S(1)}, bf16[16,3328]{1,0:T(8,128)(2,1)S(1)}, u32[]{:S(2)}, u32[]{:S(2)}) collective-permute-start(bf16[16,3328]{1,0:T(8,128)(2,1)S(1)} %get-tuple-element.108), channel_id=1, source_target_pairs={{0,1},{1,2},{2,3},{3,0},{4,5},{5,6},{6,7},{7,4},{8,9},{9,10},{10,1... | collective-permute-start | bytes 319496 | tf_op jit(solution)/shard_map/ppermute | solution.py:504
  356.0 9.4 %copy-start.41 = (u32[32]{0:T(128)S(1)}, u32[32]{0:T(128)}, u32[]{:S(2)}) copy-start(u32[32]{0:T(128)} %constant.293) | copy-start | bytes 388
  356.0 10.6 %copy-start.30 = (s32[2]{0:T(128)S(1)}, s32[2]{0:T(128)}, u32[]{:S(2)}) copy-start(s32[2]{0:T(128)} %param.26) | copy-start | bytes 28
  356.0 18.2 %copy-start.16 = (bf16[4,2,288,384]{3,2,1,0:T(8,128)(2,1)S(1)}, bf16[4,2,288,384]{3,2,1,0:T(8,128)(2,1)}, u32[]{:S(2)}) copy-start(bf16[4,2,288,384]{3,2,1,0:T(8,128)(2,1)} %get-tuple-element.22) | copy-start | bytes 5308420
  356.0 24.0 %all-to-all-start.2 = ((bf16[2,2,288,384]{3,2,1,0:T(8,128)(2,1)}), bf16[2,2,288,384]{3,2,1,0:T(8,128)(2,1)}, u32[]{:S(2)}, u32[]{:S(2)}) async-start(bf16[2,2,288,384]{3,2,1,0:T(8,128)(2,1)} %get-tuple-element.28), calls=%async_computation.2 | async-start | bytes 1769472 | tf_op jit(solution)/shard_map/all_to_all | solution.py:598
  360.5 60.7 %all-gather.13.cloned.1.call-start = ((), (), s32[]{:S(2)}) async-start(), calls=%async_computation.5 | async-start | bytes 1916928 | tf_op jit(solution)/shard_map/all_gather | solution.py:635
  375.3 39.9 %collective-permute-start.7 = (bf16[2,288,384]{2,1,0:T(8,128)(2,1)}, bf16[2,288,384]{2,1,0:T(8,128)(2,1)}, u32[]{:S(2)}, u32[]{:S(2)}) collective-permute-start(bf16[2,288,384]{2,1,0:T(8,128)(2,1)} %get-tuple-element.86), channel_id=1, source_target_pairs={{0,3},{1,0},{2,1},{3,2},{4,7},{5,4},{6,5},{7,6},{8,11},{9,8},{10,9... | collective-permute-start | bytes 1327112 | tf_op jit(solution)/shard_map/ppermute | solution.py:504
  376.5 38.9 %collective-permute-start.6 = (bf16[2,288,384]{2,1,0:T(8,128)(2,1)}, bf16[2,288,384]{2,1,0:T(8,128)(2,1)}, u32[]{:S(2)}, u32[]{:S(2)}) collective-permute-start(bf16[2,288,384]{2,1,0:T(8,128)(2,1)} %get-tuple-element.87), channel_id=1, source_target_pairs={{0,2},{1,3},{2,0},{3,1},{4,6},{5,7},{6,4},{7,5},{8,10},{9,11},{10,... | collective-permute-start | bytes 1327112 | tf_op jit(solution)/shard_map/ppermute | solution.py:504
  377.7 37.6 %collective-permute-start.5 = (bf16[2,288,384]{2,1,0:T(8,128)(2,1)S(1)}, bf16[2,288,384]{2,1,0:T(8,128)(2,1)}, u32[]{:S(2)}, u32[]{:S(2)}) collective-permute-start(bf16[2,288,384]{2,1,0:T(8,128)(2,1)S(1)} %get-tuple-element.88), channel_id=1, source_target_pairs={{0,1},{1,2},{2,3},{3,0},{4,5},{5,6},{6,7},{7,4},{8,9},{9,10},{10,1... | collective-permute-start | bytes 1327112 | tf_op jit(solution)/shard_map/ppermute | solution.py:504
  411.6 92.4 %all-to-all-start.3 = ((bf16[4,352,768]{2,1,0:T(8,128)(2,1)}), bf16[4,352,768]{2,1,0:T(8,128)(2,1)S(1)}, u32[]{:S(2)}, u32[]{:S(2)}) async-start(bf16[4,352,768]{2,1,0:T(8,128)(2,1)} %attend_back.1), calls=%async_computation.3 | async-start | bytes 4325376 | tf_op jit(solution)/shard_map/all_to_all | solution.py:607
  504.3 1.4 copy-start.10
  554.7 1.6 copy-start.11
  554.7 2.1 copy-start.12
  554.7 2.2 copy-start.14
  557.5 1.6 copy-start.1
Sparse Core Ops, SparseCore 0:
  25.1 28.9 all-gather.10
  56.1 61.3 all-gather.14
  120.4 59.1 all-gather.16
  182.4 128.9 all-gather.18
  365.5 25.3 all-gather.12

commit v2 on v1

v2 whole, which is shorter than its diff:
```python
import math
from functools import partial

import jax
import jax.numpy as jnp
from jax import lax
from jax.experimental import pallas as pl
from jax.experimental.pallas import tpu as pltpu
from jax.sharding import PartitionSpec as P

HEAD_DIM = 72
HEAD_PAD = 80
LANES = 128
CHUNK = 256
EPS = 1e-06
BF = jnp.bfloat16
F32 = jnp.float32
SCALE = 1.0 / math.sqrt(HEAD_DIM)
LOG2E = 1.4426950408889634
MIB = 1024 * 1024

NN = (((1,), (0,)), ((), ()))
NT = (((1,), (1,)), ((), ()))
TN = (((0,), (0,)), ((), ()))


def mm(a, b, dims=NN):
    return lax.dot_general(a, b, dims, preferred_element_type=F32)


def up_to(value, step):
    return -(-value // step) * step


def vmem():
    return pl.BlockSpec(memory_space=pltpu.VMEM)


def anywhere():
    return pl.BlockSpec(memory_space=pl.ANY)


def smem():
    return pl.BlockSpec(memory_space=pltpu.SMEM)


class Shape:
    def __init__(self, parts, slots, copies):
        self.parts, self.slots, self.copies = parts, slots, copies
        self.groups = parts // slots
        self.pairs = [(k, g) for k in range(slots) for g in range(self.groups)]
        self.bits = []
        bit = copies // 2
        while bit:
            self.bits.append(bit)
            bit //= 2
        self.orders = (self.bits, self.bits[1::-1] + self.bits[2:])
        self.batches = (
            [(0, g) for g in range(1, self.groups)],
            [(k, 0) for k in range(1, slots)],
            [(k, g) for k, g in self.pairs if k > 0 and g > 0],
        )

    def source(self, mine, member, k, g):
        return lax.rem(mine - k + self.slots, self.slots) * self.groups + lax.rem(
            member - g + self.groups, self.groups
        )

    def mask(self, spot, order=0):
        return sum(bit for n, bit in enumerate(self.orders[order]) if (spot >> n) & 1)


def run_all(copies):
    for copy in copies:
        copy.start()
    for copy in copies:
        copy.wait()


def weight_copies(shape, row, own, foreign, dest, sems):
    rows = own.shape[0]
    copies = [pltpu.make_async_copy(own, dest.at[0, pl.ds(0, rows), :], sems.at[0])]
    for k in range(1, shape.slots):
        near, far = foreign[2 * (k - 1) : 2 * k]
        half, size, _ = near.shape
        for spot in range(shape.copies):
            piece = near.at[spot] if spot < half else far.at[spot - half]
            at = pl.multiple_of(jnp.bitwise_xor(row, shape.mask(spot)) * size, 16)
            copies.append(
                pltpu.make_async_copy(
                    piece,
                    dest.at[k, pl.ds(at, size), :],
                    sems.at[1 + (k - 1) * shape.copies + spot],
                )
            )
    return copies


def project_kernel(shape, seq, sc, norm_ref, down_ref, upx_ref, own_tok, own_w, *rest):
    slots, groups, parts = shape.slots, shape.groups, shape.parts
    toks = rest[: parts - 1]
    foreign = rest[parts - 1 : parts - 1 + 2 * (slots - 1)]
    rest = rest[parts - 1 + 2 * (slots - 1) :]
    qkv_ref, n1_ref, stats_ref, inner_ref, rows_ref = rest[:5]
    tok_ref, weights, tok_sem, weight_sem = rest[5:]
    _, width, span = tok_ref.shape
    dim = parts * width
    head_rows = upx_ref.shape[2] // 3
    heads_here = head_rows // HEAD_DIM
    block = span // groups
    mine, member, row = sc[0], sc[1], sc[3]

    tok_copies = []
    for n, (k, g) in enumerate(shape.pairs):
        source = own_tok.at[mine] if n == 0 else toks[n - 1]
        tok_copies.append(
            pltpu.make_async_copy(
                source, tok_ref.at[shape.source(mine, member, k, g)], tok_sem.at[n]
            )
        )
    weight_list = weight_copies(shape, row, own_w, foreign, weights, weight_sem)
    for copy in tok_copies + weight_list:
        copy.start()
    for copy in tok_copies:
        copy.wait()

    def norm_step(c, carry):
        cols = pl.ds(pl.multiple_of(c * LANES, LANES), LANES)
        x = tok_ref[:, :, cols].reshape(dim, LANES).astype(F32)
        mean = jnp.mean(x, 0, keepdims=True)
        center = x - mean
        rstd = lax.rsqrt(jnp.mean(center * center, 0, keepdims=True) + EPS)
        n1 = center * rstd * norm_ref[:, 0:1] + norm_ref[:, 1:2]
        n1_ref[:, cols] = n1.astype(BF)
        stats_ref[0:1, cols] = mean
        stats_ref[1:2, cols] = rstd
        return carry

    lax.fori_loop(0, span // LANES, norm_step, 0)
    stats_ref[2:8, :] = jnp.zeros((6, span), F32)
    for copy in weight_list:
        copy.wait()

    def proj_step(c, carry):
        start = pl.multiple_of(c * CHUNK, CHUNK)
        cols = pl.ds(start, CHUNK)
        n1 = n1_ref[:, cols]
        rank = down_ref.shape[0]
        inner = mm(down_ref[...], n1)
        line = lax.broadcasted_iota(jnp.int32, (rank, CHUNK), 0)
        inner_x = jnp.where(line == 48, 1.0, 0.5 * inner).astype(BF)
        inner_ref[:, cols] = inner_x
        spot = lax.broadcasted_iota(jnp.int32, (HEAD_PAD - HEAD_DIM, CHUNK), 0)
        place = start + lax.broadcasted_iota(jnp.int32, (HEAD_PAD - HEAD_DIM, CHUNK), 1)
        tails = (
            jnp.where(spot == 0, 1.0, 0.0),
            jnp.where((spot == 0) & (place >= seq), -1e30, 0.0),
            jnp.zeros((HEAD_PAD - HEAD_DIM, CHUNK), F32),
        )
        for k in range(slots):
            proj = mm(weights[k, 0 : 3 * head_rows, :], n1) + mm(upx_ref[k], inner_x, TN)
            for j in range(3):
                for h in range(heads_here):
                    at = j * head_rows + h * HEAD_DIM
                    piece = jnp.concatenate([proj[at : at + HEAD_DIM, :], tails[j]], 0)
                    qkv_ref[j, k * heads_here + h, :, cols] = piece.astype(BF)
        return carry

    lax.fori_loop(0, span // CHUNK, proj_step, 0)

    for g in range(groups):
        rows_ref[g] = tok_ref[:, :, g * block : (g + 1) * block].reshape(dim, block)


def project(shape, seq, scalars, norm, down, upx, own_tok, toks, own_w, foreign):
    slots, groups, parts = shape.slots, shape.groups, shape.parts
    _, width, span = own_tok.shape
    head_rows = upx.shape[2] // 3
    heads = slots * head_rows // HEAD_DIM
    dim = parts * width
    weight_rows = max([own_w.shape[0]] + [w.shape[1] * shape.copies for w in foreign])
    out = (
        jax.ShapeDtypeStruct((3, heads, HEAD_PAD, span), BF),
        jax.ShapeDtypeStruct((dim, span), BF),
        jax.ShapeDtypeStruct((8, span), F32),
        jax.ShapeDtypeStruct((down.shape[0], span), BF),
        jax.ShapeDtypeStruct((groups, dim, span // groups), BF),
    )
    return pl.pallas_call(
        partial(project_kernel, shape, seq),
        out_shape=out,
        in_specs=[smem()] + [vmem()] * 3 + [anywhere()] * (2 + len(toks) + len(foreign)),
        out_specs=tuple(vmem() for _ in out),
        scratch_shapes=[
            pltpu.VMEM((parts, width, span), BF),
            pltpu.VMEM((slots, weight_rows, dim), BF),
            pltpu.SemaphoreType.DMA((parts,)),
            pltpu.SemaphoreType.DMA((1 + (slots - 1) * shape.copies,)),
        ],
        compiler_params=pltpu.CompilerParams(vmem_limit_bytes=48 * MIB),
        cost_estimate=pl.CostEstimate(flops=4 * 10**9, bytes_accessed=40 * 10**6, transcendentals=10**6),
        name="project",
    )(scalars, norm, down, upx, own_tok, own_w, *toks, *foreign)


def attend_kernel(slots, groups, sc, qkv_ref, lse_ref, heads_ref, scr):
    span = scr.shape[1]
    head_rows = scr.shape[0] // slots
    block = span // groups
    h = pl.program_id(0)
    keys = qkv_ref[1, 0].T
    vals = qkv_ref[2, 0]
    at = pl.multiple_of(h * HEAD_DIM, 8)
    for c in range(span // CHUNK):
        cols = slice(c * CHUNK, (c + 1) * CHUNK)
        scores = mm(keys, qkv_ref[0, 0, :, cols]) * (SCALE * LOG2E)
        top = jnp.max(scores, 0, keepdims=True)
        raised = jnp.exp2(scores - top)
        total = jnp.sum(raised, 0, keepdims=True)
        out = mm(vals, raised.astype(BF)) / total
        scr[pl.ds(at, HEAD_DIM), cols] = out[0:HEAD_DIM, :]
        lse_ref[0, 0:1, cols] = top + jnp.log2(total)

    @pl.when(h == pl.num_programs(0) - 1)
    def _():
        for g in range(groups):
            cols = slice(g * block, (g + 1) * block)
            for k in range(slots):
                heads_ref[g, k] = scr[k * head_rows : (k + 1) * head_rows, cols].astype(BF)


def attend(shape, scalars, qkv):
    slots, groups = shape.slots, shape.groups
    _, heads, _, span = qkv.shape
    head_rows = heads * HEAD_DIM // slots
    out = (
        jax.ShapeDtypeStruct((heads, 1, span), F32),
        jax.ShapeDtypeStruct((groups, slots, head_rows, span // groups), BF),
    )
    return pl.pallas_call(
        partial(attend_kernel, slots, groups),
        grid=(heads,),
        out_shape=out,
        in_specs=[smem(), pl.BlockSpec((3, 1, HEAD_PAD, span), lambda h: (0, h, 0, 0))],
        out_specs=(
            pl.BlockSpec((1, 1, span), lambda h: (h, 0, 0)),
            pl.BlockSpec(out[1].shape, lambda h: (0, 0, 0, 0)),
        ),
        scratch_shapes=[pltpu.VMEM((slots * head_rows, span), F32)],
        compiler_params=pltpu.CompilerParams(vmem_limit_bytes=40 * MIB),
        cost_estimate=pl.CostEstimate(flops=4 * 10**9, bytes_accessed=60 * 10**6, transcendentals=5 * 10**6),
        name="attend",
    )(scalars, qkv)


def middle_kernel(
    shape, sizes, sc, vec_ref, tab_ref, rows_hbm, own_heads, own_expand, own_reduce, own_merge, *rest
):
    slots, groups, parts = shape.slots, shape.groups, shape.parts
    piece, merge_rows = sizes
    gathered, rest = rest[:12], rest[12:]
    heads_hbm = (own_heads,) + rest[: groups - 1]
    cots = rest[groups - 1 : groups - 1 + parts]
    facs = rest[groups - 1 + parts : groups - 1 + 2 * parts]
    rest = rest[groups - 1 + 2 * parts :]
    layer_ref, resid_ref, back_ref, gm_ref = rest[:4]
    both, wm, heads_rel, heads_in, rows_in, cot_in, fac_in = rest[4:11]
    acc_out, acc_back, n2x, gx, eug, rdg, sem, own_sem, w_sem = rest[11:]
    _, head_rows, block = heads_in.shape
    dim = parts * head_rows
    hidden_rows = fac_in.shape[2]
    full = parts * hidden_rows
    tail = slice(dim, dim + LANES)
    mine, member, valid, row, ident = sc[0], sc[1], sc[2], sc[3], sc[4]
    here = mine * groups + member

    small = [pltpu.make_async_copy(own_heads.at[member], heads_rel.at[0], sem.at[0])]
    for g in range(1, groups):
        small.append(pltpu.make_async_copy(heads_hbm[g], heads_rel.at[g], sem.at[g]))
    small.append(pltpu.make_async_copy(rows_hbm.at[member], rows_in, sem.at[groups]))
    for n, (k, g) in enumerate(shape.pairs):
        spot = shape.source(mine, member, k, g)
        at = groups + 1 + 2 * n
        small.append(pltpu.make_async_copy(cots[n], cot_in.at[spot], sem.at[at]))
        small.append(pltpu.make_async_copy(facs[n], fac_in.at[spot], sem.at[at + 1]))
    merges, mlps = [], []
    cols = pl.ds(0, dim)
    start = pl.multiple_of(here * hidden_rows, 16)
    for n, source in enumerate((own_expand, own_reduce)):
        mlps.append(
            pltpu.make_async_copy(
                source, both.at[n, pl.ds(start, hidden_rows), cols], own_sem.at[n]
            )
        )
    start = pl.multiple_of(here * head_rows, 16)
    merges.append(
        pltpu.make_async_copy(own_merge, wm.at[pl.ds(start, head_rows), cols], own_sem.at[2])
    )
    lines = (piece + merge_rows) // 2
    real = head_rows // merge_rows
    spare = shape.copies - real
    half = shape.copies // 2
    done = 0
    for batch in range(3):
        for order in range(2):
            near, far = gathered[4 * batch + 2 * order : 4 * batch + 2 * order + 2]
            for spot in range(shape.copies):
                origin = jnp.bitwise_xor(row, shape.mask(spot, order))
                for n, (k, g) in enumerate(shape.batches[batch]):
                    shard = shape.source(mine, member, k, g)
                    source = near.at[spot, n] if spot < half else far.at[spot - half, n]
                    first = order * lines
                    count = min(lines, piece - first)
                    index = (done + n) * 2 * shape.copies
                    index = index + 2 * spot + order
                    base = shard * hidden_rows + lax.rem(origin, half) * piece + first
                    mlps.append(
                        pltpu.make_async_copy(
                            source.at[pl.ds(0, count), :],
                            both.at[origin // half, pl.ds(pl.multiple_of(base, 16), count), cols],
                            w_sem.at[0, index],
                        )
                    )
                    if count < lines:
                        base = jnp.where(
                            origin < real,
                            shard * head_rows + origin * merge_rows,
                            dim + (shard * spare + origin - real) * merge_rows,
                        )
                        merges.append(
                            pltpu.make_async_copy(
                                source.at[pl.ds(count, merge_rows), :],
                                wm.at[pl.ds(pl.multiple_of(base, 16), merge_rows), cols],
                                w_sem.at[1, index],
                            )
                        )
        done += len(shape.batches[batch])
    for copy in small + merges + mlps:
        copy.start()
    for copy in small:
        copy.wait()

    for g in range(groups):
        for k in range(slots):
            spot = lax.rem(member - g + groups, groups) + groups * lax.rem(mine + k, slots)
            heads_in[spot] = heads_rel[g, k]
    heads = heads_in[...].reshape(dim, block).T
    grads = cot_in[...].reshape(dim, block).T * valid.astype(F32).astype(BF)

    for t in range(parts):
        fac = fac_in[t]
        spread = jnp.concatenate(
            [fac[0:16, :], fac[48:64, :], jnp.zeros((LANES - 32, hidden_rows), BF)], 0
        )
        both[0, t * hidden_rows : (t + 1) * hidden_rows, tail] = spread.T
        spread = jnp.concatenate([fac[16:32, :], jnp.zeros((LANES - 16, hidden_rows), BF)], 0)
        both[1, t * hidden_rows : (t + 1) * hidden_rows, tail] = spread.T
        spread = jnp.concatenate(
            [fac[32:48, 0:head_rows], jnp.zeros((LANES - 16, head_rows), BF)], 0
        )
        wm[t * head_rows : (t + 1) * head_rows, tail] = spread.T

    for copy in merges:
        copy.wait()
    merged = mm(heads, wm[0:dim, :])
    inner_m = (0.5 * merged[:, tail]).astype(BF)
    x = rows_in[...].T.astype(F32)
    hidden = x + merged[:, :dim] + mm(inner_m, tab_ref[0]) + vec_ref[0:1, :]
    mean = jnp.mean(hidden, 1, keepdims=True)
    center = hidden - mean
    rstd = lax.rsqrt(jnp.mean(center * center, 1, keepdims=True) + EPS)
    unit = center * rstd
    n2 = (unit * vec_ref[2:3, :] + vec_ref[3:4, :]).astype(BF)
    n2x[:, 0:dim] = n2
    lane = lax.broadcasted_iota(jnp.int32, (block, LANES), 1)
    inner_e = jnp.where(lane == 16, 1.0, 0.5 * mm(n2, tab_ref[1], NT)).astype(BF)
    n2x[:, tail] = inner_e
    gx[:, 0:dim] = grads
    thr_r = (0.5 * mm(grads, tab_ref[2], NT)).astype(BF)
    gx[:, tail] = thr_r
    inner_et = inner_e.T
    thr_rt = thr_r.T
    acc_out[...] = jnp.zeros_like(acc_out)
    acc_back[...] = jnp.zeros_like(acc_back)
    for copy in mlps:
        copy.wait()

    def step(c, carry):
        at = pl.ds(pl.multiple_of(c * CHUNK, CHUNK), CHUNK)
        we_c = both[0, at, :]
        wr_c = both[1, at, :]
        pre = mm(n2x[...], we_c, NT)
        grad_act = mm(gx[...], wr_c, NT)
        square = pre * pre
        th = jnp.tanh(pre * (0.7978845608028654 + 0.035677408136300125 * square))
        half = 0.5 * (1.0 + th)
        act = (pre * half).astype(BF)
        slope = half + pre * (0.5 * (1.0 - th * th)) * (
            0.7978845608028654 + 0.10703222440890037 * square
        )
        grad_pre = (grad_act * slope).astype(BF)
        acc_out[...] += mm(act, wr_c)
        acc_back[...] += mm(grad_pre, we_c)
        eug[:, at] = mm(inner_et[0:16, :], grad_pre)
        rdg[:, at] = mm(thr_rt[0:16, :], act)
        return carry

    lax.fori_loop(0, full // CHUNK, step, 0)

    inner_r = (0.5 * acc_out[:, tail]).astype(BF)
    layer = hidden + acc_out[:, 0:dim] + mm(inner_r, tab_ref[2]) + vec_ref[1:2, :]
    thr_e = (0.5 * acc_back[:, tail]).astype(BF)
    scaled = (acc_back[:, 0:dim] + mm(thr_e, tab_ref[1])) * vec_ref[2:3, :]
    first = jnp.mean(scaled, 1, keepdims=True)
    second = jnp.mean(scaled * unit, 1, keepdims=True)
    grad_hidden = grads.astype(F32) + rstd * (scaled - first - unit * second)
    branch = grad_hidden.astype(BF)
    thr_m = (0.5 * mm(branch, tab_ref[0], NT)).astype(BF)
    grad_heads = mm(branch, wm[0:dim, 0:dim], NT) + mm(thr_m, wm[0:dim, tail], NT)
    grad_heads_t = grad_heads.T.astype(BF)
    layer_t = layer.T.astype(BF)
    resid_ref[...] = grad_hidden.T
    for t in range(parts):
        at = slice(t * head_rows, (t + 1) * head_rows)
        layer_ref[t] = layer_t[at, :]
        back_ref[t % groups, lax.rem(t // groups - mine + slots, slots)] = grad_heads_t[at, :]

    whole = (
        mm(thr_m, heads, TN)[0:16, :],
        mm(inner_m, branch, TN)[0:16, :],
        mm(thr_e, n2, TN)[0:16, :],
        mm(inner_r, grads, TN)[0:16, :],
    )
    for t in range(parts):
        at = slice(t * hidden_rows, (t + 1) * hidden_rows)
        gm_ref[t, :, 0:hidden_rows] = eug[:, at].astype(BF)
        gm_ref[t, :, hidden_rows : 2 * hidden_rows] = rdg[:, at].astype(BF)
        for n in range(4):
            off = 2 * hidden_rows + n * head_rows
            gm_ref[t, :, off : off + head_rows] = whole[n][
                :, t * head_rows : (t + 1) * head_rows
            ].astype(BF)
        off = 2 * hidden_rows + 4 * head_rows
        gm_ref[t, :, off:] = jnp.full((16, gm_ref.shape[2] - off), ident, jnp.int32).astype(F32).astype(BF)


def middle(shape, sizes, scalars, vec, tab, rows, heads, own_w, gathered, cots, facs):
    slots, groups, parts = shape.slots, shape.groups, shape.parts
    own_heads, others = heads
    _, _, head_rows, block = own_heads.shape
    dim = parts * head_rows
    hidden_rows = facs[0].shape[1]
    full = parts * hidden_rows
    cols = up_to(2 * hidden_rows + 4 * head_rows + 1, LANES)
    spare = parts * (shape.copies - head_rows // sizes[1]) * sizes[1]
    out = (
        jax.ShapeDtypeStruct((parts, head_rows, block), BF),
        jax.ShapeDtypeStruct((dim, block), F32),
        jax.ShapeDtypeStruct((groups, slots, head_rows, block), BF),
        jax.ShapeDtypeStruct((parts, 16, cols), BF),
    )
    return pl.pallas_call(
        partial(middle_kernel, shape, sizes),
        out_shape=out,
        in_specs=[smem()] + [vmem()] * 2 + [anywhere()] * (5 + len(gathered) + len(others) + 2 * parts),
        out_specs=tuple(vmem() for _ in out),
        scratch_shapes=[
            pltpu.VMEM((2, full, dim + LANES), BF),
            pltpu.VMEM((dim + spare, dim + LANES), BF),
            pltpu.VMEM((groups, slots, head_rows, block), BF),
            pltpu.VMEM((parts, head_rows, block), BF),
            pltpu.VMEM((dim, block), BF),
            pltpu.VMEM((parts, head_rows, block), BF),
            pltpu.VMEM((parts, 64, hidden_rows), BF),
            pltpu.VMEM((block, dim + LANES), F32),
            pltpu.VMEM((block, dim + LANES), F32),
            pltpu.VMEM((block, dim + LANES), BF),
            pltpu.VMEM((block, dim + LANES), BF),
            pltpu.VMEM((16, full), F32),
            pltpu.VMEM((16, full), F32),
            pltpu.SemaphoreType.DMA((groups + 1 + 2 * parts,)),
            pltpu.SemaphoreType.DMA((3,)),
            pltpu.SemaphoreType.DMA((2, 2 * parts * shape.copies)),
        ],
        compiler_params=pltpu.CompilerParams(vmem_limit_bytes=60 * MIB),
        cost_estimate=pl.CostEstimate(flops=20 * 10**9, bytes_accessed=100 * 10**6, transcendentals=2 * 10**6),
        name="middle",
    )(scalars, vec, tab, rows, own_heads, *own_w, *gathered, *others, *cots, *facs)


def heads_back_kernel(shape, slot, sc, qkv_ref, lse_ref, own_dout, *rest):
    groups = shape.groups
    douts = (own_dout,) + rest[: groups - 1]
    out_ref, dout_rel, dot_scr, grad_scr, sem = rest[groups - 1 :]
    _, head_rows, block = dout_rel.shape
    span = groups * block
    heads_here = head_rows // HEAD_DIM
    member = sc[1]
    h = pl.program_id(0)

    @pl.when(h == 0)
    def _():
        copies = []
        for g in range(groups):
            source = own_dout.at[member, slot] if g == 0 else douts[g].at[slot]
            spot = lax.rem(member - g + groups, groups)
            copies.append(pltpu.make_async_copy(source, dout_rel.at[spot], sem.at[g]))
        run_all(copies)
        pad = jnp.zeros((HEAD_PAD - HEAD_DIM, block), F32)
        for g in range(groups):
            piece = dout_rel[g].astype(F32)
            for n in range(heads_here):
                one = jnp.concatenate([piece[n * HEAD_DIM : (n + 1) * HEAD_DIM, :], pad], 0)
                dot_scr[n, :, g * block : (g + 1) * block] = one.astype(BF)

    query_t = qkv_ref[0, 0]
    keys_t = qkv_ref[1, 0]
    query = query_t.T
    keys = keys_t.T
    vals = qkv_ref[2, 0].T
    dout_t = dot_scr[h]
    dout = dout_t.T
    dvals = jnp.zeros((span, HEAD_PAD), F32)
    dkeys = jnp.zeros((span, HEAD_PAD), F32)
    row = pl.multiple_of(h * HEAD_DIM, 8)
    for c in range(span // CHUNK):
        cols = slice(c * CHUNK, (c + 1) * CHUNK)
        scores = mm(keys, query_t[:, cols]) * (SCALE * LOG2E)
        probs = jnp.exp2(scores - lse_ref[0, 0:1, cols])
        dprobs = mm(vals, dout_t[:, cols])
        delta = jnp.sum(probs * dprobs, 0, keepdims=True)
        dscores = (probs * (dprobs - delta)).astype(BF)
        dvals += mm(probs.astype(BF), dout[cols, :])
        dkeys += mm(dscores, query[cols, :])
        dquery = mm(keys_t, dscores) * SCALE
        grad_scr[pl.ds(row, HEAD_DIM), cols] = dquery[0:HEAD_DIM, :]
    row = pl.multiple_of(row + head_rows, 8)
    grad_scr[pl.ds(row, HEAD_DIM), :] = (dkeys * SCALE).T[0:HEAD_DIM, :]
    row = pl.multiple_of(row + head_rows, 8)
    grad_scr[pl.ds(row, HEAD_DIM), :] = dvals.T[0:HEAD_DIM, :]

    @pl.when(h == heads_here - 1)
    def _():
        out_ref[...] = grad_scr[...].astype(BF)


def heads_back(shape, slot, scalars, qkv, lse, dout):
    own, others = dout
    groups, _, head_rows, block = own.shape
    span = groups * block
    heads_here = head_rows // HEAD_DIM
    return pl.pallas_call(
        partial(heads_back_kernel, shape, slot),
        grid=(heads_here,),
        out_shape=jax.ShapeDtypeStruct((3 * head_rows, span), BF),
        in_specs=[
            smem(),
            pl.BlockSpec((3, 1, HEAD_PAD, span), lambda h: (0, slot * heads_here + h, 0, 0)),
            pl.BlockSpec((1, 1, span), lambda h: (slot * heads_here + h, 0, 0)),
            anywhere(),
        ]
        + [anywhere()] * len(others),
        out_specs=pl.BlockSpec((3 * head_rows, span), lambda h: (0, 0)),
        scratch_shapes=[
            pltpu.VMEM((groups, head_rows, block), BF),
            pltpu.VMEM((heads_here, HEAD_PAD, span), BF),
            pltpu.VMEM((3 * head_rows, span), F32),
            pltpu.SemaphoreType.DMA((groups,)),
        ],
        compiler_params=pltpu.CompilerParams(vmem_limit_bytes=40 * MIB),
        cost_estimate=pl.CostEstimate(flops=4 * 10**9, bytes_accessed=40 * 10**6, transcendentals=3 * 10**6),
        name="heads_back",
    )(scalars, qkv, lse, own, *others)


def rank_back_kernel(shape, sc, down_ref, upx_ref, n1_ref, inner_ref, *rest):
    slots, groups, parts = shape.slots, shape.groups, shape.parts
    grads = rest[:slots]
    td_ref, thr_ref, tu_scr = rest[slots:]
    dim, span = n1_ref.shape
    width = dim // parts
    head_rows = upx_ref.shape[2] // 3
    mine, member, ident = sc[0], sc[1], sc[4]
    rank = down_ref.shape[0]
    spread = 3 * head_rows
    thr = jnp.zeros((rank, span), F32)
    row_of = lax.broadcasted_iota(jnp.int32, (rank, spread), 0) // 16
    part_of = lax.broadcasted_iota(jnp.int32, (rank, spread), 1) // head_rows
    for k in range(slots):
        thr = thr + mm(upx_ref[k], grads[k][...])
        ups = mm(inner_ref[...], grads[k][...], NT)
        ups = jnp.where(row_of == part_of, ups, 0.0)
        tu_scr[k] = ups[0:16, :] + ups[16:32, :] + ups[32:48, :]
    line = lax.broadcasted_iota(jnp.int32, (rank, span), 0)
    thr_b = jnp.where(line < 48, 0.5 * thr, 0.0).astype(BF)
    thr_ref[...] = thr_b
    downs = mm(thr_b, n1_ref[...], NT)
    rest_cols = td_ref.shape[2] - width - head_rows
    ids = jnp.full((48, rest_cols), ident, jnp.int32).astype(F32)
    for t in range(parts):
        own = jnp.where(member == t % groups, 1.0, 0.0)
        ups = tu_scr[lax.rem(t // groups - mine + slots, slots)] * own
        ups = jnp.concatenate([ups[:, j * head_rows : (j + 1) * head_rows] for j in range(3)], 0)
        down_part = downs[0:48, t * width : (t + 1) * width]
        td_ref[t] = jnp.concatenate([down_part, ups, ids], 1).astype(BF)


def rank_back(shape, scalars, down, upx, n1, inner, grads):
    slots, parts = shape.slots, shape.parts
    dim, span = n1.shape
    head_rows = upx.shape[2] // 3
    cols = up_to(dim // parts + head_rows + 1, LANES)
    out = (
        jax.ShapeDtypeStruct((parts, 48, cols), BF),
        jax.ShapeDtypeStruct((down.shape[0], span), BF),
    )
    return pl.pallas_call(
        partial(rank_back_kernel, shape),
        out_shape=out,
        in_specs=[smem()] + [vmem()] * (4 + slots),
        out_specs=(vmem(), vmem()),
        scratch_shapes=[pltpu.VMEM((slots, 16, 3 * head_rows), F32)],
        compiler_params=pltpu.CompilerParams(vmem_limit_bytes=40 * MIB),
        cost_estimate=pl.CostEstimate(flops=10**9, bytes_accessed=10 * 10**6, transcendentals=0),
        name="rank_back",
    )(scalars, down, upx, n1, inner, *grads)


def norm_back_kernel(shape, sc, norm_ref, down_ref, thr_ref, stats_ref, rows_ref, resid_ref, own_w, *rest):
    slots, groups, parts = shape.slots, shape.groups, shape.parts
    foreign = rest[: 2 * (slots - 1)]
    rest = rest[2 * (slots - 1) :]
    grads = rest[:slots]
    out_ref, weights, e1_scr, sem = rest[slots:]
    _, dim, block = rows_ref.shape
    span = groups * block
    width = dim // parts
    spread = own_w.shape[0]
    member, row = sc[1], sc[3]
    run_all(weight_copies(shape, row, own_w, foreign, weights, sem))

    def final_step(c, carry):
        cols = pl.ds(pl.multiple_of(c * CHUNK, CHUNK), CHUNK)
        total = mm(down_ref[...], thr_ref[:, cols], TN)
        for k in range(slots):
            total = total + mm(weights[k, 0:spread, :], grads[k][:, cols], TN)
        e1_scr[:, cols] = total * norm_ref[:, 0:1]
        return carry

    lax.fori_loop(0, span // CHUNK, final_step, 0)
    for g in range(groups):
        cols = slice(g * block, (g + 1) * block)
        e1 = e1_scr[:, cols]
        first = jnp.sum(e1, 0, keepdims=True)
        mean, rstd = stats_ref[0:1, cols], stats_ref[1:2, cols]
        unit = (rows_ref[g].astype(F32) - mean) * rstd
        second = jnp.sum(e1 * unit, 0, keepdims=True)
        lines = []
        for value in (first, second, mean, rstd):
            high = value.astype(BF).astype(F32)
            lines += [high, value - high]
        lines = jnp.concatenate(lines + [jnp.zeros((8, block), F32)], 0).astype(BF)
        e1 = e1 + resid_ref[...] * (jnp.where(member == g, 1.0, 0.0) / rstd)
        for t in range(parts):
            out_ref[t, 0:width, cols] = e1[t * width : (t + 1) * width, :].astype(BF)
            out_ref[t, width : width + 16, cols] = lines


def norm_back(shape, scalars, norm, down, thr, stats, rows, resid, own_w, foreign, grads):
    slots, parts = shape.slots, shape.parts
    groups, dim, block = rows.shape
    span = groups * block
    weight_rows = max([own_w.shape[0]] + [w.shape[1] * shape.copies for w in foreign])
    return pl.pallas_call(
        partial(norm_back_kernel, shape),
        out_shape=jax.ShapeDtypeStruct((parts, dim // parts + 16, span), BF),
        in_specs=[smem()] + [vmem()] * 6 + [anywhere()] * (1 + len(foreign)) + [vmem()] * slots,
        out_specs=vmem(),
        scratch_shapes=[
            pltpu.VMEM((slots, weight_rows, dim), BF),
            pltpu.VMEM((dim, span), F32),
            pltpu.SemaphoreType.DMA((1 + (slots - 1) * shape.copies,)),
        ],
        compiler_params=pltpu.CompilerParams(vmem_limit_bytes=48 * MIB),
        cost_estimate=pl.CostEstimate(flops=3 * 10**9, bytes_accessed=20 * 10**6, transcendentals=0),
        name="norm_back",
    )(scalars, norm, down, thr, stats, rows, resid, own_w, *foreign, *grads)


def tokens_kernel(shape, seq, sc, img_ref, own, *rest):
    slots, groups, parts = shape.slots, shape.groups, shape.parts
    out_ref, held, sem = rest[parts - 1 :]
    mine, member, place = sc[0], sc[1], sc[5]
    _, width, span = img_ref.shape
    dim = parts * width
    copies = []
    for n, (k, g) in enumerate(shape.pairs):
        source = own.at[place] if n == 0 else rest[n - 1]
        copies.append(
            pltpu.make_async_copy(source, held.at[shape.source(mine, member, k, g)], sem.at[n])
        )
    run_all(copies)
    for n in range(slots):
        total = held[n * groups].astype(F32)
        lines = total[width : width + 16, :]
        mean = lines[4:5, :] + lines[5:6, :]
        rstd = lines[6:7, :] + lines[7:8, :]
        for g in range(1, groups):
            total = total + held[n * groups + g].astype(F32)
        first = (total[width : width + 1, :] + total[width + 1 : width + 2, :]) / dim
        second = (total[width + 2 : width + 3, :] + total[width + 3 : width + 4, :]) / dim
        unit = (img_ref[n].astype(F32) - mean) * rstd
        grad = rstd * (total[0:width, :] - first - unit * second)
        out_ref[:, n * seq : (n + 1) * seq] = grad[:, 0:seq]


def tokens_result(shape, seq, scalars, images, own, others):
    slots, parts = shape.slots, shape.parts
    _, width, span = images.shape
    return pl.pallas_call(
        partial(tokens_kernel, shape, seq),
        out_shape=jax.ShapeDtypeStruct((width, slots * seq), F32),
        in_specs=[smem(), vmem()] + [anywhere()] * parts,
        out_specs=vmem(),
        scratch_shapes=[
            pltpu.VMEM((parts, width + 16, span), BF),
            pltpu.SemaphoreType.DMA((parts,)),
        ],
        compiler_params=pltpu.CompilerParams(vmem_limit_bytes=40 * MIB),
        cost_estimate=pl.CostEstimate(flops=10**7, bytes_accessed=6 * 10**6, transcendentals=0),
        name="tokens_result",
    )(scalars, images, own, *others)


def layer_kernel(shape, seq, sc, own, *rest):
    slots, groups, parts = shape.slots, shape.groups, shape.parts
    out_ref, held, sem = rest[parts - 1 :]
    mine, member, place = sc[0], sc[1], sc[5]
    copies = []
    for n, (k, g) in enumerate(shape.pairs):
        source = own.at[place] if n == 0 else rest[n - 1]
        copies.append(
            pltpu.make_async_copy(source, held.at[shape.source(mine, member, k, g)], sem.at[n])
        )
    run_all(copies)
    for n in range(slots):
        image = jnp.concatenate([held[n * groups + g].astype(F32) for g in range(groups)], 1)
        out_ref[:, n * seq : (n + 1) * seq] = image[:, 0:seq].astype(BF)


def layer_result(shape, seq, scalars, own, others):
    slots, parts = shape.slots, shape.parts
    _, width, block = own.shape
    return pl.pallas_call(
        partial(layer_kernel, shape, seq),
        out_shape=jax.ShapeDtypeStruct((width, slots * seq), BF),
        in_specs=[smem()] + [anywhere()] * parts,
        out_specs=vmem(),
        scratch_shapes=[
            pltpu.VMEM((parts, width, block), BF),
            pltpu.SemaphoreType.DMA((parts,)),
        ],
        compiler_params=pltpu.CompilerParams(vmem_limit_bytes=40 * MIB),
        cost_estimate=pl.CostEstimate(flops=10**7, bytes_accessed=3 * 10**6, transcendentals=0),
        name="layer_result",
    )(scalars, own, *others)


def tables_kernel(shape, sc, downs, held, downs_ref, merge_ref, expand_ref, reduce_ref, downs_in, held_in, sem):
    mine, member = sc[0], sc[1]
    copies = []
    for n, (k, g) in enumerate(shape.pairs):
        spot = shape.source(mine, member, k, g)
        copies.append(pltpu.make_async_copy(downs.at[:, n], downs_in.at[:, spot], sem.at[0, n]))
        copies.append(pltpu.make_async_copy(held.at[:, n], held_in.at[:, spot], sem.at[1, n]))
    run_all(copies)
    adapters = downs_ref.shape[1]
    width = downs_in.shape[3]
    for t in range(shape.parts):
        lanes = slice(t * width, (t + 1) * width)
        rows = downs_in[:, t].astype(F32).reshape(adapters * 48, width)
        for a in range(adapters):
            for j in range(3):
                downs_ref[j, a, :, lanes] = rows[48 * a + 16 * j : 48 * a + 16 * j + 16, :]
        rows = held_in[:, t].astype(F32).reshape(adapters, 16, 3 * width)
        for n, ref in enumerate((merge_ref, expand_ref, reduce_ref)):
            ref[:, :, lanes] = rows[:, :, n * width : (n + 1) * width]


def whole_tables(shape, scalars, downs, held):
    copies, parts, rows, width = downs.shape
    adapters = copies * rows // 48
    dim = parts * width
    out = (jax.ShapeDtypeStruct((3, adapters, 16, dim), F32),) + (
        jax.ShapeDtypeStruct((adapters, 16, dim), F32),
    ) * 3
    result = pl.pallas_call(
        partial(tables_kernel, shape),
        out_shape=out,
        in_specs=[smem(), anywhere(), anywhere()],
        out_specs=tuple(vmem() for _ in out),
        scratch_shapes=[
            pltpu.VMEM(downs.shape, BF),
            pltpu.VMEM(held.shape, BF),
            pltpu.SemaphoreType.DMA((2, parts)),
        ],
        compiler_params=pltpu.CompilerParams(vmem_limit_bytes=40 * MIB),
        cost_estimate=pl.CostEstimate(flops=10**7, bytes_accessed=6 * 10**6, transcendentals=0),
        name="whole_tables",
    )(scalars, downs, held)
    return result[0], result[1:]


def by_adapter_kernel(parts_of, adapters, count, terms_ref, *outs):
    images, rows, cols = terms_ref.shape
    for spot, (first, size) in enumerate(parts_of):
        for a in range(adapters):
            total = jnp.zeros((rows, size), F32)
            for e in range(images):
                which = terms_ref[e, 0:1, cols - 1 : cols].astype(F32)
                chosen = jnp.where(jnp.abs(which - a * count) < 0.5, 1.0, 0.0)
                total = total + terms_ref[e, :, first : first + size].astype(F32) * chosen
            outs[spot][a] = total.astype(outs[spot].dtype)


def by_adapter(terms, adapters, count, parts_of, types):
    images, rows, cols = terms.shape
    out = tuple(
        jax.ShapeDtypeStruct((adapters, rows, size), kind)
        for (_, size), kind in zip(parts_of, types, strict=True)
    )
    return pl.pallas_call(
        partial(by_adapter_kernel, parts_of, adapters, count),
        out_shape=out,
        in_specs=[vmem()],
        out_specs=tuple(vmem() for _ in out),
        compiler_params=pltpu.CompilerParams(vmem_limit_bytes=40 * MIB),
        cost_estimate=pl.CostEstimate(flops=10**7, bytes_accessed=5 * 10**6, transcendentals=0),
        name="by_adapter",
    )(terms)


def shards(
    tokens,
    cotangent,
    adapter_index,
    valid_image,
    first_gain,
    first_shift,
    triple_weight,
    triple_bias,
    triple_down,
    triple_up,
    merge_weight,
    merge_bias,
    merge_down,
    merge_up,
    second_gain,
    second_shift,
    expand_weight,
    expand_bias,
    expand_down,
    expand_up,
    reduce_weight,
    reduce_bias,
    reduce_down,
    reduce_up,
    *,
    parts,
    copies,
):
    slots = adapter_index.shape[0]
    shape = Shape(parts, slots, copies)
    groups = shape.groups
    seq = tokens.shape[0] // slots
    width = tokens.shape[1]
    dim = width * parts
    head_rows = triple_weight.shape[2]
    adapters = triple_down.shape[1]
    span = up_to(seq, CHUNK)
    block = span // groups
    place = lax.axis_index("tensor")
    row = lax.axis_index("dp")
    mine, member = place // groups, place % groups

    def at(x, n, axis=0):
        return lax.dynamic_index_in_dim(x, n, axis, False)

    index = at(adapter_index, mine)
    valid = at(valid_image, mine)
    scalars = jnp.stack([mine, member, valid, row, index, place]).astype(jnp.int32)

    def jump(x, k, g):
        perm = [
            (s, ((s // groups + k) % slots) * groups + (s % groups + g) % groups)
            for s in range(parts)
        ]
        return lax.ppermute(x, "tensor", perm)

    def swap(pick):
        return [
            jump(pick((mine + k) % slots, (member + g) % groups), k, g)
            for k, g in shape.pairs[1:]
        ]

    def spread_images(x):
        first = [at(x, mine)] + [jump(at(x, (mine + k) % slots), k, 0) for k in range(1, slots)]
        out = []
        for x_k in first:
            out.append(x_k)
            out += [jump(x_k, 0, g) for g in range(1, groups)]
        return out

    def cross(x, bit):
        return lax.ppermute(x, "dp", [(d, d ^ bit) for d in range(copies)])

    def widen(near, bits):
        for bit in bits:
            near = jnp.concatenate([near, cross(near, bit)], 0)
        return near

    def hyper(near, order):
        near = widen(near, order[:-1])
        return [near, cross(near, order[-1])]

    def after(x, *others):
        return lax.optimization_barrier((x, *others))[0]

    def images_of(x):
        flat = x.T
        return jnp.stack(
            [
                jnp.pad(flat[:, n * seq : (n + 1) * seq], ((0, 0), (0, span - seq)))
                for n in range(slots)
            ]
        )

    images = images_of(tokens)
    toks = spread_images(images)[1:]
    ready = toks[groups - 1]

    flat_triple = triple_weight.transpose(0, 2, 1).reshape(3 * head_rows, dim)
    piece_rows = up_to(3 * head_rows, 16 * copies) // copies
    padded = jnp.pad(flat_triple, ((0, piece_rows * copies - 3 * head_rows), (0, 0)))
    my_piece = lax.dynamic_slice_in_dim(padded, row * piece_rows, piece_rows, 0)
    foreign = []
    for k in range(1, slots):
        foreign += hyper(jump(my_piece, -k, 0)[None], shape.bits)

    merge_rows = up_to(width, 16 * copies) // copies
    merge_piece = lax.dynamic_slice_in_dim(
        jnp.pad(merge_weight, ((0, merge_rows * copies - width), (0, 0))), row * merge_rows, merge_rows, 0
    )
    hidden_here = reduce_weight.shape[0]
    hidden_rows = up_to(hidden_here, 8 * copies)
    extra = ((0, hidden_rows - hidden_here), (0, 0))
    mlp_rows = 2 * hidden_rows // copies
    half = copies // 2

    def mlp_part(x):
        return lax.dynamic_slice_in_dim(jnp.pad(x, extra), (row % half) * mlp_rows, mlp_rows, 0)

    mlp_piece = jnp.where(row < half, mlp_part(expand_weight.T), mlp_part(reduce_weight))
    my_w = jnp.concatenate([mlp_piece, merge_piece], 0)
    lines = my_w.shape[0] // 2

    def halves(pieces):
        return [
            jnp.stack([x[order * lines : (order + 1) * lines] for x in pieces])[None]
            for order in range(2)
        ]

    def step(pieces, first, last=None):
        return [widen(x, order[first:last]) for x, order in zip(pieces, shape.orders)]

    def cores(pieces):
        out = []
        for x in pieces:
            out += [x, cross(x, shape.bits[-1])]
        return out

    pair_w = halves([jump(my_w, 0, g) for _, g in shape.batches[0]])
    late_w = after(my_w, ready)
    cross_w = [jump(late_w, k, 0) for k, _ in shape.batches[1]]
    pair_w = step(pair_w, 0, -1)
    gathered = cores(pair_w)
    own_expand = jnp.pad(after(expand_weight.T, ready), extra)
    own_reduce = jnp.pad(after(reduce_weight, ready), extra)

    def up_pack(which):
        table = at(triple_up, which, 1)
        lines = [
            jnp.pad(table[j], ((0, 0), (j * head_rows, (2 - j) * head_rows))) for j in range(3)
        ]
        bias = jnp.pad(triple_bias.reshape(1, 3 * head_rows), ((0, 15), (0, 0)))
        return jnp.concatenate(lines + [bias], 0)

    ups = [up_pack(index)]
    for k in range(1, slots):
        ups.append(jump(up_pack(at(adapter_index, (mine - k) % slots)), -k, 0))
    upx = jnp.stack(ups)
    down = jnp.pad(at(triple_down, index, 1).transpose(0, 2, 1).reshape(48, dim), ((0, 16), (0, 0)))
    norm = jnp.pad(jnp.stack([first_gain, first_shift], 1).astype(F32), ((0, 0), (0, 6)))

    late_index = after(adapter_index, ready)

    def factor_pack(which):
        def lanes(x):
            return jnp.pad(x, ((0, 16 - x.shape[0]), (0, hidden_rows - x.shape[1])))

        return jnp.concatenate(
            [
                lanes(at(expand_up, which)),
                lanes(at(reduce_down, which).T),
                lanes(at(merge_down, which).T),
                lanes(expand_bias[None, :]),
            ],
            0,
        )

    fac_parts = jnp.stack([factor_pack(late_index[n]) for n in range(slots)])
    late = after(index, ready)
    tab = jnp.stack(
        [
            jnp.pad(x, ((0, LANES - 16), (0, 0)))
            for x in (at(merge_up, late), at(expand_down, late).T, at(reduce_up, late))
        ]
    )
    vec = jnp.pad(
        jnp.stack([merge_bias, reduce_bias, second_gain, second_shift]).astype(F32), ((0, 4), (0, 0))
    )

    cot_images = images_of(after(cotangent, ready))

    def trade(x):
        return x, [jump(at(x, (member + g) % groups), 0, g) for g in range(1, groups)]

    begin = after(scalars, own_expand, own_reduce, tab, vec, fac_parts, cot_images, *pair_w)
    qkv, n1, stats, inner, rows = project(
        shape, seq, begin, norm, down, upx, images, toks, flat_triple, foreign
    )
    cross_w = [after(x, stats) for x in cross_w]
    far_w = halves([jump(cross_w[k - 1], 0, g) for k, g in shape.batches[2]])
    cross_w = halves(cross_w)
    late_starts = cross_w
    cross_w = step(cross_w, 0, 1)
    late_cot = after(cot_images, stats)

    def cot_part(i, m):
        return lax.dynamic_slice(late_cot, (i, 0, m * block), (1, width, block))[0]

    cots = [cot_part(mine, member)] + swap(cot_part)
    facs = spread_images(after(fac_parts, stats))
    lse, heads = attend(shape, after(scalars, late_cot, *late_starts), qkv)
    heads = trade(heads)
    cross_w = step([after(x, lse) for x in cross_w], 1, -1)
    far_w = step([after(x, lse) for x in far_w], 0, 1)
    gathered += cores([after(x, *heads[1]) for x in cross_w])
    gathered += cores(step([after(x, *heads[1]) for x in far_w], 1, -1))
    layer, resid, back, gm = middle(
        shape,
        (mlp_rows, merge_rows),
        scalars,
        vec,
        tab,
        rows,
        heads,
        (own_expand, own_reduce, merge_weight),
        gathered,
        cots,
        facs,
    )
    dout = trade(back)

    def spread_rows(x):
        share = x.shape[0] // copies
        own = lax.dynamic_slice_in_dim(x, row * share, share, 0)
        return jnp.stack([own] + [jump(own, k, g) for k, g in shape.pairs[1:]])

    def by_place(x):
        return lambda i, m: at(x, i * groups + m)

    def sum_members(own, others):
        pieces = [at(own, place)] + others
        sums = []
        for k in range(slots):
            total = pieces[k * groups].astype(F32)
            for g in range(1, groups):
                total = total + pieces[k * groups + g].astype(F32)
            sums.append(total.astype(BF))
        return jnp.stack(sums)

    gm_own, gm_others = gm, swap(by_place(gm))
    layers = swap(by_place(layer))
    grads = [heads_back(shape, 0, scalars, qkv, lse, dout)]
    gm = sum_members(after(gm_own, grads[0]), gm_others)
    near = [gm] + [cross(gm, d) for d in range(2, copies, 2)]
    for k in range(1, slots):
        grads.append(heads_back(shape, k, after(scalars, gm), qkv, lse, dout))
    near = after(jnp.concatenate(near, 0), grads[-1])
    gm = jnp.concatenate([near, cross(near, 1)], 0)
    td, thr = rank_back(shape, scalars, down, upx, n1, inner, grads)
    td_own, td_others = td, swap(by_place(td))
    last = norm_back(shape, scalars, norm, down, thr, stats, rows, resid, flat_triple, foreign, grads)
    lasts = swap(by_place(last))
    td = sum_members(after(td_own, last), td_others)
    td = lax.all_gather(td, "dp", tiled=True)
    down_terms, up_terms = by_adapter(
        td, adapters, groups, ((0, width), (width, head_rows)), (BF, F32)
    )
    downs = spread_rows(down_terms.reshape(adapters * 48, width))
    off = 2 * hidden_rows
    expand_up_grad, reduce_down_grad, merge_down_grad, held = by_adapter(
        after(gm, last),
        adapters,
        groups,
        ((0, hidden_here), (hidden_rows, hidden_here), (off, width), (off + width, 3 * width)),
        (F32, F32, F32, BF),
    )
    held = spread_rows(held.reshape(adapters * 16, 3 * width))
    layer_out = layer_result(shape, seq, after(scalars, last), layer, layers).T
    downs, held = whole_tables(shape, scalars, lax.all_gather(downs, "dp"), lax.all_gather(held, "dp"))
    tokens_grad = tokens_result(shape, seq, after(scalars, downs), images, last, lasts).T
    triple_up_grad = up_terms.reshape(adapters, 3, 16, head_rows).transpose(1, 0, 2, 3)

    return (
        layer_out,
        tokens_grad,
        downs.transpose(0, 1, 3, 2),
        triple_up_grad,
        merge_down_grad.transpose(0, 2, 1),
        held[0],
        held[1].transpose(0, 2, 1),
        expand_up_grad,
        reduce_down_grad.transpose(0, 2, 1),
        held[2],
    )


def solution(mesh):
    in_specs = (
        P("dp", "tensor"),
        P("dp", "tensor"),
        P("dp"),
        P("dp"),
        P(),
        P(),
        P(None, None, "tensor"),
        P(None, "tensor"),
        P(),
        P(None, None, None, "tensor"),
        P("tensor", None),
        P(),
        P(None, "tensor", None),
        P(),
        P(),
        P(),
        P(None, "tensor"),
        P("tensor"),
        P(),
        P(None, None, "tensor"),
        P("tensor", None),
        P(),
        P(None, "tensor", None),
        P(),
    )
    out_specs = (
        P("dp", "tensor"),
        P("dp", "tensor"),
        P(),
        P(None, None, None, "tensor"),
        P(None, "tensor", None),
        P(),
        P(),
        P(None, None, "tensor"),
        P(None, "tensor", None),
        P(),
    )
    return jax.shard_map(
        partial(shards, parts=mesh.shape["tensor"], copies=mesh.shape["dp"]),
        mesh=mesh,
        in_specs=in_specs,
        out_specs=out_specs,
        check_vma=False,
    )
```

time: 573 us -> 419 us (0.73)
  waiting for transfers between devices: 219 us -> 119 us
  blocking collectives: 95.6 us -> 32 us
  local copies, waits for them, and re-layouts: 73.3 us -> 33.5 us
  starting transfers between devices: 35.1 us -> 72.9 us
  Pallas kernels: 97.6 us -> 128 us
  between operations: 23.6 us -> 11.8 us
    all_gather x5 -> x0, waiting for transfers between devices: 138 us -> none  [the longest x1 132 us: shards(): lax.all_gather(mlp_piece, ('tensor', 'dp'))]
    all_gather x3, blocking collectives: 88.2 us -> 32 us  [the longest x1 11.4 us: shards(): lax.all_gather(downs, 'dp')]
    ppermute x11 -> x59, starting transfers between devices: 18.1 us -> 72.9 us  [the longest x34 52.5 us: jump(): return lax.ppermute(x, 'tensor', perm)]
    ppermute x11 -> x59, waiting for transfers between devices: 68.7 us -> 119 us  [the longest x34 62.1 us: jump(): return lax.ppermute(x, 'tensor', perm)]
    pallas_call x3 -> x12, Pallas kernels: 97.6 us -> 128 us  [the longest x1 45.4 us: middle(): pl.pallas_call(partial(middle_kernel, shape, sizes), out_shape=out, in_sp...]
    all_to_all x4 -> x0, starting transfers between devices: 16.9 us -> none  [the longest x2 8.33 us: trade(): return lax.all_to_all(x, 'tensor', 0, 0, axis_index_groups=group_list)]
    slice x10 -> x1, local copies, waits for them, and re-layouts: 13.7 us -> 0.58 us  [shards(): fac_parts = jnp.stack([factor_pack(late_index[n]) for n in range(slots)])]
    all_to_all x4 -> x0, waiting for transfers between devices: 12.4 us -> none  [the longest x2 12.4 us: trade(): return lax.all_to_all(x, 'tensor', 0, 0, axis_index_groups=group_list)]
  transfers between devices with their start and end apart: 20 -> 59, of which waited for: 7 -> 23; matrix products, arithmetic and copies ran while one was open for 12% -> 10% of each run, Pallas kernels for 10% -> 19%
where the time goes in v2:
time: 419 us; the launch traced here: 414 us
  Pallas kernels  128 us (31%)
  waiting for transfers between devices  119 us (28%)
  starting transfers between devices  72.9 us (17%)
  local copies, waits for them, and re-layouts  33.5 us (8%)
  blocking collectives  32 us (8%)
  other arithmetic  16.5 us (4%)
  between operations  11.8 us (3%)
    ppermute x34, waiting for transfers between devices, jump(): return lax.ppermute(x, 'tensor', perm)  62.1 us
    ppermute x25, waiting for transfers between devices, cross(): return lax.ppermute(x, 'dp', [(d, d ^ bit) for d in range(copies)])  57.2 us
    ppermute x34, starting transfers between devices, jump(): return lax.ppermute(x, 'tensor', perm)  52.5 us
    pallas_call x1, Pallas kernels, middle(): pl.pallas_call(partial(middle_kernel, shape, sizes), out_shape=out, in_sp...  45.4 us
    pallas_call x2, Pallas kernels, heads_back(): pl.pallas_call(partial(heads_back_kernel, shape, slot), grid=(heads_here,...  20.7 us
    ppermute x25, starting transfers between devices, cross(): return lax.ppermute(x, 'dp', [(d, d ^ bit) for d in range(copies)])  20.4 us
    pallas_call x1, Pallas kernels, project(): pl.pallas_call(partial(project_kernel, shape, seq), out_shape=out, in_spe...  15.2 us
    pallas_call x1, Pallas kernels, attend(): pl.pallas_call(partial(attend_kernel, slots, groups), grid=(heads,), out_...  14.5 us
  transfers between devices with their start and end apart: 59, of which 23 were waited for; matrix products, arithmetic and copies ran while one was open for 10% of the time, Pallas kernels for 19%

profile of v2, /device:TPU:0, one launch (start us, length us, event | category | flops | bytes accessed | tf_op | source)
XLA Modules:
  0.0 413.6 jit_solution(13034770230584802374)
XLA Ops:
  8.3 4.0 collective-permute-start
  12.3 1.8 pad_dynamic-slice_fusion.2
  17.4 1.9 collective-permute-start.2
  21.5 2.6 collective-permute-start.1
  28.3 1.7 collective-permute-done.9
  30.1 1.6 collective-permute-start.10
  31.7 23.7 %collective-permute-done.1.rest_1_ = bf16[288,768]{1,0:T(8,128)(2,1)S(1)} collective-permute-done((bf16[288,768]{1,0:T(8,128)(2,1)}, bf16[288,768]{1,0:T(8,128)(2,1)S(1)}, u32[]{:S(2)}, u32[]{:S(2)}) %collective-permute-start.1) | collective-permute-done | bytes 442400 | tf_op jit(solution)/shard_map/ppermute | solution.py:898
  67.8 3.3 collective-permute-start.13
  73.3 1.6 collective-permute-start.11
  76.1 1.6 collective-permute-start.3
  78.3 9.8 %collective-permute-done.11 = bf16[2,112,1152]{2,1,0:T(8,128)(2,1)S(1)} collective-permute-done((bf16[2,112,1152]{2,1,0:T(8,128)(2,1)S(1)}, bf16[2,112,1152]{2,1,0:T(8,128)(2,1)S(1)}, u32[]{:S(2)}, u32[]{:S(2)}) %collective-permute-start.11) | collective-permute-done | bytes 516128 | tf_op jit(solution)/shard_map/ppermute | solution.py:915
  89.5 1.6 collective-permute-start.4
  91.0 4.5 %collective-permute-done.5 = bf16[1,1,160,1152]{3,2,1,0:T(8,128)(2,1)S(1)} collective-permute-done((bf16[1,1,160,1152]{3,2,1,0:T(8,128)(2,1)S(1)}, bf16[1,1,160,1152]{3,2,1,0:T(8,128)(2,1)S(1)}, u32[]{:S(2)}, u32[]{:S(2)}) %collective-permute-start.5) | collective-permute-done | bytes 368672 | tf_op jit(solution)/shard_map/ppermute | solution.py:915
  96.9 1.7 pad.123.own_expand
  99.5 1.7 pad.124.own_reduce
  102.4 7.5 %collective-permute-done.4 = bf16[2,1,160,1152]{3,2,1,0:T(8,128)(2,1)S(1)} collective-permute-done((bf16[2,1,160,1152]{3,2,1,0:T(8,128)(2,1)S(1)}, bf16[2,1,160,1152]{3,2,1,0:T(8,128)(2,1)S(1)}, u32[]{:S(2)}, u32[]{:S(2)}) %collective-permute-start.4) | collective-permute-done | bytes 737312 | tf_op jit(solution)/shard_map/ppermute | solution.py:915
  112.2 8.5 %collective-permute-done.8.rest_2_ = bf16[288,768]{1,0:T(8,128)(2,1)S(1)} collective-permute-done((bf16[288,768]{1,0:T(8,128)(2,1)S(1)}, bf16[288,768]{1,0:T(8,128)(2,1)S(1)}, u32[]{:S(2)}, u32[]{:S(2)}) %collective-permute-start.8) | collective-permute-done | bytes 442400 | tf_op jit(solution)/shard_map/ppermute | solution.py:898
  120.7 15.2 %project.1 = (bf16[3,8,80,768]{3,2,1,0:T(8,128)(2,1)}, bf16[1152,768]{1,0:T(8,128)(2,1)}, f32[8,768]{1,0:T(8,128)S(1)}, bf16[64,768]{1,0:T(8,128)(2,1)S(1)}, bf16[2,1152,384]{2,1,0:T(8,128)(2,1)}) custom-call(s32[6]{0:T(128)S(1)} %stack.141.sc, f32[1152,8]{1,0:T(8,128)S(1)} %pad_convert_fusion.norm_ref, bf16[64,1152]{1,0:T(8,128)(2,1)S(1)} %pad.113.down_ref, ...), custom_call_target="tpu_custom_call" | custom-call | flops 4000000000 | bytes 40000000 | tf_op jit(solution)/shard_map/project/pallas_call | solution.py:189
  138.2 1.5 collective-permute-start.16
  139.7 1.8 copy-done.19
  141.5 14.5 %attend.1 = (f32[8,1,768]{2,1,0:T(1,128)S(1)}, bf16[2,2,288,384]{3,2,1,0:T(8,128)(2,1)S(1)}) custom-call(s32[6]{0:T(128)S(1)} %stack.141.sc, bf16[3,8,80,768]{3,2,1,0:T(8,128)(2,1)S(1)} %copy-done.19), custom_call_target="tpu_custom_call" | custom-call | flops 4000000000 | bytes 60000000 | tf_op jit(solution)/shard_map/attend/pallas_call | solution.py:240
  159.2 1.6 collective-permute-start.17
  161.4 8.8 %collective-permute-done.27 = bf16[1,1,160,1152]{3,2,1,0:T(8,128)(2,1)S(1)} collective-permute-done((bf16[1,1,160,1152]{3,2,1,0:T(8,128)(2,1)S(1)}, bf16[1,1,160,1152]{3,2,1,0:T(8,128)(2,1)S(1)}, u32[]{:S(2)}, u32[]{:S(2)}) %collective-permute-start.27) | collective-permute-done | bytes 368672 | tf_op jit(solution)/shard_map/ppermute | solution.py:915
  170.7 1.9 collective-permute-start.34
  172.6 1.7 collective-permute-start.33
  174.5 8.7 %collective-permute-done.17 = bf16[2,1,160,1152]{3,2,1,0:T(8,128)(2,1)S(1)} collective-permute-done((bf16[2,1,160,1152]{3,2,1,0:T(8,128)(2,1)S(1)}, bf16[2,1,160,1152]{3,2,1,0:T(8,128)(2,1)S(1)}, u32[]{:S(2)}, u32[]{:S(2)}) %collective-permute-start.17) | collective-permute-done | bytes 737312 | tf_op jit(solution)/shard_map/ppermute | solution.py:915
  190.3 7.2 %collective-permute-done.25 = bf16[2,1,160,1152]{3,2,1,0:T(8,128)(2,1)S(1)} collective-permute-done((bf16[2,1,160,1152]{3,2,1,0:T(8,128)(2,1)S(1)}, bf16[2,1,160,1152]{3,2,1,0:T(8,128)(2,1)S(1)}, u32[]{:S(2)}, u32[]{:S(2)}) %collective-permute-start.25) | collective-permute-done | bytes 737312 | tf_op jit(solution)/shard_map/ppermute | solution.py:915
  197.5 3.6 collective-permute-start.32
  205.1 2.6 collective-permute-done.32.rest_16_
  207.7 8.3 %collective-permute-done.31.rest_15_ = bf16[288,384]{1,0:T(8,128)(2,1)S(1)} collective-permute-done((bf16[288,384]{1,0:T(8,128)(2,1)S(1)}, bf16[288,384]{1,0:T(8,128)(2,1)S(1)}, u32[]{:S(2)}, u32[]{:S(2)}) %collective-permute-start.31) | collective-permute-done | bytes 221216 | tf_op jit(solution)/shard_map/ppermute | solution.py:898
  217.2 2.4 collective-permute-done.22.rest_7_
  219.6 2.1 collective-permute-done.19.rest_5_
  221.7 2.1 collective-permute-done.29.rest_11_
  223.8 2.1 collective-permute-done.26.rest_9_
  225.9 45.4 %middle.1 = (bf16[4,288,384]{2,1,0:T(8,128)(2,1)}, f32[1152,384]{1,0:T(8,128)}, bf16[2,2,288,384]{3,2,1,0:T(8,128)(2,1)}, bf16[4,16,3456]{2,1,0:T(8,128)(2,1)}) custom-call(s32[6]{0:T(128)} %copy-done.15, f32[8,1152]{1,0:T(8,128)} %fusion.53.vec_ref, bf16[3,128,1152]{2,1,0:T(8,128)(2,1)} %pad_maximum_fusion.7.tab_ref, ...), custom_call_target="tpu_custom_call" | custom-call | flops 20000000000 | bytes 100000000 | tf_op jit(solution)/shard_map/middle/pallas_call | solution.py:462
  273.7 3.2 collective-permute-start.38
  278.3 2.7 collective-permute-start.42
  281.0 7.4 %collective-permute-done.36.rest_0_ = bf16[2,288,384]{2,1,0:T(8,128)(2,1)S(1)} collective-permute-done((bf16[2,288,384]{2,1,0:T(8,128)(2,1)S(1)}, bf16[2,288,384]{2,1,0:T(8,128)(2,1)S(1)}, u32[]{:S(2)}, u32[]{:S(2)}) %collective-permute-start.36) | collective-permute-done | bytes 442400 | tf_op jit(solution)/shard_map/ppermute | solution.py:898
  288.3 2.8 collective-permute-start.41
  291.2 1.8 copy-done.20
  293.0 10.4 %heads_back.2.rest_0_.rest_2_ = bf16[864,768]{1,0:T(8,128)(2,1)S(1)} custom-call(s32[6]{0:T(128)S(1)} %copy-done.16, bf16[3,8,80,768]{3,2,1,0:T(8,128)(2,1)S(1)} %copy-done.20, f32[8,1,768]{2,1,0:T(1,128)S(1)} %copy-done.22, bf16[2,2,288,384]{3,2,1,0:T(8,128)(2,1)S(1)} %copy-done.10, bf16[2,288,384]{2,1,0:T(8,128)(2,1)S(1)} %collective-permute-done.36.rest_0_), custom_call_target="tpu_custom_call" | custom-call | flops 4000000000 | bytes 40000000 | tf_op jit(solution)/shard_map/heads_back/pallas_call | solution.py:552
  303.4 2.6 collective-permute-start.40
  307.0 10.4 %heads_back.3.rest_1_.rest_3_ = bf16[864,768]{1,0:T(8,128)(2,1)S(1)} custom-call(s32[6]{0:T(128)S(1)} %copy-done.16, bf16[3,8,80,768]{3,2,1,0:T(8,128)(2,1)S(1)} %copy-done.20, f32[8,1,768]{2,1,0:T(1,128)S(1)} %copy-done.22, bf16[2,2,288,384]{3,2,1,0:T(8,128)(2,1)S(1)} %copy-done.10, bf16[2,288,384]{2,1,0:T(8,128)(2,1)S(1)} %collective-permute-done.36.rest_0_), custom_call_target="tpu_custom_call" | custom-call | flops 4000000000 | bytes 40000000 | tf_op jit(solution)/shard_map/heads_back/pallas_call | solution.py:552
  317.4 2.4 rank_back.1
  321.5 12.5 %norm_back.1.own = bf16[4,304,768]{2,1,0:T(8,128)(2,1)} custom-call(s32[6]{0:T(128)S(1)} %copy-done.16, f32[1152,8]{1,0:T(8,128)S(1)} %pad_convert_fusion.norm_ref, bf16[64,1152]{1,0:T(8,128)(2,1)S(1)} %pad.113.down_ref, bf16[64,768]{1,0:T(8,128)(2,1)S(1)} %get-tuple-element.89.thr_ref, f32[8,768]{1,0:T(8,128)S(1)} %copy-done.14, ...), custom_call_target="tpu_custom_call" | custom-call | flops 3000000000 | bytes 20000000 | tf_op jit(solution)/shard_map/norm_back/pallas_call | solution.py:674
  335.9 1.5 collective-permute-start.50
  337.4 1.5 collective-permute-start.49
  339.0 2.8 layer_result.1
  341.8 3.0 collective-permute-start.43
  345.1 3.2 collective-permute-done.43
  348.4 9.8 %all_gather.15.terms_ref = bf16[16,48,640]{2,1,0:T(8,128)(2,1)S(1)} all-gather(bf16[2,48,640]{2,1,0:T(8,128)(2,1)S(1)} %pad_maximum_fusion.21), channel_id=1, replica_groups=mesh['dp'=8,'tensor'=4] {'dp'}, dimensions={0}, use_global_device_ids=true | all-gather | bytes 1105920 | tf_op jit(solution)/shard_map/all_gather | solution.py:1107
  358.2 2.3 by_adapter.2
  360.7 2.2 collective-permute-start.46
  362.9 2.1 collective-permute-start.48
  366.3 1.9 collective-permute-start.56
  369.1 4.7 %by_adapter.3 = (f32[8,16,1076]{2,1,0:T(8,128)}, f32[8,16,1076]{2,1,0:T(8,128)}, f32[8,16,288]{2,1,0:T(8,128)}, bf16[8,16,864]{2,1,0:T(8,128)(2,1)S(1)}) custom-call(bf16[16,16,3456]{2,1,0:T(8,128)(2,1)S(1)} %pad_maximum_fusion.terms_ref), custom_call_target="tpu_custom_call" | custom-call | flops 10000000 | bytes 5000000 | tf_op jit(solution)/shard_map/by_adapter/pallas_call | solution.py:832
  374.2 11.4 %all-gather = bf16[32,48,288]{2,1,0:T(8,128)(2,1)S(1)} all-gather(bf16[4,48,288]{2,1,0:T(8,128)(2,1)S(1)} %pad_maximum_fusion.20), channel_id=2, replica_groups=mesh['dp'=8,'tensor'=4] {'dp'}, dimensions={0}, use_global_device_ids=true | all-gather | bytes 995328 | tf_op jit(solution)/shard_map/all_gather | solution.py:1122
  385.6 2.4 collective-permute-start.53
  388.0 2.0 collective-permute-done.54
  390.0 2.2 collective-permute-start.55
  392.1 3.5 collective-permute-done.55
  395.7 10.8 %all-gather.1 = bf16[32,16,864]{2,1,0:T(8,128)(2,1)S(1)} all-gather(bf16[4,16,864]{2,1,0:T(8,128)(2,1)S(1)} %pad_maximum_fusion.22), channel_id=3, replica_groups=mesh['dp'=8,'tensor'=4] {'dp'}, dimensions={0}, use_global_device_ids=true | all-gather | bytes 995328 | tf_op jit(solution)/shard_map/all_gather | solution.py:1122
  406.5 3.2 whole_tables.1
  409.7 3.7 tokens_result.1
  (260 shorter events, 60.5 us)
Async XLA Ops:
  0.6 23.6 %copy-start = (bf16[3,8,1152,16]{2,3,1,0:T(8,128)(2,1)S(1)}, bf16[3,8,1152,16]{2,3,1,0:T(8,128)(2,1)}, u32[]{:S(2)}) copy-start(bf16[3,8,1152,16]{2,3,1,0:T(8,128)(2,1)} %param.32) | copy-start | bytes 2654212
  8.3 19.1 %collective-permute-start = (bf16[64,864]{1,0:T(8,128)(2,1)}, bf16[64,864]{1,0:T(8,128)(2,1)}, u32[]{:S(2)}, u32[]{:S(2)}) collective-permute-start(bf16[64,864]{1,0:T(8,128)(2,1)} %get-tuple-element.153), channel_id=1, source_target_pairs={{0,2},{1,3},{2,0},{3,1},{4,6},{5,7},{6,4},{7,5},{8,10},{9,11},{10,... | collective-permute-start | bytes 331784 | tf_op jit(solution)/shard_map/ppermute | solution.py:898
  14.1 15.9 %collective-permute-start.9 = (bf16[112,1152]{1,0:T(8,128)(2,1)}, bf16[112,1152]{1,0:T(8,128)(2,1)}, u32[]{:S(2)}, u32[]{:S(2)}) collective-permute-start(bf16[112,1152]{1,0:T(8,128)(2,1)} %pad_dynamic-slice_fusion.2), channel_id=1, source_target_pairs={{0,2},{1,3},{2,0},{3,1},{4,6},{5,7},{6,4},{7,5},{8,10},{9,11},{10,... | collective-permute-start | bytes 774152 | tf_op jit(solution)/shard_map/ppermute | solution.py:898
  17.4 57.5 %collective-permute-start.2 = (bf16[320,1152]{1,0:T(8,128)(2,1)}, bf16[320,1152]{1,0:T(8,128)(2,1)}, u32[]{:S(2)}, u32[]{:S(2)}) collective-permute-start(bf16[320,1152]{1,0:T(8,128)(2,1)} %pad_maximum_fusion.9), channel_id=1, source_target_pairs={{0,1},{1,0},{2,3},{3,2},{4,5},{5,4},{6,7},{7,6},{8,9},{9,8},{10,11... | collective-permute-start | bytes 2211848 | tf_op jit(solution)/shard_map/ppermute | solution.py:898
  21.0 91.1 %collective-permute-start.7 = (bf16[288,768]{1,0:T(8,128)(2,1)}, bf16[288,768]{1,0:T(8,128)(2,1)}, u32[]{:S(2)}, u32[]{:S(2)}) collective-permute-start(bf16[288,768]{1,0:T(8,128)(2,1)} %get-tuple-element.122), channel_id=1, source_target_pairs={{0,1},{1,0},{2,3},{3,2},{4,5},{5,4},{6,7},{7,6},{8,9},{9,8},{10,11... | collective-permute-start | bytes 1327112 | tf_op jit(solution)/shard_map/ppermute | solution.py:898
  21.5 33.9 %collective-permute-start.1 = (bf16[288,768]{1,0:T(8,128)(2,1)}, bf16[288,768]{1,0:T(8,128)(2,1)S(1)}, u32[]{:S(2)}, u32[]{:S(2)}) collective-permute-start(bf16[288,768]{1,0:T(8,128)(2,1)} %get-tuple-element.123), channel_id=1, source_target_pairs={{0,2},{1,3},{2,0},{3,1},{4,6},{5,7},{6,4},{7,5},{8,10},{9,11},{10,... | collective-permute-start | bytes 1327112 | tf_op jit(solution)/shard_map/ppermute | solution.py:898
  24.6 32.1 %copy-start.33 = (s32[2]{0:T(128)S(1)}, s32[2]{0:T(128)}, u32[]{:S(2)}) copy-start(s32[2]{0:T(128)} %param.26) | copy-start | bytes 28
  27.3 112.4 %copy-start.15 = (s32[6]{0:T(128)}, s32[6]{0:T(128)S(1)}, u32[]{:S(2)}) copy-start(s32[6]{0:T(128)S(1)} %stack.141.sc) | copy-start | bytes 76
  28.3 92.4 %copy-start.7 = (bf16[2,64,864]{2,1,0:T(8,128)(2,1)}, bf16[2,64,864]{2,1,0:T(8,128)(2,1)S(1)}, u32[]{:S(2)}) copy-start(bf16[2,64,864]{2,1,0:T(8,128)(2,1)S(1)} %pad_maximum_fusion.18.upx_ref) | copy-start | bytes 663556
  30.1 42.2 %collective-permute-start.10 = (bf16[1,112,1152]{2,1,0:T(8,128)(2,1)}, bf16[1,112,1152]{2,1,0:T(8,128)(2,1)S(1)}, u32[]{:S(2)}, u32[]{:S(2)}) collective-permute-start(bf16[1,112,1152]{2,1,0:T(8,128)(2,1)} %bitcast.52), channel_id=1, source_target_pairs={{0,16},{4,20},{8,24},{12,28},{16,0},{20,4},{24,8},{28,12},{1,17},{... | collective-permute-start | bytes 774152 | tf_op jit(solution)/shard_map/ppermute | solution.py:915
  67.8 68.1 %collective-permute-start.13 = (bf16[320,1152]{1,0:T(8,128)(2,1)}, bf16[320,1152]{1,0:T(8,128)(2,1)S(1)}, u32[]{:S(2)}, u32[]{:S(2)}) collective-permute-start(bf16[320,1152]{1,0:T(8,128)(2,1)} %pad_maximum_fusion.9), channel_id=1, source_target_pairs={{0,2},{1,3},{2,0},{3,1},{4,6},{5,7},{6,4},{7,5},{8,10},{9,11},{10,... | collective-permute-start | bytes 2211848 | tf_op jit(solution)/shard_map/ppermute | solution.py:898
  73.3 14.8 %collective-permute-start.11 = (bf16[2,112,1152]{2,1,0:T(8,128)(2,1)S(1)}, bf16[2,112,1152]{2,1,0:T(8,128)(2,1)S(1)}, u32[]{:S(2)}, u32[]{:S(2)}) collective-permute-start(bf16[2,112,1152]{2,1,0:T(8,128)(2,1)S(1)} %pad_maximum_fusion.16), channel_id=1, source_target_pairs={{0,8},{4,12},{8,0},{12,4},{16,24},{20,28},{24,16},{28,20},{1,9},{5... | collective-permute-start | bytes 1548296 | tf_op jit(solution)/shard_map/ppermute | solution.py:915
  76.1 13.3 %collective-permute-start.3 = (bf16[1,1,160,1152]{3,2,1,0:T(8,128)(2,1)S(1)}, bf16[1,1,160,1152]{3,2,1,0:T(8,128)(2,1)S(1)}, u32[]{:S(2)}, u32[]{:S(2)}) collective-permute-start(bf16[1,1,160,1152]{3,2,1,0:T(8,128)(2,1)S(1)} %get-tuple-element.129), channel_id=1, source_target_pairs={{0,16},{4,20},{8,24},{12,28},{16,0},{20,4},{24,8},{28,12},{1,17},{... | collective-permute-start | bytes 1105928 | tf_op jit(solution)/shard_map/ppermute | solution.py:915
  77.7 17.8 %collective-permute-start.5 = (bf16[1,1,160,1152]{3,2,1,0:T(8,128)(2,1)S(1)}, bf16[1,1,160,1152]{3,2,1,0:T(8,128)(2,1)S(1)}, u32[]{:S(2)}, u32[]{:S(2)}) collective-permute-start(bf16[1,1,160,1152]{3,2,1,0:T(8,128)(2,1)S(1)} %get-tuple-element.128), channel_id=1, source_target_pairs={{0,8},{4,12},{8,0},{12,4},{16,24},{20,28},{24,16},{28,20},{1,9},{5... | collective-permute-start | bytes 1105928 | tf_op jit(solution)/shard_map/ppermute | solution.py:915
  89.3 31.4 %collective-permute-start.12 = (bf16[4,112,1152]{2,1,0:T(8,128)(2,1)S(1)}, bf16[4,112,1152]{2,1,0:T(8,128)(2,1)S(1)}, u32[]{:S(2)}, u32[]{:S(2)}) collective-permute-start(bf16[4,112,1152]{2,1,0:T(8,128)(2,1)S(1)} %pad_maximum_fusion.6.rest_3_.rest_0_), channel_id=1, source_target_pairs={{0,4},{4,0},{8,12},{12,8},{16,20},{20,16},{24,28},{28,24},{1,5},{5... | collective-permute-start | bytes 3096584 | tf_op jit(solution)/shard_map/ppermute | solution.py:915
  89.5 20.4 %collective-permute-start.4 = (bf16[2,1,160,1152]{3,2,1,0:T(8,128)(2,1)S(1)}, bf16[2,1,160,1152]{3,2,1,0:T(8,128)(2,1)S(1)}, u32[]{:S(2)}, u32[]{:S(2)}) collective-permute-start(bf16[2,1,160,1152]{3,2,1,0:T(8,128)(2,1)S(1)} %pad_maximum_fusion.10), channel_id=1, source_target_pairs={{0,8},{4,12},{8,0},{12,4},{16,24},{20,28},{24,16},{28,20},{1,9},{5... | collective-permute-start | bytes 2211848 | tf_op jit(solution)/shard_map/ppermute | solution.py:915
  95.6 15.3 %collective-permute-start.6 = (bf16[2,1,160,1152]{3,2,1,0:T(8,128)(2,1)S(1)}, bf16[2,1,160,1152]{3,2,1,0:T(8,128)(2,1)S(1)}, u32[]{:S(2)}, u32[]{:S(2)}) collective-permute-start(bf16[2,1,160,1152]{3,2,1,0:T(8,128)(2,1)S(1)} %pad_maximum_fusion.11), channel_id=1, source_target_pairs={{0,16},{4,20},{8,24},{12,28},{16,0},{20,4},{24,8},{28,12},{1,17},{... | collective-permute-start | bytes 2211848 | tf_op jit(solution)/shard_map/ppermute | solution.py:915
  109.9 10.8 %collective-permute-start.8 = (bf16[288,768]{1,0:T(8,128)(2,1)S(1)}, bf16[288,768]{1,0:T(8,128)(2,1)S(1)}, u32[]{:S(2)}, u32[]{:S(2)}) collective-permute-start(bf16[288,768]{1,0:T(8,128)(2,1)S(1)} %copy-done.18), channel_id=1, source_target_pairs={{0,1},{1,0},{2,3},{3,2},{4,5},{5,4},{6,7},{7,6},{8,9},{9,8},{10,11... | collective-permute-start | bytes 1327112 | tf_op jit(solution)/shard_map/ppermute | solution.py:898
  110.8 105.8 %collective-permute-start.14 = (bf16[4,1,160,1152]{3,2,1,0:T(8,128)(2,1)S(1)}, bf16[4,1,160,1152]{3,2,1,0:T(8,128)(2,1)}, u32[]{:S(2)}, u32[]{:S(2)}) collective-permute-start(bf16[4,1,160,1152]{3,2,1,0:T(8,128)(2,1)S(1)} %pad_maximum_fusion.1.rest_0_), channel_id=1, source_target_pairs={{0,4},{4,0},{8,12},{12,8},{16,20},{20,16},{24,28},{28,24},{1,5},{5... | collective-permute-start | bytes 4423688 | tf_op jit(solution)/shard_map/ppermute | solution.py:915
  136.0 22.5 %collective-permute-start.23 = (bf16[320,1152]{1,0:T(8,128)(2,1)S(1)}, bf16[320,1152]{1,0:T(8,128)(2,1)S(1)}, u32[]{:S(2)}, u32[]{:S(2)}) collective-permute-start(bf16[320,1152]{1,0:T(8,128)(2,1)S(1)} %collective-permute-done.13), channel_id=1, source_target_pairs={{0,1},{1,0},{2,3},{3,2},{4,5},{5,4},{6,7},{7,6},{8,9},{9,8},{10,11... | collective-permute-start | bytes 2211848 | tf_op jit(solution)/shard_map/ppermute | solution.py:898
  136.7 24.1 %collective-permute-start.20 = (bf16[1,1,160,1152]{3,2,1,0:T(8,128)(2,1)S(1)}, bf16[1,1,160,1152]{3,2,1,0:T(8,128)(2,1)S(1)}, u32[]{:S(2)}, u32[]{:S(2)}) collective-permute-start(bf16[1,1,160,1152]{3,2,1,0:T(8,128)(2,1)S(1)} %get-tuple-element.126), channel_id=1, source_target_pairs={{0,8},{4,12},{8,0},{12,4},{16,24},{20,28},{24,16},{28,20},{1,9},{5... | collective-permute-start | bytes 1105928 | tf_op jit(solution)/shard_map/ppermute | solution.py:915
  138.2 20.9 %collective-permute-start.16 = (bf16[1,1,160,1152]{3,2,1,0:T(8,128)(2,1)S(1)}, bf16[1,1,160,1152]{3,2,1,0:T(8,128)(2,1)S(1)}, u32[]{:S(2)}, u32[]{:S(2)}) collective-permute-start(bf16[1,1,160,1152]{3,2,1,0:T(8,128)(2,1)S(1)} %get-tuple-element.127), channel_id=1, source_target_pairs={{0,16},{4,20},{8,24},{12,28},{16,0},{20,4},{24,8},{28,12},{1,17},{... | collective-permute-start | bytes 1105928 | tf_op jit(solution)/shard_map/ppermute | solution.py:915
  156.2 14.5 %collective-permute-start.18 = (bf16[2,288,384]{2,1,0:T(8,128)(2,1)S(1)}, bf16[2,288,384]{2,1,0:T(8,128)(2,1)S(1)}, u32[]{:S(2)}, u32[]{:S(2)}) collective-permute-start(bf16[2,288,384]{2,1,0:T(8,128)(2,1)S(1)} %dynamic-slice_bitcast_fusion.4), channel_id=1, source_target_pairs={{0,1},{1,0},{2,3},{3,2},{4,5},{5,4},{6,7},{7,6},{8,9},{9,8},{10,11... | collective-permute-start | bytes 1327112 | tf_op jit(solution)/shard_map/ppermute | solution.py:898
  158.5 11.6 %collective-permute-start.27 = (bf16[1,1,160,1152]{3,2,1,0:T(8,128)(2,1)S(1)}, bf16[1,1,160,1152]{3,2,1,0:T(8,128)(2,1)S(1)}, u32[]{:S(2)}, u32[]{:S(2)}) collective-permute-start(bf16[1,1,160,1152]{3,2,1,0:T(8,128)(2,1)S(1)} %get-tuple-element.82), channel_id=1, source_target_pairs={{0,8},{4,12},{8,0},{12,4},{16,24},{20,28},{24,16},{28,20},{1,9},{5... | collective-permute-start | bytes 1105928 | tf_op jit(solution)/shard_map/ppermute | solution.py:915
  159.2 23.9 %collective-permute-start.17 = (bf16[2,1,160,1152]{3,2,1,0:T(8,128)(2,1)S(1)}, bf16[2,1,160,1152]{3,2,1,0:T(8,128)(2,1)S(1)}, u32[]{:S(2)}, u32[]{:S(2)}) collective-permute-start(bf16[2,1,160,1152]{3,2,1,0:T(8,128)(2,1)S(1)} %pad_maximum_fusion.12), channel_id=1, source_target_pairs={{0,8},{4,12},{8,0},{12,4},{16,24},{20,28},{24,16},{28,20},{1,9},{5... | collective-permute-start | bytes 2211848 | tf_op jit(solution)/shard_map/ppermute | solution.py:915
  160.8 11.9 %collective-permute-start.24 = (bf16[1,1,160,1152]{3,2,1,0:T(8,128)(2,1)S(1)}, bf16[1,1,160,1152]{3,2,1,0:T(8,128)(2,1)S(1)}, u32[]{:S(2)}, u32[]{:S(2)}) collective-permute-start(bf16[1,1,160,1152]{3,2,1,0:T(8,128)(2,1)S(1)} %get-tuple-element.80), channel_id=1, source_target_pairs={{0,16},{4,20},{8,24},{12,28},{16,0},{20,4},{24,8},{28,12},{1,17},{... | collective-permute-start | bytes 1105928 | tf_op jit(solution)/shard_map/ppermute | solution.py:915
  170.1 16.3 %collective-permute-start.21 = (bf16[2,1,160,1152]{3,2,1,0:T(8,128)(2,1)S(1)}, bf16[2,1,160,1152]{3,2,1,0:T(8,128)(2,1)S(1)}, u32[]{:S(2)}, u32[]{:S(2)}) collective-permute-start(bf16[2,1,160,1152]{3,2,1,0:T(8,128)(2,1)S(1)} %pad_maximum_fusion.13), channel_id=1, source_target_pairs={{0,16},{4,20},{8,24},{12,28},{16,0},{20,4},{24,8},{28,12},{1,17},{... | collective-permute-start | bytes 2211848 | tf_op jit(solution)/shard_map/ppermute | solution.py:915
  170.7 31.3 %collective-permute-start.34 = (bf16[64,1088]{1,0:T(8,128)(2,1)S(1)}, bf16[64,1088]{1,0:T(8,128)(2,1)S(1)}, u32[]{:S(2)}, u32[]{:S(2)}) collective-permute-start(bf16[64,1088]{1,0:T(8,128)(2,1)S(1)} %get-tuple-element.133), channel_id=1, source_target_pairs={{0,2},{1,3},{2,0},{3,1},{4,6},{5,7},{6,4},{7,5},{8,10},{9,11},{10,... | collective-permute-start | bytes 417800 | tf_op jit(solution)/shard_map/ppermute | solution.py:898
  172.6 29.4 %collective-permute-start.33 = (bf16[64,1088]{1,0:T(8,128)(2,1)S(1)}, bf16[64,1088]{1,0:T(8,128)(2,1)S(1)}, u32[]{:S(2)}, u32[]{:S(2)}) collective-permute-start(bf16[64,1088]{1,0:T(8,128)(2,1)S(1)} %get-tuple-element.134.rest_17_), channel_id=1, source_target_pairs={{0,1},{1,0},{2,3},{3,2},{4,5},{5,4},{6,7},{7,6},{8,9},{9,8},{10,11... | collective-permute-start | bytes 417800 | tf_op jit(solution)/shard_map/ppermute | solution.py:898
  183.1 14.3 %collective-permute-start.25 = (bf16[2,1,160,1152]{3,2,1,0:T(8,128)(2,1)S(1)}, bf16[2,1,160,1152]{3,2,1,0:T(8,128)(2,1)S(1)}, u32[]{:S(2)}, u32[]{:S(2)}) collective-permute-start(bf16[2,1,160,1152]{3,2,1,0:T(8,128)(2,1)S(1)} %pad_maximum_fusion.14), channel_id=1, source_target_pairs={{0,8},{4,12},{8,0},{12,4},{16,24},{20,28},{24,16},{28,20},{1,9},{5... | collective-permute-start | bytes 2211848 | tf_op jit(solution)/shard_map/ppermute | solution.py:915
  186.4 16.4 %collective-permute-start.28 = (bf16[2,1,160,1152]{3,2,1,0:T(8,128)(2,1)S(1)}, bf16[2,1,160,1152]{3,2,1,0:T(8,128)(2,1)S(1)}, u32[]{:S(2)}, u32[]{:S(2)}) collective-permute-start(bf16[2,1,160,1152]{3,2,1,0:T(8,128)(2,1)S(1)} %pad_maximum_fusion.15), channel_id=1, source_target_pairs={{0,16},{4,20},{8,24},{12,28},{16,0},{20,4},{24,8},{28,12},{1,17},{... | collective-permute-start | bytes 2211848 | tf_op jit(solution)/shard_map/ppermute | solution.py:915
  197.5 10.2 %collective-permute-start.32 = (bf16[288,384]{1,0:T(8,128)(2,1)S(1)}, bf16[288,384]{1,0:T(8,128)(2,1)S(1)}, u32[]{:S(2)}, u32[]{:S(2)}) collective-permute-start(bf16[288,384]{1,0:T(8,128)(2,1)S(1)} %get-tuple-element.118), channel_id=1, source_target_pairs={{0,3},{1,2},{2,1},{3,0},{4,7},{5,6},{6,5},{7,4},{8,11},{9,10},{10,... | collective-permute-start | bytes 663560 | tf_op jit(solution)/shard_map/ppermute | solution.py:898
  202.0 23.9 %copy-start.46 = (bf16[64,1088]{1,0:T(8,128)(2,1)}, bf16[64,1088]{1,0:T(8,128)(2,1)S(1)}, u32[]{:S(2)}) copy-start(bf16[64,1088]{1,0:T(8,128)(2,1)S(1)} %collective-permute-done.34.rest_19_) | copy-start | bytes 417796
  202.0 14.0 %collective-permute-start.31 = (bf16[288,384]{1,0:T(8,128)(2,1)S(1)}, bf16[288,384]{1,0:T(8,128)(2,1)S(1)}, u32[]{:S(2)}, u32[]{:S(2)}) collective-permute-start(bf16[288,384]{1,0:T(8,128)(2,1)S(1)} %get-tuple-element.119), channel_id=1, source_target_pairs={{0,2},{1,3},{2,0},{3,1},{4,6},{5,7},{6,4},{7,5},{8,10},{9,11},{10,... | collective-permute-start | bytes 663560 | tf_op jit(solution)/shard_map/ppermute | solution.py:898
  202.0 14.0 %collective-permute-start.30 = (bf16[288,384]{1,0:T(8,128)(2,1)S(1)}, bf16[288,384]{1,0:T(8,128)(2,1)S(1)}, u32[]{:S(2)}, u32[]{:S(2)}) collective-permute-start(bf16[288,384]{1,0:T(8,128)(2,1)S(1)} %get-tuple-element.120), channel_id=1, source_target_pairs={{0,1},{1,0},{2,3},{3,2},{4,5},{5,4},{6,7},{7,6},{8,9},{9,8},{10,11... | collective-permute-start | bytes 663560 | tf_op jit(solution)/shard_map/ppermute | solution.py:898
  202.8 13.7 %collective-permute-start.35 = (bf16[64,1088]{1,0:T(8,128)(2,1)S(1)}, bf16[64,1088]{1,0:T(8,128)(2,1)S(1)}, u32[]{:S(2)}, u32[]{:S(2)}) collective-permute-start(bf16[64,1088]{1,0:T(8,128)(2,1)S(1)} %collective-permute-done.34.rest_19_), channel_id=1, source_target_pairs={{0,1},{1,0},{2,3},{3,2},{4,5},{5,4},{6,7},{7,6},{8,9},{9,8},{10,11... | collective-permute-start | bytes 417800 | tf_op jit(solution)/shard_map/ppermute | solution.py:898
  207.7 9.5 %collective-permute-start.15 = (bf16[4,1,160,1152]{3,2,1,0:T(8,128)(2,1)}, bf16[4,1,160,1152]{3,2,1,0:T(8,128)(2,1)}, u32[]{:S(2)}, u32[]{:S(2)}) collective-permute-start(bf16[4,1,160,1152]{3,2,1,0:T(8,128)(2,1)} %pad_maximum_fusion.2.rest_2_), channel_id=1, source_target_pairs={{0,4},{4,0},{8,12},{12,8},{16,20},{20,16},{24,28},{28,24},{1,5},{5... | collective-permute-start | bytes 4423688 | tf_op jit(solution)/shard_map/ppermute | solution.py:915
  216.0 3.6 collective-permute-start.22
  216.0 5.7 %collective-permute-start.19 = (bf16[4,1,160,1152]{3,2,1,0:T(8,128)(2,1)}, bf16[4,1,160,1152]{3,2,1,0:T(8,128)(2,1)}, u32[]{:S(2)}, u32[]{:S(2)}) collective-permute-start(bf16[4,1,160,1152]{3,2,1,0:T(8,128)(2,1)} %pad_maximum_fusion.3.rest_4_), channel_id=1, source_target_pairs={{0,4},{4,0},{8,12},{12,8},{16,20},{20,16},{24,28},{28,24},{1,5},{5... | collective-permute-start | bytes 4423688 | tf_op jit(solution)/shard_map/ppermute | solution.py:915
  216.5 7.3 %collective-permute-start.29 = (bf16[4,1,160,1152]{3,2,1,0:T(8,128)(2,1)}, bf16[4,1,160,1152]{3,2,1,0:T(8,128)(2,1)}, u32[]{:S(2)}, u32[]{:S(2)}) collective-permute-start(bf16[4,1,160,1152]{3,2,1,0:T(8,128)(2,1)} %constant_dynamic-update-slice_fusion.2.rest_10_), channel_id=1, source_target_pairs={{0,4},{4,0},{8,12},{12,8},{16,20},{20,16},{24,28},{28,24},{1,5},{5... | collective-permute-start | bytes 4423688 | tf_op jit(solution)/shard_map/ppermute | solution.py:915
  216.7 9.2 %collective-permute-start.26 = (bf16[4,1,160,1152]{3,2,1,0:T(8,128)(2,1)}, bf16[4,1,160,1152]{3,2,1,0:T(8,128)(2,1)}, u32[]{:S(2)}, u32[]{:S(2)}) collective-permute-start(bf16[4,1,160,1152]{3,2,1,0:T(8,128)(2,1)} %constant_dynamic-update-slice_fusion.rest_8_), channel_id=1, source_target_pairs={{0,4},{4,0},{8,12},{12,8},{16,20},{20,16},{24,28},{28,24},{1,5},{5... | collective-permute-start | bytes 4423688 | tf_op jit(solution)/shard_map/ppermute | solution.py:915
  272.6 15.7 %collective-permute-start.36 = (bf16[2,288,384]{2,1,0:T(8,128)(2,1)S(1)}, bf16[2,288,384]{2,1,0:T(8,128)(2,1)S(1)}, u32[]{:S(2)}, u32[]{:S(2)}) collective-permute-start(bf16[2,288,384]{2,1,0:T(8,128)(2,1)S(1)} %dynamic-slice_bitcast_fusion.3), channel_id=1, source_target_pairs={{0,1},{1,0},{2,3},{3,2},{4,5},{5,4},{6,7},{7,6},{8,9},{9,8},{10,11... | collective-permute-start | bytes 1327112 | tf_op jit(solution)/shard_map/ppermute | solution.py:898
  273.7 33.1 %collective-permute-start.38 = (bf16[16,3456]{1,0:T(8,128)(2,1)S(1)}, bf16[16,3456]{1,0:T(8,128)(2,1)S(1)}, u32[]{:S(2)}, u32[]{:S(2)}) collective-permute-start(bf16[16,3456]{1,0:T(8,128)(2,1)S(1)} %get-tuple-element.130), channel_id=1, source_target_pairs={{0,2},{1,3},{2,0},{3,1},{4,6},{5,7},{6,4},{7,5},{8,10},{9,11},{10,... | collective-permute-start | bytes 331784 | tf_op jit(solution)/shard_map/ppermute | solution.py:898
  277.0 29.9 %collective-permute-start.39 = (bf16[16,3456]{1,0:T(8,128)(2,1)S(1)}, bf16[16,3456]{1,0:T(8,128)(2,1)S(1)}, u32[]{:S(2)}, u32[]{:S(2)}) collective-permute-start(bf16[16,3456]{1,0:T(8,128)(2,1)S(1)} %get-tuple-element.131), channel_id=1, source_target_pairs={{0,3},{1,2},{2,1},{3,0},{4,7},{5,6},{6,5},{7,4},{8,11},{9,10},{10,... | collective-permute-start | bytes 331784 | tf_op jit(solution)/shard_map/ppermute | solution.py:898
  278.2 25.2 %collective-permute-start.37 = (bf16[16,3456]{1,0:T(8,128)(2,1)S(1)}, bf16[16,3456]{1,0:T(8,128)(2,1)S(1)}, u32[]{:S(2)}, u32[]{:S(2)}) collective-permute-start(bf16[16,3456]{1,0:T(8,128)(2,1)S(1)} %get-tuple-element.132), channel_id=1, source_target_pairs={{0,1},{1,0},{2,3},{3,2},{4,5},{5,4},{6,7},{7,6},{8,9},{9,8},{10,11... | collective-permute-start | bytes 331784 | tf_op jit(solution)/shard_map/ppermute | solution.py:898
  278.3 57.1 %collective-permute-start.42 = (bf16[288,384]{1,0:T(8,128)(2,1)S(1)}, bf16[288,384]{1,0:T(8,128)(2,1)S(1)}, u32[]{:S(2)}, u32[]{:S(2)}) collective-permute-start(bf16[288,384]{1,0:T(8,128)(2,1)S(1)} %get-tuple-element.115), channel_id=1, source_target_pairs={{0,3},{1,2},{2,1},{3,0},{4,7},{5,6},{6,5},{7,4},{8,11},{9,10},{10,... | collective-permute-start | bytes 663560 | tf_op jit(solution)/shard_map/ppermute | solution.py:898
  288.3 47.6 %collective-permute-start.41 = (bf16[288,384]{1,0:T(8,128)(2,1)S(1)}, bf16[288,384]{1,0:T(8,128)(2,1)S(1)}, u32[]{:S(2)}, u32[]{:S(2)}) collective-permute-start(bf16[288,384]{1,0:T(8,128)(2,1)S(1)} %get-tuple-element.116), channel_id=1, source_target_pairs={{0,2},{1,3},{2,0},{3,1},{4,6},{5,7},{6,4},{7,5},{8,10},{9,11},{10,... | collective-permute-start | bytes 663560 | tf_op jit(solution)/shard_map/ppermute | solution.py:898
  303.4 34.0 %collective-permute-start.40 = (bf16[288,384]{1,0:T(8,128)(2,1)S(1)}, bf16[288,384]{1,0:T(8,128)(2,1)S(1)}, u32[]{:S(2)}, u32[]{:S(2)}) collective-permute-start(bf16[288,384]{1,0:T(8,128)(2,1)S(1)} %get-tuple-element.117), channel_id=1, source_target_pairs={{0,1},{1,0},{2,3},{3,2},{4,5},{5,4},{6,7},{7,6},{8,9},{9,8},{10,11... | collective-permute-start | bytes 663560 | tf_op jit(solution)/shard_map/ppermute | solution.py:898
  319.9 21.9 %collective-permute-start.45 = (bf16[48,640]{1,0:T(8,128)(2,1)S(1)}, bf16[48,640]{1,0:T(8,128)(2,1)S(1)}, u32[]{:S(2)}, u32[]{:S(2)}) collective-permute-start(bf16[48,640]{1,0:T(8,128)(2,1)S(1)} %get-tuple-element.146), channel_id=1, source_target_pairs={{0,3},{1,2},{2,1},{3,0},{4,7},{5,6},{6,5},{7,4},{8,11},{9,10},{10,... | collective-permute-start | bytes 184328 | tf_op jit(solution)/shard_map/ppermute | solution.py:898
  320.0 24.8 %collective-permute-start.44 = (bf16[48,640]{1,0:T(8,128)(2,1)S(1)}, bf16[48,640]{1,0:T(8,128)(2,1)S(1)}, u32[]{:S(2)}, u32[]{:S(2)}) collective-permute-start(bf16[48,640]{1,0:T(8,128)(2,1)S(1)} %get-tuple-element.147), channel_id=1, source_target_pairs={{0,2},{1,3},{2,0},{3,1},{4,6},{5,7},{6,4},{7,5},{8,10},{9,11},{10,... | collective-permute-start | bytes 184328 | tf_op jit(solution)/shard_map/ppermute | solution.py:898
  335.4 9.6 %collective-permute-start.51 = (bf16[2,16,3456]{2,1,0:T(8,128)(2,1)S(1)}, bf16[2,16,3456]{2,1,0:T(8,128)(2,1)S(1)}, u32[]{:S(2)}, u32[]{:S(2)}) collective-permute-start(bf16[2,16,3456]{2,1,0:T(8,128)(2,1)S(1)} %pad_maximum_fusion.19), channel_id=1, source_target_pairs={{0,24},{4,28},{8,16},{12,20},{16,8},{20,12},{24,0},{28,4},{1,25},{... | collective-permute-start | bytes 663560 | tf_op jit(solution)/shard_map/ppermute | solution.py:915
  335.9 9.0 %collective-permute-start.50 = (bf16[2,16,3456]{2,1,0:T(8,128)(2,1)S(1)}, bf16[2,16,3456]{2,1,0:T(8,128)(2,1)S(1)}, u32[]{:S(2)}, u32[]{:S(2)}) collective-permute-start(bf16[2,16,3456]{2,1,0:T(8,128)(2,1)S(1)} %pad_maximum_fusion.19), channel_id=1, source_target_pairs={{0,16},{4,20},{8,24},{12,28},{16,0},{20,4},{24,8},{28,12},{1,17},{... | collective-permute-start | bytes 663560 | tf_op jit(solution)/shard_map/ppermute | solution.py:915
  337.4 7.5 %collective-permute-start.49 = (bf16[2,16,3456]{2,1,0:T(8,128)(2,1)S(1)}, bf16[2,16,3456]{2,1,0:T(8,128)(2,1)S(1)}, u32[]{:S(2)}, u32[]{:S(2)}) collective-permute-start(bf16[2,16,3456]{2,1,0:T(8,128)(2,1)S(1)} %pad_maximum_fusion.19), channel_id=1, source_target_pairs={{0,8},{4,12},{8,0},{12,4},{16,24},{20,28},{24,16},{28,20},{1,9},{5... | collective-permute-start | bytes 663560 | tf_op jit(solution)/shard_map/ppermute | solution.py:915
  341.8 6.5 %collective-permute-start.43 = (bf16[48,640]{1,0:T(8,128)(2,1)S(1)}, bf16[48,640]{1,0:T(8,128)(2,1)S(1)}, u32[]{:S(2)}, u32[]{:S(2)}) collective-permute-start(bf16[48,640]{1,0:T(8,128)(2,1)S(1)} %get-tuple-element.145), channel_id=1, source_target_pairs={{0,1},{1,0},{2,3},{3,2},{4,5},{5,4},{6,7},{7,6},{8,9},{9,8},{10,11... | collective-permute-start | bytes 184328 | tf_op jit(solution)/shard_map/ppermute | solution.py:898
  344.8 64.8 %collective-permute-start.58 = (bf16[304,768]{1,0:T(8,128)(2,1)S(1)}, bf16[304,768]{1,0:T(8,128)(2,1)S(1)}, u32[]{:S(2)}, u32[]{:S(2)}) collective-permute-start(bf16[304,768]{1,0:T(8,128)(2,1)S(1)} %get-tuple-element.112), channel_id=1, source_target_pairs={{0,3},{1,2},{2,1},{3,0},{4,7},{5,6},{6,5},{7,4},{8,11},{9,10},{10,... | collective-permute-start | bytes 1400840 | tf_op jit(solution)/shard_map/ppermute | solution.py:898
  345.0 24.0 %collective-permute-start.52 = (bf16[8,16,3456]{2,1,0:T(8,128)(2,1)S(1)}, bf16[8,16,3456]{2,1,0:T(8,128)(2,1)S(1)}, u32[]{:S(2)}, u32[]{:S(2)}) collective-permute-start(bf16[8,16,3456]{2,1,0:T(8,128)(2,1)S(1)} %constant_dynamic-update-slice_fusion.4), channel_id=1, source_target_pairs={{0,4},{4,0},{8,12},{12,8},{16,20},{20,16},{24,28},{28,24},{1,5},{5... | collective-permute-start | bytes 2654216 | tf_op jit(solution)/shard_map/ppermute | solution.py:915
  360.6 5.7 %collective-permute-start.47 = (bf16[48,288]{1,0:T(8,128)(2,1)S(1)}, bf16[48,288]{1,0:T(8,128)(2,1)S(1)}, u32[]{:S(2)}, u32[]{:S(2)}) collective-permute-start(bf16[48,288]{1,0:T(8,128)(2,1)S(1)} %constant_dynamic-slice_fusion.1), channel_id=1, source_target_pairs={{0,2},{1,3},{2,0},{3,1},{4,6},{5,7},{6,4},{7,5},{8,10},{9,11},{10,... | collective-permute-start | bytes 82952 | tf_op jit(solution)/shard_map/ppermute | solution.py:898
  360.7 5.6 %collective-permute-start.46 = (bf16[48,288]{1,0:T(8,128)(2,1)S(1)}, bf16[48,288]{1,0:T(8,128)(2,1)S(1)}, u32[]{:S(2)}, u32[]{:S(2)}) collective-permute-start(bf16[48,288]{1,0:T(8,128)(2,1)S(1)} %constant_dynamic-slice_fusion.1), channel_id=1, source_target_pairs={{0,1},{1,0},{2,3},{3,2},{4,5},{5,4},{6,7},{7,6},{8,9},{9,8},{10,11... | collective-permute-start | bytes 82952 | tf_op jit(solution)/shard_map/ppermute | solution.py:898
  362.9 6.0 %collective-permute-start.48 = (bf16[48,288]{1,0:T(8,128)(2,1)S(1)}, bf16[48,288]{1,0:T(8,128)(2,1)S(1)}, u32[]{:S(2)}, u32[]{:S(2)}) collective-permute-start(bf16[48,288]{1,0:T(8,128)(2,1)S(1)} %constant_dynamic-slice_fusion.1), channel_id=1, source_target_pairs={{0,3},{1,2},{2,1},{3,0},{4,7},{5,6},{6,5},{7,4},{8,11},{9,10},{10,... | collective-permute-start | bytes 82952 | tf_op jit(solution)/shard_map/ppermute | solution.py:898
  366.3 43.4 %collective-permute-start.57 = (bf16[304,768]{1,0:T(8,128)(2,1)S(1)}, bf16[304,768]{1,0:T(8,128)(2,1)S(1)}, u32[]{:S(2)}, u32[]{:S(2)}) collective-permute-start(bf16[304,768]{1,0:T(8,128)(2,1)S(1)} %get-tuple-element.113), channel_id=1, source_target_pairs={{0,2},{1,3},{2,0},{3,1},{4,6},{5,7},{6,4},{7,5},{8,10},{9,11},{10,... | collective-permute-start | bytes 1400840 | tf_op jit(solution)/shard_map/ppermute | solution.py:898
  366.3 43.4 %collective-permute-start.56 = (bf16[304,768]{1,0:T(8,128)(2,1)S(1)}, bf16[304,768]{1,0:T(8,128)(2,1)S(1)}, u32[]{:S(2)}, u32[]{:S(2)}) collective-permute-start(bf16[304,768]{1,0:T(8,128)(2,1)S(1)} %get-tuple-element.114), channel_id=1, source_target_pairs={{0,1},{1,0},{2,3},{3,2},{4,5},{5,4},{6,7},{7,6},{8,9},{9,8},{10,11... | collective-permute-start | bytes 1400840 | tf_op jit(solution)/shard_map/ppermute | solution.py:898
  373.9 16.1 %collective-permute-start.54 = (bf16[16,864]{1,0:T(8,128)(2,1)S(1)}, bf16[16,864]{1,0:T(8,128)(2,1)S(1)}, u32[]{:S(2)}, u32[]{:S(2)}) collective-permute-start(bf16[16,864]{1,0:T(8,128)(2,1)S(1)} %constant_dynamic-slice_fusion), channel_id=1, source_target_pairs={{0,2},{1,3},{2,0},{3,1},{4,6},{5,7},{6,4},{7,5},{8,10},{9,11},{10,... | collective-permute-start | bytes 82952 | tf_op jit(solution)/shard_map/ppermute | solution.py:898
  385.6 6.6 %collective-permute-start.53 = (bf16[16,864]{1,0:T(8,128)(2,1)S(1)}, bf16[16,864]{1,0:T(8,128)(2,1)S(1)}, u32[]{:S(2)}, u32[]{:S(2)}) collective-permute-start(bf16[16,864]{1,0:T(8,128)(2,1)S(1)} %constant_dynamic-slice_fusion), channel_id=1, source_target_pairs={{0,1},{1,0},{2,3},{3,2},{4,5},{5,4},{6,7},{7,6},{8,9},{9,8},{10,11... | collective-permute-start | bytes 82952 | tf_op jit(solution)/shard_map/ppermute | solution.py:898
  390.0 5.7 %collective-permute-start.55 = (bf16[16,864]{1,0:T(8,128)(2,1)S(1)}, bf16[16,864]{1,0:T(8,128)(2,1)S(1)}, u32[]{:S(2)}, u32[]{:S(2)}) collective-permute-start(bf16[16,864]{1,0:T(8,128)(2,1)S(1)} %constant_dynamic-slice_fusion), channel_id=1, source_target_pairs={{0,3},{1,2},{2,1},{3,0},{4,7},{5,6},{6,5},{7,4},{8,11},{9,10},{10,... | collective-permute-start | bytes 82952 | tf_op jit(solution)/shard_map/ppermute | solution.py:898
  (45 other events, 337.1 us)

commit v3 on v2

v3 whole, which is shorter than its diff:
```python
import math
from functools import partial

import jax
import jax.numpy as jnp
from jax import lax
from jax.experimental import pallas as pl
from jax.experimental.pallas import tpu as pltpu
from jax.sharding import PartitionSpec as P

HEAD_DIM = 72
HEAD_PAD = 80
LANES = 128
CHUNK = 256
UNITS = 512
EPS = 1e-06
BF = jnp.bfloat16
F32 = jnp.float32
SCALE = 1.0 / math.sqrt(HEAD_DIM)
LOG2E = 1.4426950408889634
MIB = 1024 * 1024

NN = (((1,), (0,)), ((), ()))
NT = (((1,), (1,)), ((), ()))
TN = (((0,), (0,)), ((), ()))


def mm(a, b, dims=NN):
    return lax.dot_general(a, b, dims, preferred_element_type=F32)


def up_to(value, step):
    return -(-value // step) * step


def vmem():
    return pl.BlockSpec(memory_space=pltpu.VMEM)


def anywhere():
    return pl.BlockSpec(memory_space=pl.ANY)


def smem():
    return pl.BlockSpec(memory_space=pltpu.SMEM)


class Shape:
    def __init__(self, parts, slots, copies):
        self.parts, self.slots, self.copies = parts, slots, copies
        self.groups = parts // slots
        self.pairs = [(k, g) for k in range(slots) for g in range(self.groups)]
        self.far = [(0, g) for g in range(1, self.groups)]
        self.far += [(k, 0) for k in range(1, slots)]
        self.far += [(k, g) for k in range(1, slots) for g in range(1, self.groups)]
        self.order = [(0, 0)] + self.far
        self.bits = []
        bit = copies // 2
        while bit:
            self.bits.append(bit)
            bit //= 2

    def source(self, mine, member, k, g):
        return lax.rem(mine - k + self.slots, self.slots) * self.groups + lax.rem(
            member - g + self.groups, self.groups
        )

    def mask(self, spot):
        return sum(bit for n, bit in enumerate(self.bits) if (spot >> n) & 1)


def run_all(copies):
    for copy in copies:
        copy.start()
    for copy in copies:
        copy.wait()


def weight_copies(shape, row, own, foreign, dest, sems):
    rows = own.shape[0]
    copies = [pltpu.make_async_copy(own, dest.at[0, pl.ds(0, rows), :], sems.at[0])]
    for k in range(1, shape.slots):
        near, far = foreign[2 * (k - 1) : 2 * k]
        half, size, _ = near.shape
        for spot in range(shape.copies):
            piece = near.at[spot] if spot < half else far.at[spot - half]
            at = pl.multiple_of(jnp.bitwise_xor(row, shape.mask(spot)) * size, 16)
            copies.append(
                pltpu.make_async_copy(
                    piece,
                    dest.at[k, pl.ds(at, size), :],
                    sems.at[1 + (k - 1) * shape.copies + spot],
                )
            )
    return copies


def project_kernel(shape, seq, sc, norm_ref, down_ref, ups_ref, own_tok, own_w, *rest):
    slots, groups, parts = shape.slots, shape.groups, shape.parts
    toks = rest[: parts - 1]
    foreign = rest[parts - 1 : parts - 1 + 2 * (slots - 1)]
    rest = rest[parts - 1 + 2 * (slots - 1) :]
    qkv_ref, n1_ref, stats_ref, inner_ref, rows_ref, upx_ref = rest[:6]
    tok_ref, weights, tok_sem, weight_sem = rest[6:]
    _, width, span = tok_ref.shape
    dim = parts * width
    head_rows = upx_ref.shape[2] // 3
    heads_here = head_rows // HEAD_DIM
    block = span // groups
    mine, member, row = sc[0], sc[1], sc[3]

    tok_copies = []
    for n, (k, g) in enumerate(shape.pairs):
        source = own_tok.at[mine] if n == 0 else toks[n - 1]
        tok_copies.append(
            pltpu.make_async_copy(
                source, tok_ref.at[shape.source(mine, member, k, g)], tok_sem.at[n]
            )
        )
    weight_list = weight_copies(shape, row, own_w, foreign, weights, weight_sem)
    for copy in tok_copies + weight_list:
        copy.start()
    for copy in tok_copies:
        copy.wait()

    def norm_step(c, carry):
        cols = pl.ds(pl.multiple_of(c * LANES, LANES), LANES)
        x = tok_ref[:, :, cols].reshape(dim, LANES).astype(F32)
        mean = jnp.mean(x, 0, keepdims=True)
        center = x - mean
        rstd = lax.rsqrt(jnp.mean(center * center, 0, keepdims=True) + EPS)
        n1 = center * rstd * norm_ref[:, 0:1] + norm_ref[:, 1:2]
        n1_ref[:, cols] = n1.astype(BF)
        stats_ref[0:1, cols] = mean
        stats_ref[1:2, cols] = rstd
        return carry

    lax.fori_loop(0, span // LANES, norm_step, 0)
    stats_ref[2:8, :] = jnp.zeros((6, span), F32)
    part_of = lax.broadcasted_iota(jnp.int32, (16, 3 * head_rows), 1) // head_rows
    for k in range(slots):
        up = ups_ref[k, 0:16, 0 : 3 * head_rows]
        lines = [jnp.where(part_of == j, up, jnp.zeros_like(up)) for j in range(3)]
        upx_ref[k] = jnp.concatenate(lines + [ups_ref[k, 16:32, 0 : 3 * head_rows]], 0)
    for copy in weight_list:
        copy.wait()

    def proj_step(c, carry):
        start = pl.multiple_of(c * CHUNK, CHUNK)
        cols = pl.ds(start, CHUNK)
        n1 = n1_ref[:, cols]
        rank = down_ref.shape[0]
        inner = mm(down_ref[...], n1)
        line = lax.broadcasted_iota(jnp.int32, (rank, CHUNK), 0)
        inner_x = jnp.where(line == 48, 1.0, 0.5 * inner).astype(BF)
        inner_ref[:, cols] = inner_x
        spot = lax.broadcasted_iota(jnp.int32, (HEAD_PAD - HEAD_DIM, CHUNK), 0)
        place = start + lax.broadcasted_iota(jnp.int32, (HEAD_PAD - HEAD_DIM, CHUNK), 1)
        tails = (
            jnp.where(spot == 0, 1.0, 0.0),
            jnp.where((spot == 0) & (place >= seq), -1e30, 0.0),
            jnp.zeros((HEAD_PAD - HEAD_DIM, CHUNK), F32),
        )
        for k in range(slots):
            proj = mm(weights[k, 0 : 3 * head_rows, :], n1) + mm(upx_ref[k], inner_x, TN)
            for j in range(3):
                for h in range(heads_here):
                    at = j * head_rows + h * HEAD_DIM
                    piece = jnp.concatenate([proj[at : at + HEAD_DIM, :], tails[j]], 0)
                    qkv_ref[j, k * heads_here + h, :, cols] = piece.astype(BF)
        return carry

    lax.fori_loop(0, span // CHUNK, proj_step, 0)

    for g in range(groups):
        rows_ref[g] = tok_ref[:, :, g * block : (g + 1) * block].reshape(dim, block)


def project(shape, seq, scalars, norm, down, ups, own_tok, toks, own_w, foreign):
    slots, groups, parts = shape.slots, shape.groups, shape.parts
    _, width, span = own_tok.shape
    head_rows = own_w.shape[0] // 3
    heads = slots * head_rows // HEAD_DIM
    dim = parts * width
    weight_rows = max([own_w.shape[0]] + [w.shape[1] * shape.copies for w in foreign])
    out = (
        jax.ShapeDtypeStruct((3, heads, HEAD_PAD, span), BF),
        jax.ShapeDtypeStruct((dim, span), BF),
        jax.ShapeDtypeStruct((8, span), F32),
        jax.ShapeDtypeStruct((down.shape[0], span), BF),
        jax.ShapeDtypeStruct((groups, dim, span // groups), BF),
        jax.ShapeDtypeStruct((slots, 64, 3 * head_rows), BF),
    )
    return pl.pallas_call(
        partial(project_kernel, shape, seq),
        out_shape=out,
        in_specs=[smem()] + [vmem()] * 3 + [anywhere()] * (2 + len(toks) + len(foreign)),
        out_specs=tuple(vmem() for _ in out),
        scratch_shapes=[
            pltpu.VMEM((parts, width, span), BF),
            pltpu.VMEM((slots, weight_rows, dim), BF),
            pltpu.SemaphoreType.DMA((parts,)),
            pltpu.SemaphoreType.DMA((1 + (slots - 1) * shape.copies,)),
        ],
        compiler_params=pltpu.CompilerParams(vmem_limit_bytes=48 * MIB),
        cost_estimate=pl.CostEstimate(flops=4 * 10**9, bytes_accessed=40 * 10**6, transcendentals=10**6),
        name="project",
    )(scalars, norm, down, ups, own_tok, own_w, *toks, *foreign)


def attend_kernel(slots, sc, qkv_ref, lse_ref, heads_ref, scr):
    span = scr.shape[1]
    head_rows = scr.shape[0] // slots
    h = pl.program_id(0)
    keys = qkv_ref[1, 0].T
    vals = qkv_ref[2, 0]
    at = pl.multiple_of(h * HEAD_DIM, 8)
    for c in range(span // CHUNK):
        cols = slice(c * CHUNK, (c + 1) * CHUNK)
        scores = mm(keys, qkv_ref[0, 0, :, cols]) * (SCALE * LOG2E)
        top = jnp.max(scores, 0, keepdims=True)
        raised = jnp.exp2(scores - top)
        total = jnp.sum(raised, 0, keepdims=True)
        out = mm(vals, raised.astype(BF)) / total
        scr[pl.ds(at, HEAD_DIM), cols] = out[0:HEAD_DIM, :]
        lse_ref[0, 0:1, cols] = top + jnp.log2(total)

    @pl.when(h == pl.num_programs(0) - 1)
    def _():
        for k in range(slots):
            heads_ref[k] = scr[k * head_rows : (k + 1) * head_rows, :].astype(BF)


def attend(shape, scalars, qkv):
    slots = shape.slots
    _, heads, _, span = qkv.shape
    head_rows = heads * HEAD_DIM // slots
    out = (
        jax.ShapeDtypeStruct((heads, 1, span), F32),
        jax.ShapeDtypeStruct((slots, head_rows, span), BF),
    )
    return pl.pallas_call(
        partial(attend_kernel, slots),
        grid=(heads,),
        out_shape=out,
        in_specs=[smem(), pl.BlockSpec((3, 1, HEAD_PAD, span), lambda h: (0, h, 0, 0))],
        out_specs=(
            pl.BlockSpec((1, 1, span), lambda h: (h, 0, 0)),
            pl.BlockSpec(out[1].shape, lambda h: (0, 0, 0)),
        ),
        scratch_shapes=[pltpu.VMEM((slots * head_rows, span), F32)],
        compiler_params=pltpu.CompilerParams(vmem_limit_bytes=40 * MIB),
        cost_estimate=pl.CostEstimate(flops=4 * 10**9, bytes_accessed=60 * 10**6, transcendentals=5 * 10**6),
        name="attend",
    )(scalars, qkv)


def load_factors(fac, both, base, hidden_rows, tail):
    blank = jnp.zeros((LANES - 32, hidden_rows), BF)
    both[0, base : base + hidden_rows, tail] = jnp.concatenate([fac[0:32, :], blank], 0).T
    spread = jnp.concatenate([fac[32:48, :], jnp.zeros((16, hidden_rows), BF), blank], 0)
    both[1, base : base + hidden_rows, tail] = spread.T


def hidden_units(both, n2x, gx, acc_out, acc_back, eug, rdg, tail):
    rows = both.shape[1]
    inner_t = n2x[:, tail].T
    thr_t = gx[:, tail].T

    def units(at):
        we_c = both[0, at, :]
        wr_c = both[1, at, :]
        pre = mm(n2x[...], we_c, NT)
        grad_act = mm(gx[...], wr_c, NT)
        square = pre * pre
        th = jnp.tanh(pre * (0.7978845608028654 + 0.035677408136300125 * square))
        half = 0.5 * (1.0 + th)
        act = (pre * half).astype(BF)
        slope = half + pre * (0.5 * (1.0 - th * th)) * (
            0.7978845608028654 + 0.10703222440890037 * square
        )
        grad_pre = (grad_act * slope).astype(BF)
        acc_out[...] += mm(act, wr_c)
        acc_back[...] += mm(grad_pre, we_c)
        eug[:, at] = mm(inner_t[0:16, :], grad_pre)
        rdg[:, at] = mm(thr_t[0:16, :], act)

    def step(c, carry):
        units(pl.ds(pl.multiple_of(c * UNITS, UNITS), UNITS))
        return carry

    lax.fori_loop(0, rows // UNITS, step, 0)
    if rows % UNITS:
        units(slice(rows // UNITS * UNITS, rows))


def normalise(hidden):
    mean = jnp.mean(hidden, 1, keepdims=True)
    center = hidden - mean
    rstd = lax.rsqrt(jnp.mean(center * center, 1, keepdims=True) + EPS)
    return center * rstd, rstd


def merge_copies(parts, merge_hbm, wm, dim, sems):
    rows = dim // parts
    return [
        pltpu.make_async_copy(
            merge_hbm.at[t, pl.ds(0, rows), :], wm.at[pl.ds(t * rows, rows), pl.ds(0, dim)], sems.at[t]
        )
        for t in range(parts)
    ]


def pick_block(parts, which):
    out = parts[0]
    for n in range(1, len(parts)):
        out = jnp.where(which == n, parts[n], out)
    return out


def hidden_kernel(
    shape, turn, sc, vec_ref, tab_ref, fac_ref, rows_ref, own_expand, own_reduce, merge_hbm, own_cot, own_heads, *rest
):
    slots, groups, parts = shape.slots, shape.groups, shape.parts
    cots, rest = rest[: parts - 1], rest[parts - 1 :]
    heads_hbm, rest = (own_heads,) + rest[: groups - 1], rest[groups - 1 :]
    pieces, rest = rest[: slots - 1], rest[slots - 1 :]
    layer_ref, back_ref, gm_ref, gw_ref = rest[:4]
    kept, rest = (rest[4:9], rest[9:]) if turn == 0 else (None, rest[4:])
    both, wm, heads_in, cot_in, n2x, gx, acc_out, acc_back, eug, rdg = rest[:10]
    heads_sem, cot_sem, own_sem, merge_sem, w_sem = rest[10:]
    _, head_rows, span = heads_in.shape
    block = span // groups
    dim = parts * head_rows
    hidden_rows = both.shape[1] // slots
    size = 2 * hidden_rows // shape.copies
    half = shape.copies // 2
    tail = slice(dim, dim + LANES)
    cols = pl.ds(0, dim)
    mine, member, valid, ident = sc[0], sc[1], sc[2], sc[4]

    small = []
    for n, (k, g) in enumerate(shape.pairs):
        source = own_cot.at[mine] if n == 0 else cots[n - 1]
        spot = shape.source(mine, member, k, g)
        small.append(pltpu.make_async_copy(source, cot_in.at[spot], cot_sem.at[n]))
    for g in range(groups):
        for k in range(slots):
            spot = lax.rem(member - g + groups, groups) + groups * lax.rem(mine + k, slots)
            small.append(
                pltpu.make_async_copy(heads_hbm[g].at[k], heads_in.at[spot], heads_sem.at[g, k])
            )
    merges = merge_copies(parts, merge_hbm, wm, dim, merge_sem)
    mlps = [
        pltpu.make_async_copy(source, both.at[n, pl.ds(0, hidden_rows), cols], own_sem.at[n])
        for n, source in enumerate((own_expand, own_reduce))
    ]
    for k in range(1, slots):
        for d in range(shape.copies):
            start = k * hidden_rows + d % half * size
            mlps.append(
                pltpu.make_async_copy(
                    pieces[k - 1].at[d],
                    both.at[d // half, pl.ds(start, size), cols],
                    w_sem.at[k, d],
                )
            )
    for copy in small + merges + mlps:
        copy.start()
    for k in range(slots):
        load_factors(fac_ref[k], both, k * hidden_rows, hidden_rows, tail)
    acc_out[...] = jnp.zeros_like(acc_out)
    acc_back[...] = jnp.zeros_like(acc_back)
    for copy in small:
        copy.wait()
    for t in range(parts):
        lines = cot_in[t, head_rows : head_rows + 16, 0:head_rows]
        lines = jnp.concatenate([lines, jnp.zeros((LANES - 16, head_rows), BF)], 0).T
        wm[t * head_rows : (t + 1) * head_rows, tail] = lines
    which = lax.rem(member + turn, groups)
    blocks = [slice(g * block, (g + 1) * block) for g in range(groups)]
    cot = pick_block([cot_in[:, 0:head_rows, at] for at in blocks], which)
    grads = cot.reshape(dim, block).T * valid.astype(F32).astype(BF)
    gx[:, 0:dim] = grads
    gx[:, tail] = (0.5 * mm(grads, tab_ref[2], NT)).astype(BF)
    heads = pick_block([heads_in[:, :, at] for at in blocks], which).reshape(dim, block).T
    for copy in merges:
        copy.wait()
    lane = lax.broadcasted_iota(jnp.int32, (block, LANES), 1)
    merged = mm(heads, wm[...])
    inner_m = (0.5 * merged[:, tail]).astype(BF)
    hidden = rows_ref[which].T.astype(F32) + merged[:, :dim] + mm(inner_m, tab_ref[0]) + vec_ref[0:1, :]
    unit, _ = normalise(hidden)
    n2 = (unit * vec_ref[2:3, :] + vec_ref[3:4, :]).astype(BF)
    n2x[:, 0:dim] = n2
    n2x[:, tail] = jnp.where(lane == 16, 1.0, 0.5 * mm(n2, tab_ref[1], NT)).astype(BF)
    if kept:
        for ref, value in zip(kept, (hidden, heads, inner_m, grads, wm[:, tail]), strict=True):
            ref[...] = value
    for copy in mlps:
        copy.wait()
    hidden_units(both, n2x, gx, acc_out, acc_back, eug, rdg, tail)

    inner_r = (0.5 * acc_out[:, tail]).astype(BF)
    thr_e = (0.5 * acc_back[:, tail]).astype(BF)
    layer = acc_out[:, 0:dim] + mm(inner_r, tab_ref[2])
    if kept:
        layer = layer + kept[0][...] + vec_ref[1:2, :]
    layer = layer.T.astype(BF)
    for t in range(parts):
        layer_ref[t] = layer[t * head_rows : (t + 1) * head_rows, :]
    back_ref[...] = (acc_back[:, 0:dim] + mm(thr_e, tab_ref[1])).astype(back_ref.dtype)
    whole = (
        mm(thr_e, n2x[:, 0:dim], TN)[0:16, :],
        mm(inner_r, gx[:, 0:dim], TN)[0:16, :],
    )
    ids = jnp.full((32, LANES), ident, jnp.int32).astype(F32)
    if turn:
        ids = jnp.zeros_like(ids)
    gw_ref[...] = jnp.concatenate([jnp.concatenate(whole, 0), ids], 1).astype(BF)
    blank = jnp.zeros((16, 2 * (dim + LANES) - 2 * hidden_rows), F32)
    for k in range(slots):
        at = slice(k * hidden_rows, (k + 1) * hidden_rows)
        line = jnp.concatenate([eug[:, at], rdg[:, at], blank], 1)
        gm_ref[k, 0:16, :] = line[:, 0 : dim + LANES].astype(BF)
        gm_ref[k, 16:32, :] = line[:, dim + LANES :].astype(BF)


def hidden_part(shape, turn, scalars, vec, tab, fac, rows, own_w, merge, own_cot, cots, heads, pieces):
    slots, groups, parts = shape.slots, shape.groups, shape.parts
    own_heads, others = heads
    _, head_rows, span = own_heads.shape
    block = span // groups
    dim = parts * head_rows
    hidden_rows = fac.shape[2]
    count = slots * hidden_rows
    out = (
        jax.ShapeDtypeStruct((parts, head_rows, block), BF),
        jax.ShapeDtypeStruct((block, dim), BF if turn else F32),
        jax.ShapeDtypeStruct((slots, 32, dim + LANES), BF),
        jax.ShapeDtypeStruct((32, dim + LANES), BF),
    )
    if turn == 0:
        out += (
            jax.ShapeDtypeStruct((block, dim), F32),
            jax.ShapeDtypeStruct((block, dim), BF),
            jax.ShapeDtypeStruct((block, LANES), BF),
            jax.ShapeDtypeStruct((block, dim), BF),
            jax.ShapeDtypeStruct((dim, LANES), BF),
        )
    inputs = 5 + len(cots) + len(others) + len(pieces)
    return pl.pallas_call(
        partial(hidden_kernel, shape, turn),
        out_shape=out,
        in_specs=[smem()] + [vmem()] * 4 + [anywhere()] * inputs,
        out_specs=tuple(vmem() for _ in out),
        scratch_shapes=[
            pltpu.VMEM((2, count, dim + LANES), BF),
            pltpu.VMEM((dim, dim + LANES), BF),
            pltpu.VMEM((parts, head_rows, span), BF),
            pltpu.VMEM((parts,) + own_cot.shape[1:], BF),
            pltpu.VMEM((block, dim + LANES), BF),
            pltpu.VMEM((block, dim + LANES), BF),
            pltpu.VMEM((block, dim + LANES), F32),
            pltpu.VMEM((block, dim + LANES), F32),
            pltpu.VMEM((16, count), F32),
            pltpu.VMEM((16, count), F32),
            pltpu.SemaphoreType.DMA((groups, slots)),
            pltpu.SemaphoreType.DMA((parts,)),
            pltpu.SemaphoreType.DMA((2,)),
            pltpu.SemaphoreType.DMA((parts,)),
            pltpu.SemaphoreType.DMA((slots, shape.copies)),
        ],
        compiler_params=pltpu.CompilerParams(vmem_limit_bytes=62 * MIB),
        cost_estimate=pl.CostEstimate(flops=10 * 10**9, bytes_accessed=60 * 10**6, transcendentals=10**6),
        name="hidden_part",
    )(scalars, vec, tab, fac, rows, *own_w, merge, own_cot, own_heads, *cots, *others, *pieces)


def branch_kernel(shape, sc, vec_ref, tab_ref, merge_hbm, *rest):
    slots, groups, parts = shape.slots, shape.groups, shape.parts
    inputs, rest = rest[: groups + 5], rest[groups + 5 :]
    resid_ref, back_ref, gw_ref, wm, sem, in_sem = rest[:6]
    held = rest[6:]
    own_back, hidden_ref, heads_ref, inner_ref, grads_ref, tails_ref = held[:6]
    others = held[6:]
    _, dim = hidden_ref.shape
    head_rows = dim // parts
    mine, ident = sc[0], sc[4]
    merges = merge_copies(parts, merge_hbm, wm, dim, sem)
    loads = [
        pltpu.make_async_copy(source, dest, in_sem.at[n])
        for n, (source, dest) in enumerate(zip(inputs, held, strict=True))
    ]
    for copy in loads + merges:
        copy.start()
    for copy in loads:
        copy.wait()
    total = own_back[...]
    for other in others:
        total = total + other[...].astype(F32)
    scaled = total * vec_ref[2:3, :]
    unit, rstd = normalise(hidden_ref[...])
    first = jnp.mean(scaled, 1, keepdims=True)
    second = jnp.mean(scaled * unit, 1, keepdims=True)
    grad_hidden = grads_ref[...].astype(F32) + rstd * (scaled - first - unit * second)
    branch = grad_hidden.astype(BF)
    thr_m = (0.5 * mm(branch, tab_ref[0], NT)).astype(BF)
    resid_ref[...] = grad_hidden.T
    whole = (
        mm(inner_ref[...], branch, TN)[0:16, :],
        mm(thr_m, heads_ref[...], TN)[0:16, :],
    )
    ids = jnp.full((32, LANES), ident, jnp.int32).astype(F32)
    gw_ref[...] = jnp.concatenate([jnp.concatenate(whole, 0), ids], 1).astype(BF)
    for copy in merges:
        copy.wait()
    grad_heads = (mm(branch, wm[...], NT) + mm(thr_m, tails_ref[...], NT)).T.astype(BF)
    for t in range(parts):
        at = slice(t * head_rows, (t + 1) * head_rows)
        back_ref[t % groups, lax.rem(t // groups - mine + slots, slots)] = grad_heads[at, :]


def branch_part(shape, scalars, vec, tab, kept, merge, others):
    slots, groups, parts = shape.slots, shape.groups, shape.parts
    block, dim = kept[0].shape
    out = (
        jax.ShapeDtypeStruct((dim, block), F32),
        jax.ShapeDtypeStruct((groups, slots, dim // parts, block), BF),
        jax.ShapeDtypeStruct((32, dim + LANES), BF),
    )
    return pl.pallas_call(
        partial(branch_kernel, shape),
        out_shape=out,
        in_specs=[smem()] + [vmem()] * 2 + [anywhere()] * (1 + len(kept) + len(others)),
        out_specs=tuple(vmem() for _ in out),
        scratch_shapes=[
            pltpu.VMEM((dim, dim), BF),
            pltpu.SemaphoreType.DMA((parts,)),
            pltpu.SemaphoreType.DMA((len(kept) + len(others),)),
        ]
        + [pltpu.VMEM(x.shape, x.dtype) for x in (*kept, *others)],
        compiler_params=pltpu.CompilerParams(vmem_limit_bytes=48 * MIB),
        cost_estimate=pl.CostEstimate(flops=2 * 10**9, bytes_accessed=10**7, transcendentals=0),
        name="branch_part",
    )(scalars, vec, tab, merge, *kept, *others)


def heads_back_kernel(shape, slot, sc, qkv_ref, lse_ref, own_dout, *rest):
    groups = shape.groups
    douts = (own_dout,) + rest[: groups - 1]
    out_ref, dout_rel, dot_scr, grad_scr, sem = rest[groups - 1 :]
    _, head_rows, block = dout_rel.shape
    span = groups * block
    heads_here = head_rows // HEAD_DIM
    member = sc[1]
    h = pl.program_id(0)

    @pl.when(h == 0)
    def _():
        copies = []
        for g in range(groups):
            source = own_dout.at[member, slot] if g == 0 else douts[g].at[slot]
            spot = lax.rem(member - g + groups, groups)
            copies.append(pltpu.make_async_copy(source, dout_rel.at[spot], sem.at[g]))
        run_all(copies)
        pad = jnp.zeros((HEAD_PAD - HEAD_DIM, block), F32)
        for g in range(groups):
            piece = dout_rel[g].astype(F32)
            for n in range(heads_here):
                one = jnp.concatenate([piece[n * HEAD_DIM : (n + 1) * HEAD_DIM, :], pad], 0)
                dot_scr[n, :, g * block : (g + 1) * block] = one.astype(BF)

    query_t = qkv_ref[0, 0]
    keys_t = qkv_ref[1, 0]
    query = query_t.T
    keys = keys_t.T
    vals = qkv_ref[2, 0].T
    dout_t = dot_scr[h]
    dout = dout_t.T
    dvals = jnp.zeros((span, HEAD_PAD), F32)
    dkeys = jnp.zeros((span, HEAD_PAD), F32)
    row = pl.multiple_of(h * HEAD_DIM, 8)
    for c in range(span // CHUNK):
        cols = slice(c * CHUNK, (c + 1) * CHUNK)
        scores = mm(keys, query_t[:, cols]) * (SCALE * LOG2E)
        probs = jnp.exp2(scores - lse_ref[0, 0:1, cols])
        dprobs = mm(vals, dout_t[:, cols])
        delta = jnp.sum(probs * dprobs, 0, keepdims=True)
        dscores = (probs * (dprobs - delta)).astype(BF)
        dvals += mm(probs.astype(BF), dout[cols, :])
        dkeys += mm(dscores, query[cols, :])
        dquery = mm(keys_t, dscores) * SCALE
        grad_scr[pl.ds(row, HEAD_DIM), cols] = dquery[0:HEAD_DIM, :]
    row = pl.multiple_of(row + head_rows, 8)
    grad_scr[pl.ds(row, HEAD_DIM), :] = (dkeys * SCALE).T[0:HEAD_DIM, :]
    row = pl.multiple_of(row + head_rows, 8)
    grad_scr[pl.ds(row, HEAD_DIM), :] = dvals.T[0:HEAD_DIM, :]

    @pl.when(h == heads_here - 1)
    def _():
        out_ref[...] = grad_scr[...].astype(BF)


def heads_back(shape, slot, scalars, qkv, lse, dout):
    own, others = dout
    groups, _, head_rows, block = own.shape
    span = groups * block
    heads_here = head_rows // HEAD_DIM
    return pl.pallas_call(
        partial(heads_back_kernel, shape, slot),
        grid=(heads_here,),
        out_shape=jax.ShapeDtypeStruct((3 * head_rows, span), BF),
        in_specs=[
            smem(),
            pl.BlockSpec((3, 1, HEAD_PAD, span), lambda h: (0, slot * heads_here + h, 0, 0)),
            pl.BlockSpec((1, 1, span), lambda h: (slot * heads_here + h, 0, 0)),
            anywhere(),
        ]
        + [anywhere()] * len(others),
        out_specs=pl.BlockSpec((3 * head_rows, span), lambda h: (0, 0)),
        scratch_shapes=[
            pltpu.VMEM((groups, head_rows, block), BF),
            pltpu.VMEM((heads_here, HEAD_PAD, span), BF),
            pltpu.VMEM((3 * head_rows, span), F32),
            pltpu.SemaphoreType.DMA((groups,)),
        ],
        compiler_params=pltpu.CompilerParams(vmem_limit_bytes=40 * MIB),
        cost_estimate=pl.CostEstimate(flops=10**9, bytes_accessed=40 * 10**6, transcendentals=0),
        name="heads_back",
    )(scalars, qkv, lse, own, *others)


def rank_back_kernel(shape, sc, down_ref, upx_ref, n1_ref, inner_ref, *rest):
    slots = shape.slots
    grads = rest[:slots]
    td_ref, tu_ref, thr_ref = rest[slots:]
    dim, span = n1_ref.shape
    head_rows = upx_ref.shape[2] // 3
    ident = sc[4]
    rank = down_ref.shape[0]
    spread = 3 * head_rows
    thr = jnp.zeros((rank, span), F32)
    row_of = lax.broadcasted_iota(jnp.int32, (rank, spread), 0) // 16
    part_of = lax.broadcasted_iota(jnp.int32, (rank, spread), 1) // head_rows
    for k in range(slots):
        thr = thr + mm(upx_ref[k], grads[k][...])
        ups = mm(inner_ref[...], grads[k][...], NT)
        ups = jnp.where(row_of == part_of, ups, 0.0)
        ups = ups[0:16, :] + ups[16:32, :] + ups[32:48, :]
        blank = jnp.zeros((16, dim + LANES - spread), F32)
        tu_ref[k] = jnp.concatenate([ups, blank], 1).astype(BF)
    line = lax.broadcasted_iota(jnp.int32, (rank, span), 0)
    thr_b = jnp.where(line < 48, 0.5 * thr, 0.0).astype(BF)
    thr_ref[...] = thr_b
    downs = mm(thr_b, n1_ref[...], NT)
    ids = jnp.full((48, LANES), ident, jnp.int32).astype(F32)
    td_ref[...] = jnp.concatenate([downs[0:48, :], ids], 1).astype(BF)


def rank_back(shape, scalars, down, upx, n1, inner, grads):
    slots = shape.slots
    dim, span = n1.shape
    out = (
        jax.ShapeDtypeStruct((48, dim + LANES), BF),
        jax.ShapeDtypeStruct((slots, 16, dim + LANES), BF),
        jax.ShapeDtypeStruct((down.shape[0], span), BF),
    )
    return pl.pallas_call(
        partial(rank_back_kernel, shape),
        out_shape=out,
        in_specs=[smem()] + [vmem()] * (4 + slots),
        out_specs=(vmem(), vmem(), vmem()),
        compiler_params=pltpu.CompilerParams(vmem_limit_bytes=40 * MIB),
        cost_estimate=pl.CostEstimate(flops=10**9, bytes_accessed=40 * 10**6, transcendentals=0),
        name="rank_back",
    )(scalars, down, upx, n1, inner, *grads)


def norm_back_kernel(shape, sc, norm_ref, down_ref, thr_ref, stats_ref, rows_ref, resid_ref, own_w, *rest):
    slots, groups, parts = shape.slots, shape.groups, shape.parts
    foreign = rest[: 2 * (slots - 1)]
    rest = rest[2 * (slots - 1) :]
    grads = rest[:slots]
    out_ref, weights, e1_scr, sem = rest[slots:]
    _, dim, block = rows_ref.shape
    span = groups * block
    width = dim // parts
    spread = own_w.shape[0]
    member, row = sc[1], sc[3]
    run_all(weight_copies(shape, row, own_w, foreign, weights, sem))

    def final_step(c, carry):
        cols = pl.ds(pl.multiple_of(c * CHUNK, CHUNK), CHUNK)
        total = mm(down_ref[...], thr_ref[:, cols], TN)
        for k in range(slots):
            total = total + mm(weights[k, 0:spread, :], grads[k][:, cols], TN)
        e1_scr[:, cols] = total * norm_ref[:, 0:1]
        return carry

    lax.fori_loop(0, span // CHUNK, final_step, 0)
    for g in range(groups):
        cols = slice(g * block, (g + 1) * block)
        e1 = e1_scr[:, cols]
        first = jnp.sum(e1, 0, keepdims=True)
        mean, rstd = stats_ref[0:1, cols], stats_ref[1:2, cols]
        unit = (rows_ref[g].astype(F32) - mean) * rstd
        second = jnp.sum(e1 * unit, 0, keepdims=True)
        lines = []
        for value in (first, second, mean, rstd):
            high = value.astype(BF).astype(F32)
            lines += [high, value - high]
        lines = jnp.concatenate(lines + [jnp.zeros((8, block), F32)], 0).astype(BF)
        e1 = e1 + resid_ref[...] * (jnp.where(member == g, 1.0, 0.0) / rstd)
        for t in range(parts):
            out_ref[t, 0:width, cols] = e1[t * width : (t + 1) * width, :].astype(BF)
            out_ref[t, width : width + 16, cols] = lines


def norm_back(shape, scalars, norm, down, thr, stats, rows, resid, own_w, foreign, grads):
    slots, parts = shape.slots, shape.parts
    groups, dim, block = rows.shape
    span = groups * block
    weight_rows = max([own_w.shape[0]] + [w.shape[1] * shape.copies for w in foreign])
    return pl.pallas_call(
        partial(norm_back_kernel, shape),
        out_shape=jax.ShapeDtypeStruct((parts, dim // parts + 16, span), BF),
        in_specs=[smem()] + [vmem()] * 6 + [anywhere()] * (1 + len(foreign)) + [vmem()] * slots,
        out_specs=vmem(),
        scratch_shapes=[
            pltpu.VMEM((slots, weight_rows, dim), BF),
            pltpu.VMEM((dim, span), F32),
            pltpu.SemaphoreType.DMA((1 + (slots - 1) * shape.copies,)),
        ],
        compiler_params=pltpu.CompilerParams(vmem_limit_bytes=48 * MIB),
        cost_estimate=pl.CostEstimate(flops=10**9, bytes_accessed=40 * 10**6, transcendentals=0),
        name="norm_back",
    )(scalars, norm, down, thr, stats, rows, resid, own_w, *foreign, *grads)


def tokens_kernel(shape, seq, img_ref, held, out_ref):
    slots, groups, parts = shape.slots, shape.groups, shape.parts
    _, width, span = img_ref.shape
    dim = parts * width
    for n in range(slots):
        total = held[n * groups].astype(F32)
        lines = total[width : width + 16, :]
        mean = lines[4:5, :] + lines[5:6, :]
        rstd = lines[6:7, :] + lines[7:8, :]
        for g in range(1, groups):
            total = total + held[n * groups + g].astype(F32)
        first = (total[width : width + 1, :] + total[width + 1 : width + 2, :]) / dim
        second = (total[width + 2 : width + 3, :] + total[width + 3 : width + 4, :]) / dim
        unit = (img_ref[n].astype(F32) - mean) * rstd
        grad = rstd * (total[0:width, :] - first - unit * second)
        out_ref[:, n * seq : (n + 1) * seq] = grad[:, 0:seq]


def tokens_result(shape, seq, images, last):
    _, width, _ = images.shape
    return pl.pallas_call(
        partial(tokens_kernel, shape, seq),
        out_shape=jax.ShapeDtypeStruct((width, shape.slots * seq), F32),
        in_specs=[vmem(), vmem()],
        out_specs=vmem(),
        compiler_params=pltpu.CompilerParams(vmem_limit_bytes=40 * MIB),
        cost_estimate=pl.CostEstimate(flops=10**5, bytes_accessed=10**5, transcendentals=0),
        name="tokens_result",
    )(images, last)


def layer_kernel(shape, seq, sc, *rest):
    groups = shape.groups
    turns, out_ref = rest[:groups], rest[groups]
    for n in range(shape.slots):
        blocks = []
        for at in range(groups):
            total = turns[0][n * groups + at].astype(F32)
            for g in range(1, groups):
                total = total + turns[g][n * groups + (at - g) % groups].astype(F32)
            blocks.append(total)
        image = jnp.concatenate(blocks, 1)
        out_ref[:, n * seq : (n + 1) * seq] = image[:, 0:seq].astype(BF)


def layer_result(shape, seq, scalars, layers):
    _, width, _ = layers[0].shape
    return pl.pallas_call(
        partial(layer_kernel, shape, seq),
        out_shape=jax.ShapeDtypeStruct((width, shape.slots * seq), BF),
        in_specs=[smem()] + [vmem()] * len(layers),
        out_specs=vmem(),
        compiler_params=pltpu.CompilerParams(vmem_limit_bytes=40 * MIB),
        cost_estimate=pl.CostEstimate(flops=10**5, bytes_accessed=10**5, transcendentals=0),
        name="layer_result",
    )(scalars, *layers)


def summed(terms_ref, first, rows, adapter, count):
    images, _, cols = terms_ref.shape
    lines = slice(first, first + rows)
    total = jnp.zeros((rows, cols), F32)
    for e in range(images):
        which = terms_ref[e, 0:1, cols - 1 : cols].astype(F32)
        chosen = jnp.where(jnp.abs(which - adapter * count) < 0.5, 1.0, 0.0)
        total = total + terms_ref[e, lines, :].astype(F32) * chosen
    return total


def block_terms_kernel(count, padded, terms_ref, merge_ref, expand_ref, reduce_ref, eu_ref, rd_ref, md_ref):
    adapters, _, dim = merge_ref.shape
    hidden = eu_ref.shape[2]
    for a in range(adapters):
        whole = summed(terms_ref, 0, 64, a, count)
        for n, ref in enumerate((merge_ref, expand_ref, reduce_ref, md_ref)):
            ref[a] = whole[16 * n : 16 * n + 16, 0:dim]
        parts = summed(terms_ref, 64, 32, a, count)
        parts = jnp.concatenate([parts[0:16, :], parts[16:32, :]], 1)
        eu_ref[a] = parts[:, 0:hidden]
        rd_ref[a] = parts[:, padded : padded + hidden]


def triple_terms_kernel(count, terms_ref, down_ref, up_ref):
    _, adapters, _, dim = down_ref.shape
    rows = up_ref.shape[3]
    for a in range(adapters):
        downs = summed(terms_ref, 0, 48, a, count)
        ups = summed(terms_ref, 48, 16, a, count)
        for j in range(3):
            down_ref[j, a] = downs[16 * j : 16 * j + 16, 0:dim]
            up_ref[j, a] = ups[:, j * rows : (j + 1) * rows]


def by_adapter(kernel, terms, shapes, name):
    out = tuple(jax.ShapeDtypeStruct(one, F32) for one in shapes)
    return pl.pallas_call(
        kernel,
        out_shape=out,
        in_specs=[vmem()],
        out_specs=tuple(vmem() for _ in out),
        compiler_params=pltpu.CompilerParams(vmem_limit_bytes=40 * MIB),
        cost_estimate=pl.CostEstimate(flops=10**5, bytes_accessed=10**5, transcendentals=0),
        name=name,
    )(terms)


def shards(
    tokens,
    cotangent,
    adapter_index,
    valid_image,
    first_gain,
    first_shift,
    triple_weight,
    triple_bias,
    triple_down,
    triple_up,
    merge_weight,
    merge_bias,
    merge_down,
    merge_up,
    second_gain,
    second_shift,
    expand_weight,
    expand_bias,
    expand_down,
    expand_up,
    reduce_weight,
    reduce_bias,
    reduce_down,
    reduce_up,
    *,
    parts,
    copies,
):
    slots = adapter_index.shape[0]
    shape = Shape(parts, slots, copies)
    groups = shape.groups
    seq = tokens.shape[0] // slots
    width = tokens.shape[1]
    dim = width * parts
    head_rows = triple_weight.shape[2]
    adapters = triple_down.shape[1]
    span = up_to(seq, CHUNK)
    block = span // groups
    place = lax.axis_index("tensor")
    row = lax.axis_index("dp")
    mine, member = place // groups, place % groups

    def at(x, n, axis=0):
        return lax.dynamic_index_in_dim(x, n, axis, False)

    def jump(x, k, g):
        perm = [
            (s, ((s // groups + k) % slots) * groups + (s % groups + g) % groups)
            for s in range(parts)
        ]
        return lax.ppermute(x, "tensor", perm)

    def swap(x):
        return lax.all_to_all(x, "tensor", 0, 0)

    def spread_images(x):
        first = [at(x, mine)] + [jump(at(x, (mine + k) % slots), k, 0) for k in range(1, slots)]
        out = []
        for x_k in first:
            out.append(x_k)
            out += [jump(x_k, 0, g) for g in range(1, groups)]
        return out

    def cross(x, bit):
        return lax.ppermute(x, "dp", [(d, d ^ bit) for d in range(copies)])

    def widen(near, bits):
        for bit in bits:
            near = jnp.concatenate([near, cross(near, bit)], 0)
        return near

    def hyper(near, order):
        near = widen(near, order[:-1])
        return [near, cross(near, order[-1])]

    def after(x, *others):
        return lax.optimization_barrier((x, *others))[0]

    def images_of(x):
        flat = x.T
        return jnp.stack(
            [
                jnp.pad(flat[:, n * seq : (n + 1) * seq], ((0, 0), (0, span - seq)))
                for n in range(slots)
            ]
        )

    images = images_of(tokens)
    tok_first = [at(images, (mine + k) % slots) for k in range(slots)]
    tok_first, adapter_index, triple_weight, valid_image, expand_weight, reduce_weight = (
        lax.optimization_barrier(
            (tok_first, adapter_index, triple_weight, valid_image, expand_weight, reduce_weight)
        )
    )
    toks = [tok_first[0]] + [jump(tok_first[k], k, 0) for k in range(1, slots)]
    ready = toks[slots - 1]
    toks = [x if g == 0 else jump(x, 0, g) for x in toks for g in range(groups)][1:]

    index = at(adapter_index, mine)
    valid = at(valid_image, mine)
    scalars = jnp.stack([mine, member, valid, row, index, place]).astype(jnp.int32)

    flat_triple = triple_weight.transpose(0, 2, 1).reshape(3 * head_rows, dim)
    piece_rows = up_to(3 * head_rows, 16 * copies) // copies
    padded = jnp.pad(flat_triple, ((0, piece_rows * copies - 3 * head_rows), (0, 0)))
    my_piece = lax.dynamic_slice_in_dim(padded, row * piece_rows, piece_rows, 0)

    def up_pack(which):
        table = at(triple_up, which, 1).transpose(1, 0, 2).reshape(16, 3 * head_rows)
        bias = jnp.pad(triple_bias.reshape(1, 3 * head_rows), ((0, 15), (0, 0)))
        return jnp.pad(jnp.concatenate([table, bias], 0), ((0, 0), (0, dim - 3 * head_rows)))

    foreign, ups, arrived = [], [up_pack(index)], [ready]
    for k in range(1, slots):
        packed = up_pack(at(adapter_index, (mine - k) % slots))
        got = jump(jnp.concatenate([my_piece, packed], 0), -k, 0)
        arrived.append(got)
        ups.append(got[piece_rows:])
        foreign += hyper(got[None, :piece_rows], shape.bits)
    ups = jnp.stack(ups)
    ready = after(*arrived, toks[-1])

    merge_rows = up_to(width, 16 * copies) // copies
    merge_piece = lax.dynamic_slice_in_dim(
        jnp.pad(merge_weight, ((0, merge_rows * copies - width), (0, 0))), row * merge_rows, merge_rows, 0
    )
    hidden_here = reduce_weight.shape[0]
    hidden_rows = up_to(hidden_here, 8 * copies)
    extra = ((0, hidden_rows - hidden_here), (0, 0))
    mlp_rows = 2 * hidden_rows // copies
    half = copies // 2

    def mlp_part(x):
        return lax.dynamic_slice_in_dim(jnp.pad(x, extra), (row % half) * mlp_rows, mlp_rows, 0)

    my_w = jnp.where(row < half, mlp_part(expand_weight.T), mlp_part(reduce_weight))
    natural = ((1, 0, None),)
    near_masks = list(range(0, copies, 2))
    merge_all = lax.all_gather(merge_piece, ("tensor", "dp")).reshape(parts, merge_rows * copies, dim)
    late_w = after(my_w, ready)
    pieces = [jump(late_w, -k, 0) for k in range(1, slots)]
    own_expand = jnp.pad(after(expand_weight.T, ready), extra)
    own_reduce = jnp.pad(after(reduce_weight, ready), extra)

    down = jnp.pad(at(triple_down, index, 1).transpose(0, 2, 1).reshape(48, dim), ((0, 16), (0, 0)))
    norm = jnp.pad(jnp.stack([first_gain, first_shift], 1).astype(F32), ((0, 0), (0, 6)))

    late_index = after(adapter_index, ready)

    def factor_pack(which):
        def lanes(x):
            return jnp.pad(x, ((0, 16 - x.shape[0]), (0, hidden_rows - x.shape[1])))

        return jnp.concatenate(
            [lanes(at(expand_up, which)), lanes(expand_bias[None, :]), lanes(at(reduce_down, which).T)], 0
        )

    packs = [factor_pack(at(late_index, (mine - k) % slots)) for k in range(slots)]
    late = after(index, ready)
    tab = jnp.stack(
        [
            jnp.pad(x, ((0, LANES - 16), (0, 0)))
            for x in (at(merge_up, late), at(expand_down, late).T, at(reduce_up, late))
        ]
    )
    vec = jnp.pad(
        jnp.stack([merge_bias, reduce_bias, second_gain, second_shift]).astype(F32), ((0, 4), (0, 0))
    )

    merge_lines = [at(merge_down, late_index[n]).T for n in range(slots)]
    merge_lines = jnp.pad(jnp.stack(merge_lines), ((0, 0), (0, 0), (0, span - width)))
    cot_parts = jnp.concatenate([images_of(after(cotangent, ready)), merge_lines], 1)

    def trade(x):
        return x, [jump(at(x, (member + g) % groups), 0, g) for g in range(1, groups)]

    begin = after(scalars, own_expand, own_reduce, tab, vec, cot_parts, *packs)
    qkv, n1, stats, inner, rows, upx = project(
        shape, seq, begin, norm, down, ups, images, toks, flat_triple, foreign
    )
    fac = [packs[0]] + [jump(packs[k], -k, 0) for k in range(1, slots)]
    cots = {(k, 0): jump(at(cot_parts, (mine + k) % slots), k, 0) for k in range(1, slots)}
    own_cot = at(cot_parts, mine)
    cots.update({(0, g): jump(own_cot, 0, g) for g in range(1, groups)})
    pieces, cots = lax.optimization_barrier((pieces, cots, stats))[:2]
    pieces = [lax.all_gather(x, "dp") for x in pieces]
    begin = after(scalars, *cots.values())
    cots.update({(k, g): jump(cots[k, 0], 0, g) for k in range(1, slots) for g in range(1, groups)})
    lse, heads = attend(shape, begin, qkv)
    heads, cots, fac = lax.optimization_barrier((heads, cots, fac))
    heads = (heads, [jump(heads, 0, g) for g in range(1, groups)])
    fac = jnp.stack(fac)
    cots = [cots[pair] for pair in shape.pairs[1:]]
    layers, near, gms, gws = [None] * groups, [], [], []
    for turn in list(range(1, groups)) + [0]:
        begin = scalars
        layers[turn], back, gm, gw, *kept = hidden_part(
            shape,
            turn,
            begin,
            vec,
            tab,
            fac,
            rows,
            (own_expand, own_reduce),
            merge_all,
            cot_parts,
            cots,
            heads,
            pieces,
        )
        gms.append(gm)
        gws.append(gw)
        if turn:
            near.append(jump(back, 0, turn))
            scalars = after(scalars, back)
    near, layers[1:], kept = lax.optimization_barrier((near, layers[1:], kept))
    layers[1:] = [swap(x) for x in layers[1:]]
    resid, back, gw_branch = branch_part(
        shape, scalars, vec, tab, [back] + kept, merge_all, near
    )
    dout = trade(back)

    def spread_rows(x):
        share = x.shape[0] // copies
        own = lax.dynamic_slice_in_dim(x, row * share, share, 0)
        return jnp.stack([own] + [jump(own, k, g) for k, g in shape.pairs[1:]])

    def members_sum(x, beside):
        out, rows = [], x.shape[0]
        for k in range(slots):
            both = jnp.concatenate([x, beside[k]], 0)
            both = jump(both, k, 0) if k else both
            total = both[:rows].astype(F32)
            for g in range(1, groups):
                total = total + jump(x, k, g).astype(F32)
            out.append(jnp.concatenate([total.astype(BF), both[rows:]], 0))
        return jnp.stack(out)

    layers[0] = swap(layers[0])
    grads = [heads_back(shape, 0, after(scalars, *layers[1:]), qkv, lse, dout)]
    gms, gws, gw_branch, begin = lax.optimization_barrier((gms, gws, gw_branch, scalars, grads[0]))[:4]
    gm = sum(x.astype(F32) for x in gms).astype(BF)
    gw = sum(x.astype(F32) for x in gws).astype(BF)
    gm = members_sum(jnp.concatenate([gw_branch[0:16], gw, gw_branch[16:32]], 0), gm)
    for k in range(1, slots):
        grads.append(heads_back(shape, k, after(begin, layers[0]), qkv, lse, dout))
    gm = after(gm, grads[-1])
    td, tu, thr = rank_back(shape, after(scalars, gm), down, upx, n1, inner, grads)
    td = members_sum(td, tu)
    last = norm_back(shape, scalars, norm, down, thr, stats, rows, resid, flat_triple, foreign, grads)
    last, td = lax.optimization_barrier((last, td))
    last = swap(last)
    gm = lax.all_gather(gm, "dp", tiled=True)
    near = jnp.concatenate([td] + [cross(td, mask) for mask in near_masks[1:]], 0)
    merge_up_grad, expand_down_grad, reduce_up_grad, expand_up_grad, reduce_down_grad, merge_down_grad = by_adapter(
        partial(block_terms_kernel, groups, hidden_rows),
        gm,
        ((adapters, 16, dim),) * 3 + ((adapters, 16, hidden_here),) * 2 + ((adapters, 16, dim),),
        "block_terms",
    )
    merge_down_grad = lax.dynamic_slice_in_dim(merge_down_grad, place * width, width, 2)
    td = jnp.concatenate([near, cross(near, 1)], 0)
    layer_out = layer_result(shape, seq, after(scalars, gm), layers).T
    downs, triple_up_grad = by_adapter(
        partial(triple_terms_kernel, groups),
        td,
        ((3, adapters, 16, dim), (3, adapters, 16, head_rows)),
        "triple_terms",
    )
    tokens_grad = tokens_result(shape, seq, after(images, downs), last).T

    return (
        layer_out,
        tokens_grad,
        downs.transpose(0, 1, 3, 2),
        triple_up_grad,
        merge_down_grad.transpose(0, 2, 1),
        merge_up_grad,
        expand_down_grad.transpose(0, 2, 1),
        expand_up_grad,
        reduce_down_grad.transpose(0, 2, 1),
        reduce_up_grad,
    )


def solution(mesh):
    in_specs = (
        P("dp", "tensor"),
        P("dp", "tensor"),
        P("dp"),
        P("dp"),
        P(),
        P(),
        P(None, None, "tensor"),
        P(None, "tensor"),
        P(),
        P(None, None, None, "tensor"),
        P("tensor", None),
        P(),
        P(None, "tensor", None),
        P(),
        P(),
        P(),
        P(None, "tensor"),
        P("tensor"),
        P(),
        P(None, None, "tensor"),
        P("tensor", None),
        P(),
        P(None, "tensor", None),
        P(),
    )
    out_specs = (
        P("dp", "tensor"),
        P("dp", "tensor"),
        P(),
        P(None, None, None, "tensor"),
        P(None, "tensor", None),
        P(),
        P(),
        P(None, None, "tensor"),
        P(None, "tensor", None),
        P(),
    )
    return jax.shard_map(
        partial(shards, parts=mesh.shape["tensor"], copies=mesh.shape["dp"]),
        mesh=mesh,
        in_specs=in_specs,
        out_specs=out_specs,
        check_vma=False,
    )
```

time: 419 us -> 396 us (0.945)
  blocking collectives: 32 us -> 0 us
  starting transfers between devices: 72.9 us -> 45.2 us
  local copies, waits for them, and re-layouts: 33.5 us -> 53.2 us
  between operations: 11.8 us -> 28.8 us
  waiting for transfers between devices: 119 us -> 104 us
  Pallas kernels: 128 us -> 137 us
  other arithmetic: 16.5 us -> 21.3 us
    ppermute x25 -> x7, waiting for transfers between devices: 57.2 us -> 22.1 us  [cross(): return lax.ppermute(x, 'dp', [(d, d ^ bit) for d in range(copies)])]
    all_gather x3 -> x0, blocking collectives: 32 us -> none  [the longest x1 11.4 us: shards(): lax.all_gather(downs, 'dp')]
    ppermute x34 -> x18, starting transfers between devices: 52.5 us -> 26.2 us  [jump(): return lax.ppermute(x, 'tensor', perm)]
    unnamed x104 -> x156, local copies, waits for them, and re-layouts: 6.81 us -> 27.8 us
    ppermute x25 -> x7, starting transfers between devices: 20.4 us -> 7.2 us  [cross(): return lax.ppermute(x, 'dp', [(d, d ^ bit) for d in range(copies)])]
    pallas_call x5 -> x6, Pallas kernels: 70.2 us -> 82.1 us  [the longest x2 48.9 us: hidden_part(): pl.pallas_call(partial(hidden_kernel, shape, turn), out_shape=out, in_spe...]
    all_to_all x0 -> x3, starting transfers between devices: none -> 11.7 us  [swap(): return lax.all_to_all(x, 'tensor', 0, 0)]
    all_to_all x0 -> x3, waiting for transfers between devices: none -> 11 us  [swap(): return lax.all_to_all(x, 'tensor', 0, 0)]
  transfers between devices with their start and end apart: 59 -> 31, of which waited for: 23 -> 11; matrix products, arithmetic and copies ran while one was open for 10% -> 11% of each run, Pallas kernels for 19% -> 27%
where the time goes in v3:
time: 396 us; the launch traced here: 390 us
  Pallas kernels  137 us (35%)
  waiting for transfers between devices  104 us (26%)
  local copies, waits for them, and re-layouts  53.2 us (13%)
  starting transfers between devices  45.2 us (11%)
  between operations  28.8 us (7%)
  other arithmetic  21.3 us (5%)
    ppermute x18, waiting for transfers between devices, jump(): return lax.ppermute(x, 'tensor', perm)  71.1 us
    pallas_call x2, Pallas kernels, hidden_part(): pl.pallas_call(partial(hidden_kernel, shape, turn), out_shape=out, in_spe...  48.9 us
    unnamed x156, local copies, waits for them, and re-layouts  27.8 us
    ppermute x18, starting transfers between devices, jump(): return lax.ppermute(x, 'tensor', perm)  26.2 us
    ppermute x7, waiting for transfers between devices, cross(): return lax.ppermute(x, 'dp', [(d, d ^ bit) for d in range(copies)])  22.1 us
    pallas_call x2, Pallas kernels, heads_back(): pl.pallas_call(partial(heads_back_kernel, shape, slot), grid=(heads_here,...  21 us
    pallas_call x1, Pallas kernels, project(): pl.pallas_call(partial(project_kernel, shape, seq), out_shape=out, in_spe...  15.7 us
    pallas_call x1, Pallas kernels, attend(): pl.pallas_call(partial(attend_kernel, slots), grid=(heads,), out_shape=ou...  14.5 us
  transfers between devices with their start and end apart: 31, of which 11 were waited for; matrix products, arithmetic and copies ran while one was open for 11% of the time, Pallas kernels for 27%

profile of v3, /device:TPU:0, one launch (start us, length us, event | category | flops | bytes accessed | tf_op | source)
XLA Modules:
  0.0 389.7 jit_solution(11175017605525725749)
XLA Ops:
  7.3 1.7 pad_dynamic-slice_fusion.7
  9.1 1.2 slice.75
  10.4 1.7 fusion.7
  12.1 2.4 fusion.5
  21.9 4.0 %collective-permute-start.1 = (bf16[144,1152]{1,0:T(8,128)(2,1)}, bf16[144,1152]{1,0:T(8,128)(2,1)}, u32[]{:S(2)}, u32[]{:S(2)}) collective-permute-start(bf16[144,1152]{1,0:T(8,128)(2,1)} %fusion.8), channel_id=1, source_target_pairs={{0,2},{1,3},{2,0},{3,1},{4,6},{5,7},{6,4},{7,5},{8,10},{9,11},{10,... | collective-permute-start | bytes 995336 | tf_op jit(solution)/shard_map/ppermute | solution.py:898
  26.0 1.9 collective-permute-start.6
  29.0 1.4 stack.123.sc
  31.1 1.5 pad_maximum_fusion.1.own_tok.img_ref
  32.6 2.5 fusion.1
  35.1 18.1 %collective-permute-done.1 = bf16[144,1152]{1,0:T(8,128)(2,1)} collective-permute-done((bf16[144,1152]{1,0:T(8,128)(2,1)}, bf16[144,1152]{1,0:T(8,128)(2,1)}, u32[]{:S(2)}, u32[]{:S(2)}) %collective-permute-start.1) | collective-permute-done | bytes 331808 | tf_op jit(solution)/shard_map/ppermute | solution.py:898
  54.1 1.8 collective-permute-start.7
  56.8 9.8 %collective-permute-done.rest_1_ = bf16[288,768]{1,0:T(8,128)(2,1)S(1)} collective-permute-done((bf16[288,768]{1,0:T(8,128)(2,1)}, bf16[288,768]{1,0:T(8,128)(2,1)S(1)}, u32[]{:S(2)}, u32[]{:S(2)}) %collective-permute-start) | collective-permute-done | bytes 442400 | tf_op jit(solution)/shard_map/ppermute | solution.py:898
  67.8 1.8 collective-permute-start.8
  69.6 13.1 %collective-permute-done.2.rest_2_ = bf16[288,768]{1,0:T(8,128)(2,1)S(1)} collective-permute-done((bf16[288,768]{1,0:T(8,128)(2,1)S(1)}, bf16[288,768]{1,0:T(8,128)(2,1)S(1)}, u32[]{:S(2)}, u32[]{:S(2)}) %collective-permute-start.2) | collective-permute-done | bytes 442400 | tf_op jit(solution)/shard_map/ppermute | solution.py:898
  89.6 2.0 slice.77
  91.6 1.9 collective-permute-start.3
  95.5 1.1 pad_bitcast_fusion
  96.6 1.1 fusion.6
  100.7 1.4 collective-permute-start.4
  106.5 1.5 pad_maximum_fusion.2.rest_3_.rest_0_
  111.4 1.6 pad.109.own_expand
  114.0 1.6 pad.110.own_reduce
  115.7 15.7 %project.1 = (bf16[3,8,80,768]{3,2,1,0:T(8,128)(2,1)}, bf16[1152,768]{1,0:T(8,128)(2,1)}, f32[8,768]{1,0:T(8,128)S(1)}, bf16[64,768]{1,0:T(8,128)(2,1)S(1)}, bf1...) custom-call(s32[6]{0:T(128)S(1)} %stack.123.sc, f32[1152,8]{1,0:T(8,128)S(1)} %pad_convert_fusion.norm_ref, ...), custom_call_target="tpu_custom_call" | custom-call | flops 4000000000 | bytes 40000000 | tf_op jit(solution)/shard_map/project/pallas_call | solution.py:194
  133.4 8.3 %collective-permute-done.5.rest_1_ = bf16[304,768]{1,0:T(8,128)(2,1)} collective-permute-done((bf16[304,768]{1,0:T(8,128)(2,1)}, bf16[304,768]{1,0:T(8,128)(2,1)}, u32[]{:S(2)}, u32[]{:S(2)}) %collective-permute-start.5) | collective-permute-done | bytes 466976 | tf_op jit(solution)/shard_map/ppermute | solution.py:898
  141.8 3.1 collective-permute-start.11
  144.9 1.8 copy-done.2
  146.8 14.5 %attend.1 = (f32[8,1,768]{2,1,0:T(1,128)S(1)}, bf16[2,288,768]{2,1,0:T(8,128)(2,1)S(1)}) custom-call(s32[6]{0:T(128)S(1)} %stack.123.sc, bf16[3,8,80,768]{3,2,1,0:T(8,128)(2,1)S(1)} %copy-done.2), custom_call_target="tpu_custom_call" | custom-call | flops 4000000000 | bytes 60000000 | tf_op jit(solution)/shard_map/attend/pallas_call | solution.py:242
  163.0 20.1 %collective-permute-done.12.rest_3_ = bf16[2,288,768]{2,1,0:T(8,128)(2,1)} collective-permute-done((bf16[2,288,768]{2,1,0:T(8,128)(2,1)S(1)}, bf16[2,288,768]{2,1,0:T(8,128)(2,1)}, u32[]{:S(2)}, u32[]{:S(2)}) %collective-permute-start.12) | collective-permute-done | bytes 884768 | tf_op jit(solution)/shard_map/ppermute | solution.py:898
  183.1 23.6 %hidden_part.2 = (bf16[4,288,384]{2,1,0:T(8,128)(2,1)}, bf16[384,1152]{1,0:T(8,128)(2,1)}, bf16[2,32,1280]{2,1,0:T(8,128)(2,1)}, bf16[32,1280]{1,0:T(8,128)(2,1)}) custom-call(s32[6]{0:T(128)} %copy-done.41, f32[8,1152]{1,0:T(8,128)} %fusion.32.vec_ref, bf16[3,128,1152]{2,1,0:T(8,128)(2,1)} %pad_maximum_fusion.4.tab_ref, ...), custom_call_target="tpu_custom_call" | custom-call | flops 10000000000 | bytes 60000000 | tf_op jit(solution)/shard_map/hidden_part/pallas_call | solution.py:452
  207.2 25.3 %hidden_part.3 = (bf16[4,288,384]{2,1,0:T(8,128)(2,1)}, f32[384,1152]{1,0:T(8,128)}, bf16[2,32,1280]{2,1,0:T(8,128)(2,1)}, bf16[32,1280]{1,0:T(8,128)(2,1)}, f32...) custom-call(s32[6]{0:T(128)} %copy-done.41, ...), custom_call_target="tpu_custom_call" | custom-call | flops 10000000000 | bytes 60000000 | tf_op jit(solution)/shard_map/hidden_part/pallas_call | solution.py:452
  232.5 3.6 all-to-all-start
  236.2 1.2 copy-done.27
  237.4 1.2 copy-done.28
  241.1 6.3 %branch_part.1 = (f32[1152,384]{1,0:T(8,128)}, bf16[2,2,288,384]{3,2,1,0:T(8,128)(2,1)S(1)}, bf16[32,1280]{1,0:T(8,128)(2,1)S(1)}) custom-call(s32[6]{0:T(128)S(1)} %copy-done.42, f32[8,1152]{1,0:T(8,128)S(1)} %copy-done.32, bf16[3,128,1152]{2,1,0:T(8,128)(2,1)S(1)} %copy-done.8, bf16[4,384,1152]{2,1,0:T(8,128)(2,1)} %bitcast.129, ...), custom_call_target="tpu_custom_call" | custom-call | flops 2000000000 | bytes 10000000 | tf_op jit(solution)/shard_map/branch_part/pallas_call | solution.py:532
  248.1 2.0 collective-permute-start.14
  250.0 8.5 %all-to-all-done.rest_1_ = bf16[4,288,384]{2,1,0:T(8,128)(2,1)S(1)} async-done(((bf16[4,288,384]{2,1,0:T(8,128)(2,1)}), bf16[4,288,384]{2,1,0:T(8,128)(2,1)S(1)}, u32[]{:S(2)}, u32[]{:S(2)}) %all-to-all-start) | async-done | bytes 884768 | tf_op jit(solution)/shard_map/all_to_all | solution.py:901
  258.5 3.5 all-to-all-start.1
  262.1 1.7 collective-permute-done.14.rest_0_
  264.5 1.8 copy-done.3
  268.1 10.6 %heads_back.2.rest_0_.rest_2_ = bf16[864,768]{1,0:T(8,128)(2,1)S(1)} custom-call(s32[6]{0:T(128)S(1)} %copy-done.42, bf16[3,8,80,768]{3,2,1,0:T(8,128)(2,1)S(1)} %copy-done.3, f32[8,1,768]{2,1,0:T(1,128)S(1)} %copy-done.35, bf16[2,2,288,384]{3,2,1,0:T(8,128)(2,1)S(1)} %get-tuple-element.144.own_dout, bf16[2,288,384]{2,1,0:T(8,128)(2,1)S(1)} %copy-done.20), custom_call_target="tpu_custom_call" | custom-call | flops 1000000000 | bytes 40000000 | tf_op jit(solution)/shard_map/heads_back/pallas_call | solution.py:610
  279.8 4.5 %collective-permute-start.17 = (bf16[64,1280]{1,0:T(8,128)(2,1)}, bf16[64,1280]{1,0:T(8,128)(2,1)}, u32[]{:S(2)}, u32[]{:S(2)}) collective-permute-start(bf16[64,1280]{1,0:T(8,128)(2,1)} %pad_maximum_fusion.10), channel_id=1, source_target_pairs={{0,3},{1,2},{2,1},{3,0},{4,7},{5,6},{6,5},{7,4},{8,11},{9,10},{10,... | collective-permute-start | bytes 491528 | tf_op jit(solution)/shard_map/ppermute | solution.py:898
  287.3 1.8 copy-done.4
  290.8 10.4 %heads_back.3.rest_1_.rest_3_ = bf16[864,768]{1,0:T(8,128)(2,1)S(1)} custom-call(s32[6]{0:T(128)S(1)} %copy-done.42, bf16[3,8,80,768]{3,2,1,0:T(8,128)(2,1)S(1)} %copy-done.4, f32[8,1,768]{2,1,0:T(1,128)S(1)} %copy-done.36, bf16[2,2,288,384]{3,2,1,0:T(8,128)(2,1)S(1)} %get-tuple-element.144.own_dout, bf16[2,288,384]{2,1,0:T(8,128)(2,1)S(1)} %copy-done.21), custom_call_target="tpu_custom_call" | custom-call | flops 1000000000 | bytes 40000000 | tf_op jit(solution)/shard_map/heads_back/pallas_call | solution.py:610
  301.3 1.1 add_convert_fusion.2
  304.3 1.5 copy-done.22
  305.8 2.3 rank_back.1
  308.1 3.0 collective-permute-start.20
  311.1 1.5 collective-permute-start.19
  312.7 12.2 %norm_back.1 = bf16[4,304,768]{2,1,0:T(8,128)(2,1)} custom-call(s32[6]{0:T(128)S(1)} %copy-done.42, f32[1152,8]{1,0:T(8,128)S(1)} %copy-done.18, bf16[64,1152]{1,0:T(8,128)(2,1)S(1)} %copy-done.24, bf16[64,768]{1,0:T(8,128)(2,1)S(1)} %get-tuple-element.159.thr_ref, f32[8,768]{1,0:T(8,128)S(1)} %copy-done.44, ...), custom_call_target="tpu_custom_call" | custom-call | flops 1000000000 | bytes 40000000 | tf_op jit(solution)/shard_map/norm_back/pallas_call | solution.py:725
  325.1 4.5 %all-to-all-start.2 = ((bf16[4,304,768]{2,1,0:T(8,128)(2,1)}), bf16[4,304,768]{2,1,0:T(8,128)(2,1)S(1)}, u32[]{:S(2)}, u32[]{:S(2)}) async-start(bf16[4,304,768]{2,1,0:T(8,128)(2,1)} %norm_back.1), calls=%async_computation.2 | async-start | bytes 3735552 | tf_op jit(solution)/shard_map/all_to_all | solution.py:901
  329.7 1.7 collective-permute-start.23
  333.2 14.3 %collective-permute-done.23 = bf16[2,64,1280]{2,1,0:T(8,128)(2,1)S(1)} collective-permute-done((bf16[2,64,1280]{2,1,0:T(8,128)(2,1)S(1)}, bf16[2,64,1280]{2,1,0:T(8,128)(2,1)S(1)}, u32[]{:S(2)}, u32[]{:S(2)}) %collective-permute-start.23) | collective-permute-done | bytes 327712 | tf_op jit(solution)/shard_map/ppermute | solution.py:912
  347.5 4.5 %collective-permute-done.22 = bf16[2,64,1280]{2,1,0:T(8,128)(2,1)S(1)} collective-permute-done((bf16[2,64,1280]{2,1,0:T(8,128)(2,1)S(1)}, bf16[2,64,1280]{2,1,0:T(8,128)(2,1)S(1)}, u32[]{:S(2)}, u32[]{:S(2)}) %collective-permute-start.22) | collective-permute-done | bytes 327712 | tf_op jit(solution)/shard_map/ppermute | solution.py:912
  352.0 1.2 pad_maximum_fusion
  353.4 3.2 collective-permute-done.24
  356.6 1.4 constant_dynamic-update-slice_fusion.terms_ref
  358.1 1.5 copy-done.15
  359.6 1.7 copy-done.16
  361.3 5.6 %triple_terms.1 = (f32[3,8,16,1152]{3,2,1,0:T(8,128)}, f32[3,8,16,288]{3,2,1,0:T(8,128)}) custom-call(bf16[16,64,1280]{2,1,0:T(8,128)(2,1)S(1)} %copy-done.16), custom_call_target="tpu_custom_call" | custom-call | flops 100000 | bytes 100000 | tf_op jit(solution)/shard_map/triple_terms/pallas_call | solution.py:836
  367.0 2.5 all-to-all-done.2.held
  369.5 2.0 tokens_result.1
  371.4 2.1 copy-done.7
  373.5 6.7 %block_terms.1 = (f32[8,16,1152]{2,1,0:T(8,128)}, f32[8,16,1152]{2,1,0:T(8,128)}, f32[8,16,1152]{2,1,0:T(8,128)}, f32[8,16,1076]{2,1,0:T(8,128)}, f32[8,16,1076]{2,1,0:T(8,128)}, /*index=5*/f32[8,16,1152]{2,1,0:T(8,128)S(1)}) custom-call(bf16[16,96,1280]{2,1,0:T(8,128)(2,1)S(1)} %copy-done.7), custom_call_target="tpu_custom_call" | custom-call | flops 100000 | bytes 100000 | tf_op jit(solution)/shard_map/block_terms/pallas_call | solution.py:836
  381.1 1.7 layer_result.1
  (252 shorter events, 40.0 us)
Async XLA Ops:
  7.2 21.7 %copy-start = (bf16[3,8,1152,16]{2,3,1,0:T(8,128)(2,1)S(1)}, bf16[3,8,1152,16]{2,3,1,0:T(8,128)(2,1)}, u32[]{:S(2)}) copy-start(bf16[3,8,1152,16]{2,3,1,0:T(8,128)(2,1)} %param.32) | copy-start | bytes 2654212
  7.2 175.9 %all-gather.8.cloned.1.call-start = ((), (), s32[]{:S(2)}) async-start(), calls=%async_computation.4 | async-start | bytes 3649536 | tf_op jit(solution)/shard_map/all_gather | solution.py:986
  9.0 174.1 %all-gather.10.cloned.1.call-start = ((), (), s32[]{:S(2)}) async-start(), calls=%async_computation.5 | async-start | bytes 5640192 | tf_op jit(solution)/shard_map/all_gather | solution.py:1033
  9.1 8.6 %copy-start.73 = (bf16[3,288]{1,0:T(4,128)(2,1)S(1)}, bf16[3,288]{1,0:T(4,128)(2,1)}, u32[]{:S(2)}) copy-start(bf16[3,288]{1,0:T(4,128)(2,1)} %param.31) | copy-start | bytes 5188
  14.5 13.5 %copy-start.65 = (bf16[1152]{0:T(1024)(128)(2,1)S(1)}, bf16[1152]{0:T(1024)(128)(2,1)}, u32[]{:S(2)}) copy-start(bf16[1152]{0:T(1024)(128)(2,1)} %param.28) | copy-start | bytes 6916
  14.5 13.5 %copy-start.66 = (bf16[1152]{0:T(1024)(128)(2,1)S(1)}, bf16[1152]{0:T(1024)(128)(2,1)}, u32[]{:S(2)}) copy-start(bf16[1152]{0:T(1024)(128)(2,1)} %param.29) | copy-start | bytes 6916
  14.5 13.5 %copy-start.67 = (bf16[1152]{0:T(1024)(128)(2,1)S(1)}, bf16[1152]{0:T(1024)(128)(2,1)}, u32[]{:S(2)}) copy-start(bf16[1152]{0:T(1024)(128)(2,1)} %param.35) | copy-start | bytes 6916
  14.5 13.5 %copy-start.68 = (bf16[1152]{0:T(1024)(128)(2,1)S(1)}, bf16[1152]{0:T(1024)(128)(2,1)}, u32[]{:S(2)}) copy-start(bf16[1152]{0:T(1024)(128)(2,1)} %param.38) | copy-start | bytes 6916
  14.5 13.5 %copy-start.69 = (bf16[1152]{0:T(1024)(128)(2,1)S(1)}, bf16[1152]{0:T(1024)(128)(2,1)}, u32[]{:S(2)}) copy-start(bf16[1152]{0:T(1024)(128)(2,1)} %param.39) | copy-start | bytes 6916
  14.5 13.5 %copy-start.70 = (bf16[1076]{0:T(1024)(128)(2,1)S(1)}, bf16[1076]{0:T(1024)(128)(2,1)}, u32[]{:S(2)}) copy-start(bf16[1076]{0:T(1024)(128)(2,1)} %param.41) | copy-start | bytes 6460
  14.5 13.5 %copy-start.71 = (bf16[1152]{0:T(1024)(128)(2,1)S(1)}, bf16[1152]{0:T(1024)(128)(2,1)}, u32[]{:S(2)}) copy-start(bf16[1152]{0:T(1024)(128)(2,1)} %param.45) | copy-start | bytes 6916
  14.5 13.8 %copy-start.75 = (s32[2]{0:T(128)S(1)}, s32[2]{0:T(128)}, u32[]{:S(2)}) copy-start(s32[2]{0:T(128)} %param.27) | copy-start | bytes 28
  21.9 31.2 %collective-permute-start.1 = (bf16[144,1152]{1,0:T(8,128)(2,1)}, bf16[144,1152]{1,0:T(8,128)(2,1)}, u32[]{:S(2)}, u32[]{:S(2)}) collective-permute-start(bf16[144,1152]{1,0:T(8,128)(2,1)} %fusion.8), channel_id=1, source_target_pairs={{0,2},{1,3},{2,0},{3,1},{4,6},{5,7},{6,4},{7,5},{8,10},{9,11},{10,... | collective-permute-start | bytes 995336 | tf_op jit(solution)/shard_map/ppermute | solution.py:898
  26.0 40.6 %collective-permute-start = (bf16[288,768]{1,0:T(8,128)(2,1)}, bf16[288,768]{1,0:T(8,128)(2,1)S(1)}, u32[]{:S(2)}, u32[]{:S(2)}) collective-permute-start(bf16[288,768]{1,0:T(8,128)(2,1)} %get-tuple-element.94), channel_id=1, source_target_pairs={{0,2},{1,3},{2,0},{3,1},{4,6},{5,7},{6,4},{7,5},{8,10},{9,11},{10,... | collective-permute-start | bytes 1327112 | tf_op jit(solution)/shard_map/ppermute | solution.py:898
  26.0 89.6 %collective-permute-start.6 = (bf16[288,768]{1,0:T(8,128)(2,1)}, bf16[288,768]{1,0:T(8,128)(2,1)S(1)}, u32[]{:S(2)}, u32[]{:S(2)}) collective-permute-start(bf16[288,768]{1,0:T(8,128)(2,1)} %get-tuple-element.106), channel_id=1, source_target_pairs={{0,1},{1,0},{2,3},{3,2},{4,5},{5,4},{6,7},{7,6},{8,9},{9,8},{10,11... | collective-permute-start | bytes 1327112 | tf_op jit(solution)/shard_map/ppermute | solution.py:898
  28.9 86.7 %copy-start.23 = (bf16[64,1152]{1,0:T(8,128)(2,1)}, bf16[64,1152]{1,0:T(8,128)(2,1)S(1)}, u32[]{:S(2)}) copy-start(bf16[64,1152]{1,0:T(8,128)(2,1)S(1)} %pad.118.down_ref) | copy-start | bytes 442372
  30.4 114.6 %copy-start.41 = (s32[6]{0:T(128)}, s32[6]{0:T(128)S(1)}, u32[]{:S(2)}) copy-start(s32[6]{0:T(128)S(1)} %stack.123.sc) | copy-start | bytes 76
  31.1 84.6 %copy-start.17 = (f32[1152,8]{1,0:T(8,128)}, f32[1152,8]{1,0:T(8,128)S(1)}, u32[]{:S(2)}) copy-start(f32[1152,8]{1,0:T(8,128)S(1)} %pad_convert_fusion.norm_ref) | copy-start | bytes 110596
  32.6 83.1 %copy-start.13 = (bf16[2,288,768]{2,1,0:T(8,128)(2,1)}, bf16[2,288,768]{2,1,0:T(8,128)(2,1)S(1)}, u32[]{:S(2)}) copy-start(bf16[2,288,768]{2,1,0:T(8,128)(2,1)S(1)} %pad_maximum_fusion.1.own_tok.img_ref) | copy-start | bytes 2654212
  35.1 61.5 %copy-start.72 = (pred[768]{0:T(1024)(128)(4,1)S(1)}, pred[768]{0:T(1024)(128)(4,1)}, u32[]{:S(2)}) copy-start(pred[768]{0:T(1024)(128)(4,1)} %constant.145.clone.1) | copy-start | bytes 2308
  54.1 13.7 %copy-start.50 = (bf16[1,112,1152]{2,1,0:T(8,128)(2,1)}, bf16[1,112,1152]{2,1,0:T(8,128)(2,1)S(1)}, u32[]{:S(2)}) copy-start(bf16[1,112,1152]{2,1,0:T(8,128)(2,1)S(1)} %slice_bitcast_fusion) | copy-start | bytes 774148
  54.1 12.8 %collective-permute-start.7 = (bf16[1,112,1152]{2,1,0:T(8,128)(2,1)S(1)}, bf16[1,112,1152]{2,1,0:T(8,128)(2,1)S(1)}, u32[]{:S(2)}, u32[]{:S(2)}) collective-permute-start(bf16[1,112,1152]{2,1,0:T(8,128)(2,1)S(1)} %slice_bitcast_fusion), channel_id=1, source_target_pairs={{0,16},{4,20},{8,24},{12,28},{16,0},{20,4},{24,8},{28,12},{1,17},{... | collective-permute-start | bytes 774152 | tf_op jit(solution)/shard_map/ppermute | solution.py:912
  66.6 16.1 %collective-permute-start.2 = (bf16[288,768]{1,0:T(8,128)(2,1)S(1)}, bf16[288,768]{1,0:T(8,128)(2,1)S(1)}, u32[]{:S(2)}, u32[]{:S(2)}) collective-permute-start(bf16[288,768]{1,0:T(8,128)(2,1)S(1)} %collective-permute-done.rest_1_), channel_id=1, source_target_pairs={{0,1},{1,0},{2,3},{3,2},{4,5},{5,4},{6,7},{7,6},{8,9},{9,8},{10,11... | collective-permute-start | bytes 1327112 | tf_op jit(solution)/shard_map/ppermute | solution.py:898
  67.8 38.7 %collective-permute-start.8 = (bf16[2,112,1152]{2,1,0:T(8,128)(2,1)}, bf16[2,112,1152]{2,1,0:T(8,128)(2,1)}, u32[]{:S(2)}, u32[]{:S(2)}) collective-permute-start(bf16[2,112,1152]{2,1,0:T(8,128)(2,1)} %pad_maximum_fusion.5), channel_id=1, source_target_pairs={{0,8},{4,12},{8,0},{12,4},{16,24},{20,28},{24,16},{28,20},{1,9},{5... | collective-permute-start | bytes 1548296 | tf_op jit(solution)/shard_map/ppermute | solution.py:912
  91.6 50.1 %collective-permute-start.3 = (bf16[272,1152]{1,0:T(8,128)(2,1)}, bf16[272,1152]{1,0:T(8,128)(2,1)}, u32[]{:S(2)}, u32[]{:S(2)}) collective-permute-start(bf16[272,1152]{1,0:T(8,128)(2,1)} %fusion.1), channel_id=1, source_target_pairs={{0,2},{1,3},{2,0},{3,1},{4,6},{5,7},{6,4},{7,5},{8,10},{9,11},{10,... | collective-permute-start | bytes 1880072 | tf_op jit(solution)/shard_map/ppermute | solution.py:898
  99.6 42.1 %collective-permute-start.5 = (bf16[304,768]{1,0:T(8,128)(2,1)}, bf16[304,768]{1,0:T(8,128)(2,1)}, u32[]{:S(2)}, u32[]{:S(2)}) collective-permute-start(bf16[304,768]{1,0:T(8,128)(2,1)} %get-tuple-element.174), channel_id=1, source_target_pairs={{0,2},{1,3},{2,0},{3,1},{4,6},{5,7},{6,4},{7,5},{8,10},{9,11},{10,... | collective-permute-start | bytes 1400840 | tf_op jit(solution)/shard_map/ppermute | solution.py:898
  100.7 41.0 %collective-permute-start.4 = (bf16[304,768]{1,0:T(8,128)(2,1)}, bf16[304,768]{1,0:T(8,128)(2,1)}, u32[]{:S(2)}, u32[]{:S(2)}) collective-permute-start(bf16[304,768]{1,0:T(8,128)(2,1)} %get-tuple-element.175), channel_id=1, source_target_pairs={{0,1},{1,0},{2,3},{3,2},{4,5},{5,4},{6,7},{7,6},{8,9},{9,8},{10,11... | collective-permute-start | bytes 1400840 | tf_op jit(solution)/shard_map/ppermute | solution.py:898
  108.0 7.7 %copy-start.5 = (bf16[4,112,1152]{2,1,0:T(8,128)(2,1)}, bf16[4,112,1152]{2,1,0:T(8,128)(2,1)S(1)}, u32[]{:S(2)}) copy-start(bf16[4,112,1152]{2,1,0:T(8,128)(2,1)S(1)} %pad_maximum_fusion.2.rest_3_.rest_0_) | copy-start | bytes 3096580
  108.0 7.7 %collective-permute-start.9 = (bf16[4,112,1152]{2,1,0:T(8,128)(2,1)S(1)}, bf16[4,112,1152]{2,1,0:T(8,128)(2,1)S(1)}, u32[]{:S(2)}, u32[]{:S(2)}) collective-permute-start(bf16[4,112,1152]{2,1,0:T(8,128)(2,1)S(1)} %pad_maximum_fusion.2.rest_3_.rest_0_), channel_id=1, source_target_pairs={{0,4},{4,0},{8,12},{12,8},{16,20},{20,16},{24,28},{28,24},{1,5},{5... | collective-permute-start | bytes 3096584 | tf_op jit(solution)/shard_map/ppermute | solution.py:912
  115.7 15.7 %copy-start.25 = (bf16[4,112,1152]{2,1,0:T(8,128)(2,1)}, bf16[4,112,1152]{2,1,0:T(8,128)(2,1)S(1)}, u32[]{:S(2)}) copy-start(bf16[4,112,1152]{2,1,0:T(8,128)(2,1)S(1)} %collective-permute-done.9.rest_4_.rest_1_) | copy-start | bytes 3096580
  141.7 20.2 %collective-permute-start.10 = (bf16[304,768]{1,0:T(8,128)(2,1)}, bf16[304,768]{1,0:T(8,128)(2,1)S(1)}, u32[]{:S(2)}, u32[]{:S(2)}) collective-permute-start(bf16[304,768]{1,0:T(8,128)(2,1)} %collective-permute-done.5.rest_1_), channel_id=1, source_target_pairs={{0,1},{1,0},{2,3},{3,2},{4,5},{5,4},{6,7},{7,6},{8,9},{9,8},{10,11... | collective-permute-start | bytes 1400840 | tf_op jit(solution)/shard_map/ppermute | solution.py:898
  141.8 20.1 %collective-permute-start.11 = (bf16[48,1088]{1,0:T(8,128)(2,1)}, bf16[48,1088]{1,0:T(8,128)(2,1)S(1)}, u32[]{:S(2)}, u32[]{:S(2)}) collective-permute-start(bf16[48,1088]{1,0:T(8,128)(2,1)} %get-tuple-element.192), channel_id=1, source_target_pairs={{0,2},{1,3},{2,0},{3,1},{4,6},{5,7},{6,4},{7,5},{8,10},{9,11},{10,... | collective-permute-start | bytes 313352 | tf_op jit(solution)/shard_map/ppermute | solution.py:898
  161.9 21.2 %copy-start.45 = (bf16[2,288,768]{2,1,0:T(8,128)(2,1)}, bf16[2,288,768]{2,1,0:T(8,128)(2,1)S(1)}, u32[]{:S(2)}) copy-start(bf16[2,288,768]{2,1,0:T(8,128)(2,1)S(1)} %get-tuple-element.116.own_heads) | copy-start | bytes 2654212
  161.9 21.2 %copy-start.74 = (bf16[304,768]{1,0:T(8,128)(2,1)}, bf16[304,768]{1,0:T(8,128)(2,1)S(1)}, u32[]{:S(2)}) copy-start(bf16[304,768]{1,0:T(8,128)(2,1)S(1)} %collective-permute-done.10.rest_2_) | copy-start | bytes 1400836
  161.9 21.2 %collective-permute-start.12 = (bf16[2,288,768]{2,1,0:T(8,128)(2,1)S(1)}, bf16[2,288,768]{2,1,0:T(8,128)(2,1)}, u32[]{:S(2)}, u32[]{:S(2)}) collective-permute-start(bf16[2,288,768]{2,1,0:T(8,128)(2,1)S(1)} %get-tuple-element.116.own_heads), channel_id=1, source_target_pairs={{0,1},{1,0},{2,3},{3,2},{4,5},{5,4},{6,7},{7,6},{8,9},{9,8},{10,11... | collective-permute-start | bytes 2654216 | tf_op jit(solution)/shard_map/ppermute | solution.py:898
  206.7 29.4 %copy-start.42 = (s32[6]{0:T(128)S(1)}, s32[6]{0:T(128)}, u32[]{:S(2)}) copy-start(s32[6]{0:T(128)} %copy-done.41) | copy-start | bytes 76
  206.8 25.7 %collective-permute-start.13 = (bf16[384,1152]{1,0:T(8,128)(2,1)}, bf16[384,1152]{1,0:T(8,128)(2,1)S(1)}, u32[]{:S(2)}, u32[]{:S(2)}) collective-permute-start(bf16[384,1152]{1,0:T(8,128)(2,1)} %get-tuple-element.121), channel_id=1, source_target_pairs={{0,1},{1,0},{2,3},{3,2},{4,5},{5,4},{6,7},{7,6},{8,9},{9,8},{10,11... | collective-permute-start | bytes 2654216 | tf_op jit(solution)/shard_map/ppermute | solution.py:898
  232.5 26.0 %all-to-all-start = ((bf16[4,288,384]{2,1,0:T(8,128)(2,1)}), bf16[4,288,384]{2,1,0:T(8,128)(2,1)S(1)}, u32[]{:S(2)}, u32[]{:S(2)}) async-start(bf16[4,288,384]{2,1,0:T(8,128)(2,1)} %get-tuple-element.141), calls=%async_computation | async-start | bytes 1769472 | tf_op jit(solution)/shard_map/all_to_all | solution.py:901
  248.1 15.7 %collective-permute-start.14 = (bf16[2,288,384]{2,1,0:T(8,128)(2,1)S(1)}, bf16[2,288,384]{2,1,0:T(8,128)(2,1)S(1)}, u32[]{:S(2)}, u32[]{:S(2)}) collective-permute-start(bf16[2,288,384]{2,1,0:T(8,128)(2,1)S(1)} %dynamic-slice_bitcast_fusion.2), channel_id=1, source_target_pairs={{0,1},{1,0},{2,3},{3,2},{4,5},{5,4},{6,7},{7,6},{8,9},{9,8},{10,11... | collective-permute-start | bytes 1327112 | tf_op jit(solution)/shard_map/ppermute | solution.py:898
  258.5 27.2 %all-to-all-start.1 = ((bf16[4,288,384]{2,1,0:T(8,128)(2,1)}), bf16[4,288,384]{2,1,0:T(8,128)(2,1)S(1)}, u32[]{:S(2)}, u32[]{:S(2)}) async-start(bf16[4,288,384]{2,1,0:T(8,128)(2,1)} %get-tuple-element.151), calls=%async_computation.1 | async-start | bytes 1769472 | tf_op jit(solution)/shard_map/all_to_all | solution.py:901
  262.0 109.4 %all-gather.6.cloned.1.call-start = ((), (), s32[]{:S(2)}) async-start(), calls=%async_computation.3 | async-start | bytes 4423680 | tf_op jit(solution)/shard_map/all_gather | solution.py:1101
  268.1 10.6 %copy-start.40 = (bf16[32,1280]{1,0:T(8,128)(2,1)S(1)}, bf16[32,1280]{1,0:T(8,128)(2,1)}, u32[]{:S(2)}) copy-start(bf16[32,1280]{1,0:T(8,128)(2,1)} %copy-done.39) | copy-start | bytes 245764
  268.1 10.7 %copy-start.62 = (bf16[32,1280]{1,0:T(8,128)(2,1)S(1)}, bf16[32,1280]{1,0:T(8,128)(2,1)}, u32[]{:S(2)}) copy-start(bf16[32,1280]{1,0:T(8,128)(2,1)} %get-tuple-element.146) | copy-start | bytes 245764
  268.1 10.7 %copy-start.63 = (bf16[32,1280]{1,0:T(8,128)(2,1)S(1)}, bf16[32,1280]{1,0:T(8,128)(2,1)}, u32[]{:S(2)}) copy-start(bf16[32,1280]{1,0:T(8,128)(2,1)} %get-tuple-element.147) | copy-start | bytes 245764
  268.1 16.2 %copy-start.60 = (bf16[2,32,1280]{2,1,0:T(8,128)(2,1)S(1)}, bf16[2,32,1280]{2,1,0:T(8,128)(2,1)}, u32[]{:S(2)}) copy-start(bf16[2,32,1280]{2,1,0:T(8,128)(2,1)} %get-tuple-element.148) | copy-start | bytes 491524
  268.1 16.2 %copy-start.61 = (bf16[2,32,1280]{2,1,0:T(8,128)(2,1)S(1)}, bf16[2,32,1280]{2,1,0:T(8,128)(2,1)}, u32[]{:S(2)}) copy-start(bf16[2,32,1280]{2,1,0:T(8,128)(2,1)} %get-tuple-element.149) | copy-start | bytes 491524
  279.5 21.7 %collective-permute-start.15 = (bf16[64,1280]{1,0:T(8,128)(2,1)}, bf16[64,1280]{1,0:T(8,128)(2,1)}, u32[]{:S(2)}, u32[]{:S(2)}) collective-permute-start(bf16[64,1280]{1,0:T(8,128)(2,1)} %pad_maximum_fusion.10), channel_id=1, source_target_pairs={{0,1},{1,0},{2,3},{3,2},{4,5},{5,4},{6,7},{7,6},{8,9},{9,8},{10,11... | collective-permute-start | bytes 491528 | tf_op jit(solution)/shard_map/ppermute | solution.py:898
  279.8 22.6 %collective-permute-start.17 = (bf16[64,1280]{1,0:T(8,128)(2,1)}, bf16[64,1280]{1,0:T(8,128)(2,1)}, u32[]{:S(2)}, u32[]{:S(2)}) collective-permute-start(bf16[64,1280]{1,0:T(8,128)(2,1)} %pad_maximum_fusion.10), channel_id=1, source_target_pairs={{0,3},{1,2},{2,1},{3,0},{4,7},{5,6},{6,5},{7,4},{8,11},{9,10},{10,... | collective-permute-start | bytes 491528 | tf_op jit(solution)/shard_map/ppermute | solution.py:898
  286.7 15.7 %collective-permute-start.16 = (bf16[96,1280]{1,0:T(8,128)(2,1)}, bf16[96,1280]{1,0:T(8,128)(2,1)S(1)}, u32[]{:S(2)}, u32[]{:S(2)}) collective-permute-start(bf16[96,1280]{1,0:T(8,128)(2,1)} %pad_maximum_fusion.8), channel_id=1, source_target_pairs={{0,2},{1,3},{2,0},{3,1},{4,6},{5,7},{6,4},{7,5},{8,10},{9,11},{10,... | collective-permute-start | bytes 737288 | tf_op jit(solution)/shard_map/ppermute | solution.py:898
  290.8 10.4 %copy-start.52 = (bf16[32,1280]{1,0:T(8,128)(2,1)S(1)}, bf16[32,1280]{1,0:T(8,128)(2,1)}, u32[]{:S(2)}) copy-start(bf16[32,1280]{1,0:T(8,128)(2,1)} %copy-done.51) | copy-start | bytes 245764
  290.8 10.5 %copy-start.56 = (bf16[16,1280]{1,0:T(8,128)(2,1)S(1)}, bf16[16,1280]{1,0:T(8,128)(2,1)}, u32[]{:S(2)}) copy-start(bf16[16,1280]{1,0:T(8,128)(2,1)} %copy-done.55) | copy-start | bytes 122884
  290.8 10.5 %copy-start.58 = (bf16[16,1280]{1,0:T(8,128)(2,1)S(1)}, bf16[16,1280]{1,0:T(8,128)(2,1)}, u32[]{:S(2)}) copy-start(bf16[16,1280]{1,0:T(8,128)(2,1)} %copy-done.57) | copy-start | bytes 122884
  290.8 11.5 %copy-start.59 = (bf16[32,1280]{1,0:T(8,128)(2,1)S(1)}, bf16[32,1280]{1,0:T(8,128)(2,1)}, u32[]{:S(2)}) copy-start(bf16[32,1280]{1,0:T(8,128)(2,1)} %get-tuple-element.184) | copy-start | bytes 245764
  308.1 16.9 %collective-permute-start.20 = (bf16[48,1280]{1,0:T(8,128)(2,1)S(1)}, bf16[48,1280]{1,0:T(8,128)(2,1)S(1)}, u32[]{:S(2)}, u32[]{:S(2)}) collective-permute-start(bf16[48,1280]{1,0:T(8,128)(2,1)S(1)} %get-tuple-element.161), channel_id=1, source_target_pairs={{0,3},{1,2},{2,1},{3,0},{4,7},{5,6},{6,5},{7,4},{8,11},{9,10},{10,... | collective-permute-start | bytes 368648 | tf_op jit(solution)/shard_map/ppermute | solution.py:898
  311.1 13.8 %collective-permute-start.18 = (bf16[48,1280]{1,0:T(8,128)(2,1)S(1)}, bf16[48,1280]{1,0:T(8,128)(2,1)S(1)}, u32[]{:S(2)}, u32[]{:S(2)}) collective-permute-start(bf16[48,1280]{1,0:T(8,128)(2,1)S(1)} %get-tuple-element.161), channel_id=1, source_target_pairs={{0,1},{1,0},{2,3},{3,2},{4,5},{5,4},{6,7},{7,6},{8,9},{9,8},{10,11... | collective-permute-start | bytes 368648 | tf_op jit(solution)/shard_map/ppermute | solution.py:898
  311.1 13.8 %collective-permute-start.19 = (bf16[64,1280]{1,0:T(8,128)(2,1)S(1)}, bf16[64,1280]{1,0:T(8,128)(2,1)S(1)}, u32[]{:S(2)}, u32[]{:S(2)}) collective-permute-start(bf16[64,1280]{1,0:T(8,128)(2,1)S(1)} %pad_maximum_fusion.11), channel_id=1, source_target_pairs={{0,2},{1,3},{2,0},{3,1},{4,6},{5,7},{6,4},{7,5},{8,10},{9,11},{10,... | collective-permute-start | bytes 491528 | tf_op jit(solution)/shard_map/ppermute | solution.py:898
  325.1 44.3 %all-to-all-start.2 = ((bf16[4,304,768]{2,1,0:T(8,128)(2,1)}), bf16[4,304,768]{2,1,0:T(8,128)(2,1)S(1)}, u32[]{:S(2)}, u32[]{:S(2)}) async-start(bf16[4,304,768]{2,1,0:T(8,128)(2,1)} %norm_back.1), calls=%async_computation.2 | async-start | bytes 3735552 | tf_op jit(solution)/shard_map/all_to_all | solution.py:901
  329.7 17.9 %collective-permute-start.23 = (bf16[2,64,1280]{2,1,0:T(8,128)(2,1)S(1)}, bf16[2,64,1280]{2,1,0:T(8,128)(2,1)S(1)}, u32[]{:S(2)}, u32[]{:S(2)}) collective-permute-start(bf16[2,64,1280]{2,1,0:T(8,128)(2,1)S(1)} %pad_maximum_fusion.7), channel_id=1, source_target_pairs={{0,24},{4,28},{8,16},{12,20},{16,8},{20,12},{24,0},{28,4},{1,25},{... | collective-permute-start | bytes 983048 | tf_op jit(solution)/shard_map/ppermute | solution.py:912
  331.4 20.7 %collective-permute-start.22 = (bf16[2,64,1280]{2,1,0:T(8,128)(2,1)S(1)}, bf16[2,64,1280]{2,1,0:T(8,128)(2,1)S(1)}, u32[]{:S(2)}, u32[]{:S(2)}) collective-permute-start(bf16[2,64,1280]{2,1,0:T(8,128)(2,1)S(1)} %pad_maximum_fusion.7), channel_id=1, source_target_pairs={{0,16},{4,20},{8,24},{12,28},{16,0},{20,4},{24,8},{28,12},{1,17},{... | collective-permute-start | bytes 983048 | tf_op jit(solution)/shard_map/ppermute | solution.py:912
  332.4 19.7 %collective-permute-start.21 = (bf16[2,64,1280]{2,1,0:T(8,128)(2,1)S(1)}, bf16[2,64,1280]{2,1,0:T(8,128)(2,1)S(1)}, u32[]{:S(2)}, u32[]{:S(2)}) collective-permute-start(bf16[2,64,1280]{2,1,0:T(8,128)(2,1)S(1)} %pad_maximum_fusion.7), channel_id=1, source_target_pairs={{0,8},{4,12},{8,0},{12,4},{16,24},{20,28},{24,16},{28,20},{1,9},{5... | collective-permute-start | bytes 983048 | tf_op jit(solution)/shard_map/ppermute | solution.py:912
  353.3 3.4 collective-permute-start.24
  353.4 16.1 %copy-start.14 = (bf16[2,288,768]{2,1,0:T(8,128)(2,1)S(1)}, bf16[2,288,768]{2,1,0:T(8,128)(2,1)}, u32[]{:S(2)}) copy-start(bf16[2,288,768]{2,1,0:T(8,128)(2,1)} %copy-done.13) | copy-start | bytes 2654212
  373.5 7.5 %copy-start.12 = (bf16[4,288,384]{2,1,0:T(8,128)(2,1)S(1)}, bf16[4,288,384]{2,1,0:T(8,128)(2,1)}, u32[]{:S(2)}) copy-start(bf16[4,288,384]{2,1,0:T(8,128)(2,1)} %copy-done.11) | copy-start | bytes 2654212
  373.5 9.2 %copy-start.1 = (bf16[3,8,1152,16]{2,3,1,0:T(8,128)(2,1)S(1)}, bf16[3,8,1152,16]{2,3,1,0:T(8,128)(2,1)}, u32[]{:S(2)}) copy-start(bf16[3,8,1152,16]{2,3,1,0:T(8,128)(2,1)} %param.32) | copy-start | bytes 2654212
  (43 other events, 121.7 us)
Sparse Core Ops, SparseCore 0:
  10.9 85.9 all-gather.7
  141.9 39.7 all-gather.9
  304.4 48.9 all-gather.5

commit v4 on v3

--- a/solution.py
+++ b/solution.py
@@ -986,13 +986,13 @@
     merge_all = lax.all_gather(merge_piece, ("tensor", "dp")).reshape(parts, merge_rows * copies, dim)
     late_w = after(my_w, ready)
     pieces = [jump(late_w, -k, 0) for k in range(1, slots)]
-    own_expand = jnp.pad(after(expand_weight.T, ready), extra)
-    own_reduce = jnp.pad(after(reduce_weight, ready), extra)
+    own_expand = jnp.pad(expand_weight.T, extra)
+    own_reduce = jnp.pad(reduce_weight, extra)
 
     down = jnp.pad(at(triple_down, index, 1).transpose(0, 2, 1).reshape(48, dim), ((0, 16), (0, 0)))
     norm = jnp.pad(jnp.stack([first_gain, first_shift], 1).astype(F32), ((0, 0), (0, 6)))
 
-    late_index = after(adapter_index, ready)
+    late_index = adapter_index
 
     def factor_pack(which):
         def lanes(x):
@@ -1003,7 +1003,7 @@
         )
 
     packs = [factor_pack(at(late_index, (mine - k) % slots)) for k in range(slots)]
-    late = after(index, ready)
+    late = index
     tab = jnp.stack(
         [
             jnp.pad(x, ((0, LANES - 16), (0, 0)))
@@ -1016,7 +1016,7 @@
 
     merge_lines = [at(merge_down, late_index[n]).T for n in range(slots)]
     merge_lines = jnp.pad(jnp.stack(merge_lines), ((0, 0), (0, 0), (0, span - width)))
-    cot_parts = jnp.concatenate([images_of(after(cotangent, ready)), merge_lines], 1)
+    cot_parts = jnp.concatenate([images_of(after(cotangent, adapter_index)), merge_lines], 1)
 
     def trade(x):
         return x, [jump(at(x, (member + g) % groups), 0, g) for g in range(1, groups)]
@@ -1025,18 +1025,18 @@
     qkv, n1, stats, inner, rows, upx = project(
         shape, seq, begin, norm, down, ups, images, toks, flat_triple, foreign
     )
+    own_cot = after(at(cot_parts, mine), ready)
+    cots = {(0, g): jump(own_cot, 0, g) for g in range(1, groups)}
+    pieces, cot_parts, packs = lax.optimization_barrier((pieces, cot_parts, packs, stats))[:3]
+    begin = after(scalars, cot_parts, *pieces)
+    cots.update({(k, 0): jump(at(cot_parts, (mine + k) % slots), k, 0) for k in range(1, slots)})
     fac = [packs[0]] + [jump(packs[k], -k, 0) for k in range(1, slots)]
-    cots = {(k, 0): jump(at(cot_parts, (mine + k) % slots), k, 0) for k in range(1, slots)}
-    own_cot = at(cot_parts, mine)
-    cots.update({(0, g): jump(own_cot, 0, g) for g in range(1, groups)})
-    pieces, cots = lax.optimization_barrier((pieces, cots, stats))[:2]
     pieces = [lax.all_gather(x, "dp") for x in pieces]
-    begin = after(scalars, *cots.values())
-    cots.update({(k, g): jump(cots[k, 0], 0, g) for k in range(1, slots) for g in range(1, groups)})
     lse, heads = attend(shape, begin, qkv)
-    heads, cots, fac = lax.optimization_barrier((heads, cots, fac))
+    cots, fac = lax.optimization_barrier((cots, fac, lse))[:2]
     heads = (heads, [jump(heads, 0, g) for g in range(1, groups)])
     fac = jnp.stack(fac)
+    cots.update({(k, g): jump(cots[k, 0], 0, g) for k in range(1, slots) for g in range(1, groups)})
     cots = [cots[pair] for pair in shape.pairs[1:]]
     layers, near, gms, gws = [None] * groups, [], [], []
     for turn in list(range(1, groups)) + [0]:
@@ -1115,7 +1115,7 @@
         ((3, adapters, 16, dim), (3, adapters, 16, head_rows)),
         "triple_terms",
     )
-    tokens_grad = tokens_result(shape, seq, after(images, downs), last).T
+    tokens_grad = tokens_result(shape, seq, after(images, downs, merge_up_grad, layer_out), last).T
 
     return (
         layer_out,

time: 396 us -> 390 us (0.985)
  starting transfers between devices: 45.2 us -> 49.9 us
  other arithmetic: 21.3 us -> 16.8 us
    ppermute x18, starting transfers between devices: 26.2 us -> 31.1 us  [jump(): return lax.ppermute(x, 'tensor', perm)]
    unnamed x156 -> x166, local copies, waits for them, and re-layouts: 27.8 us -> 27.8 us
  transfers between devices with their start and end apart: 31 -> 31, of which waited for: 11 -> 12; matrix products, arithmetic and copies ran while one was open for 11% -> 10% of each run, Pallas kernels for 27% -> 29%
where the time goes in v4:
time: 390 us; the launch traced here: 384 us
  Pallas kernels  139 us (36%)
  waiting for transfers between devices  102 us (26%)
  local copies, waits for them, and re-layouts  52.5 us (13%)
  starting transfers between devices  49.9 us (13%)
  between operations  25.1 us (6%)
  other arithmetic  16.8 us (4%)
    ppermute x18, waiting for transfers between devices, jump(): return lax.ppermute(x, 'tensor', perm)  67.2 us
    pallas_call x2, Pallas kernels, hidden_part(): pl.pallas_call(partial(hidden_kernel, shape, turn), out_shape=out, in_spe...  49 us
    ppermute x18, starting transfers between devices, jump(): return lax.ppermute(x, 'tensor', perm)  31.1 us
    unnamed x166, local copies, waits for them, and re-layouts  27.8 us
    ppermute x7, waiting for transfers between devices, cross(): return lax.ppermute(x, 'dp', [(d, d ^ bit) for d in range(copies)])  25.5 us
    pallas_call x2, Pallas kernels, heads_back(): pl.pallas_call(partial(heads_back_kernel, shape, slot), grid=(heads_here,...  21 us
    pallas_call x1, Pallas kernels, project(): pl.pallas_call(partial(project_kernel, shape, seq), out_shape=out, in_spe...  15.7 us
    pallas_call x1, Pallas kernels, attend(): pl.pallas_call(partial(attend_kernel, slots), grid=(heads,), out_shape=ou...  14.5 us
  transfers between devices with their start and end apart: 31, of which 12 were waited for; matrix products, arithmetic and copies ran while one was open for 10% of the time, Pallas kernels for 29%

profile of v4, /device:TPU:0, one launch (start us, length us, event | category | flops | bytes accessed | tf_op | source)
XLA Modules:
  0.0 384.4 jit_solution(6716158841316428981)
XLA Ops:
  7.3 1.7 pad_dynamic-slice_fusion.5
  9.1 1.2 slice.75
  11.2 1.2 fusion.4
  19.8 4.0 %collective-permute-start.1 = (bf16[144,1152]{1,0:T(8,128)(2,1)}, bf16[144,1152]{1,0:T(8,128)(2,1)}, u32[]{:S(2)}, u32[]{:S(2)}) collective-permute-start(bf16[144,1152]{1,0:T(8,128)(2,1)} %fusion.7), channel_id=1, source_target_pairs={{0,2},{1,3},{2,0},{3,1},{4,6},{5,7},{6,4},{7,5},{8,10},{9,11},{10,... | collective-permute-start | bytes 995336 | tf_op jit(solution)/shard_map/ppermute | solution.py:898
  23.9 1.9 collective-permute-start.5
  29.8 1.2 slice.77
  39.4 12.4 %collective-permute-done.1 = bf16[144,1152]{1,0:T(8,128)(2,1)} collective-permute-done((bf16[144,1152]{1,0:T(8,128)(2,1)}, bf16[144,1152]{1,0:T(8,128)(2,1)}, u32[]{:S(2)}, u32[]{:S(2)}) %collective-permute-start.1) | collective-permute-done | bytes 331808 | tf_op jit(solution)/shard_map/ppermute | solution.py:898
  52.8 1.9 collective-permute-start.6
  54.7 1.0 pad_maximum_fusion.4.tab_ref
  55.7 5.3 %collective-permute-done.6 = bf16[1,112,1152]{2,1,0:T(8,128)(2,1)S(1)} collective-permute-done((bf16[1,112,1152]{2,1,0:T(8,128)(2,1)S(1)}, bf16[1,112,1152]{2,1,0:T(8,128)(2,1)S(1)}, u32[]{:S(2)}, u32[]{:S(2)}) %collective-permute-start.6) | collective-permute-done | bytes 258080 | tf_op jit(solution)/shard_map/ppermute | solution.py:912
  61.8 1.2 collective-permute-start.7
  64.8 3.5 pad.103.own_expand
  68.3 1.7 pad.104.own_reduce
  70.0 1.3 stack.123.sc
  72.4 1.1 collective-permute-start.2
  73.5 1.2 pad_maximum_fusion.2.rest_3_.rest_0_
  74.9 1.8 dynamic-slice_select_fusion
  76.7 15.6 %collective-permute-done.2.rest_2_ = bf16[288,768]{1,0:T(8,128)(2,1)S(1)} collective-permute-done((bf16[288,768]{1,0:T(8,128)(2,1)S(1)}, bf16[288,768]{1,0:T(8,128)(2,1)S(1)}, u32[]{:S(2)}, u32[]{:S(2)}) %collective-permute-start.2) | collective-permute-done | bytes 442400 | tf_op jit(solution)/shard_map/ppermute | solution.py:898
  92.3 3.4 collective-permute-start.4
  96.7 15.7 %project.1 = (bf16[3,8,80,768]{3,2,1,0:T(8,128)(2,1)}, bf16[1152,768]{1,0:T(8,128)(2,1)}, f32[8,768]{1,0:T(8,128)S(1)}, bf16[64,768]{1,0:T(8,128)(2,1)S(1)}, bf1...) custom-call(s32[6]{0:T(128)S(1)} %stack.123.sc, f32[1152,8]{1,0:T(8,128)S(1)} %pad_convert_fusion.norm_ref, ...), custom_call_target="tpu_custom_call" | custom-call | flops 4000000000 | bytes 40000000 | tf_op jit(solution)/shard_map/project/pallas_call | solution.py:194
  114.4 7.9 %collective-permute-done.4 = bf16[272,1152]{1,0:T(8,128)(2,1)S(1)} collective-permute-done((bf16[272,1152]{1,0:T(8,128)(2,1)S(1)}, bf16[272,1152]{1,0:T(8,128)(2,1)S(1)}, u32[]{:S(2)}, u32[]{:S(2)}) %collective-permute-start.4) | collective-permute-done | bytes 626720 | tf_op jit(solution)/shard_map/ppermute | solution.py:898
  124.1 3.4 collective-permute-start.9
  127.5 1.8 copy-done.2
  129.4 14.5 %attend.1 = (f32[8,1,768]{2,1,0:T(1,128)S(1)}, bf16[2,288,768]{2,1,0:T(8,128)(2,1)S(1)}) custom-call(s32[6]{0:T(128)S(1)} %stack.123.sc, bf16[3,8,80,768]{3,2,1,0:T(8,128)(2,1)S(1)} %copy-done.2), custom_call_target="tpu_custom_call" | custom-call | flops 4000000000 | bytes 60000000 | tf_op jit(solution)/shard_map/attend/pallas_call | solution.py:242
  145.4 20.4 %collective-permute-done.10 = bf16[48,1088]{1,0:T(8,128)(2,1)S(1)} collective-permute-done((bf16[48,1088]{1,0:T(8,128)(2,1)S(1)}, bf16[48,1088]{1,0:T(8,128)(2,1)S(1)}, u32[]{:S(2)}, u32[]{:S(2)}) %collective-permute-start.10) | collective-permute-done | bytes 104480 | tf_op jit(solution)/shard_map/ppermute | solution.py:898
  165.7 4.0 %collective-permute-start.11 = (bf16[304,768]{1,0:T(8,128)(2,1)S(1)}, bf16[304,768]{1,0:T(8,128)(2,1)S(1)}, u32[]{:S(2)}, u32[]{:S(2)}) collective-permute-start(bf16[304,768]{1,0:T(8,128)(2,1)S(1)} %collective-permute-done.9.rest_1_), channel_id=1, source_target_pairs={{0,1},{1,0},{2,3},{3,2},{4,5},{5,4},{6,7},{7,6},{8,9},{9,8},{10,11... | collective-permute-start | bytes 1400840 | tf_op jit(solution)/shard_map/ppermute | solution.py:898
  171.4 8.7 %collective-permute-done.11.rest_2_ = bf16[304,768]{1,0:T(8,128)(2,1)S(1)} collective-permute-done((bf16[304,768]{1,0:T(8,128)(2,1)S(1)}, bf16[304,768]{1,0:T(8,128)(2,1)S(1)}, u32[]{:S(2)}, u32[]{:S(2)}) %collective-permute-start.11) | collective-permute-done | bytes 466976 | tf_op jit(solution)/shard_map/ppermute | solution.py:898
  180.8 23.7 %hidden_part.2 = (bf16[4,288,384]{2,1,0:T(8,128)(2,1)}, bf16[384,1152]{1,0:T(8,128)(2,1)}, bf16[2,32,1280]{2,1,0:T(8,128)(2,1)}, bf16[32,1280]{1,0:T(8,128)(2,1)}) custom-call(s32[6]{0:T(128)} %copy-done.39, f32[8,1152]{1,0:T(8,128)} %fusion.31.vec_ref, bf16[3,128,1152]{2,1,0:T(8,128)(2,1)} %pad_maximum_fusion.4.tab_ref, ...), custom_call_target="tpu_custom_call" | custom-call | flops 10000000000 | bytes 60000000 | tf_op jit(solution)/shard_map/hidden_part/pallas_call | solution.py:452
  204.5 1.8 collective-permute-start.13
  206.3 25.3 %hidden_part.3 = (bf16[4,288,384]{2,1,0:T(8,128)(2,1)}, f32[384,1152]{1,0:T(8,128)}, bf16[2,32,1280]{2,1,0:T(8,128)(2,1)}, bf16[32,1280]{1,0:T(8,128)(2,1)}, f32...) custom-call(s32[6]{0:T(128)} %copy-done.39, ...), custom_call_target="tpu_custom_call" | custom-call | flops 10000000000 | bytes 60000000 | tf_op jit(solution)/shard_map/hidden_part/pallas_call | solution.py:452
  231.6 3.6 all-to-all-start
  235.3 1.2 copy-done.25
  236.5 1.2 copy-done.26
  240.3 6.3 %branch_part.1 = (f32[1152,384]{1,0:T(8,128)}, bf16[2,2,288,384]{3,2,1,0:T(8,128)(2,1)S(1)}, bf16[32,1280]{1,0:T(8,128)(2,1)S(1)}) custom-call(s32[6]{0:T(128)S(1)} %copy-done.40, f32[8,1152]{1,0:T(8,128)S(1)} %copy-done.30, bf16[3,128,1152]{2,1,0:T(8,128)(2,1)S(1)} %copy-done.8, bf16[4,384,1152]{2,1,0:T(8,128)(2,1)} %bitcast.128, ...), custom_call_target="tpu_custom_call" | custom-call | flops 2000000000 | bytes 10000000 | tf_op jit(solution)/shard_map/branch_part/pallas_call | solution.py:532
  247.2 1.9 collective-permute-start.14
  249.2 7.2 %all-to-all-done.rest_1_ = bf16[4,288,384]{2,1,0:T(8,128)(2,1)S(1)} async-done(((bf16[4,288,384]{2,1,0:T(8,128)(2,1)}), bf16[4,288,384]{2,1,0:T(8,128)(2,1)S(1)}, u32[]{:S(2)}, u32[]{:S(2)}) %all-to-all-start) | async-done | bytes 884768 | tf_op jit(solution)/shard_map/all_to_all | solution.py:901
  256.3 3.5 all-to-all-start.1
  259.9 2.3 collective-permute-done.14.rest_0_
  262.9 1.8 copy-done.3
  264.8 1.0 copy-done.18
  266.5 10.6 %heads_back.2.rest_0_.rest_2_ = bf16[864,768]{1,0:T(8,128)(2,1)S(1)} custom-call(s32[6]{0:T(128)S(1)} %copy-done.40, bf16[3,8,80,768]{3,2,1,0:T(8,128)(2,1)S(1)} %copy-done.3, f32[8,1,768]{2,1,0:T(1,128)S(1)} %copy-done.33, bf16[2,2,288,384]{3,2,1,0:T(8,128)(2,1)S(1)} %get-tuple-element.136.own_dout, bf16[2,288,384]{2,1,0:T(8,128)(2,1)S(1)} %copy-done.18), custom_call_target="tpu_custom_call" | custom-call | flops 1000000000 | bytes 40000000 | tf_op jit(solution)/shard_map/heads_back/pallas_call | solution.py:610
  277.9 3.3 collective-permute-start.17
  282.7 1.6 all-to-all-done.1.rest_0_
  285.2 1.8 copy-done.4
  287.0 1.0 copy-done.19
  288.8 10.4 %heads_back.3.rest_1_.rest_3_ = bf16[864,768]{1,0:T(8,128)(2,1)S(1)} custom-call(s32[6]{0:T(128)S(1)} %copy-done.40, bf16[3,8,80,768]{3,2,1,0:T(8,128)(2,1)S(1)} %copy-done.4, f32[8,1,768]{2,1,0:T(1,128)S(1)} %copy-done.34, bf16[2,2,288,384]{3,2,1,0:T(8,128)(2,1)S(1)} %get-tuple-element.136.own_dout, bf16[2,288,384]{2,1,0:T(8,128)(2,1)S(1)} %copy-done.19), custom_call_target="tpu_custom_call" | custom-call | flops 1000000000 | bytes 40000000 | tf_op jit(solution)/shard_map/heads_back/pallas_call | solution.py:610
  299.2 1.1 add_convert_fusion.2
  302.2 1.5 copy-done.20
  303.7 2.3 rank_back.1
  306.1 2.0 collective-permute-start.20
  308.0 1.6 collective-permute-start.18
  310.6 12.2 %norm_back.1 = bf16[4,304,768]{2,1,0:T(8,128)(2,1)} custom-call(s32[6]{0:T(128)S(1)} %copy-done.40, f32[1152,8]{1,0:T(8,128)S(1)} %copy-done.16, bf16[64,1152]{1,0:T(8,128)(2,1)S(1)} %copy-done.22, bf16[64,768]{1,0:T(8,128)(2,1)S(1)} %get-tuple-element.151.thr_ref, f32[8,768]{1,0:T(8,128)S(1)} %copy-done.42, ...), custom_call_target="tpu_custom_call" | custom-call | flops 1000000000 | bytes 40000000 | tf_op jit(solution)/shard_map/norm_back/pallas_call | solution.py:725
  323.1 4.7 %all-to-all-start.2 = ((bf16[4,304,768]{2,1,0:T(8,128)(2,1)}), bf16[4,304,768]{2,1,0:T(8,128)(2,1)}, u32[]{:S(2)}, u32[]{:S(2)}) async-start(bf16[4,304,768]{2,1,0:T(8,128)(2,1)} %norm_back.1), calls=%async_computation.2 | async-start | bytes 3735552 | tf_op jit(solution)/shard_map/all_to_all | solution.py:901
  327.8 2.0 collective-permute-start.23
  331.3 14.1 %collective-permute-done.23 = bf16[2,64,1280]{2,1,0:T(8,128)(2,1)S(1)} collective-permute-done((bf16[2,64,1280]{2,1,0:T(8,128)(2,1)S(1)}, bf16[2,64,1280]{2,1,0:T(8,128)(2,1)S(1)}, u32[]{:S(2)}, u32[]{:S(2)}) %collective-permute-start.23) | collective-permute-done | bytes 327712 | tf_op jit(solution)/shard_map/ppermute | solution.py:912
  345.5 4.7 %collective-permute-done.22 = bf16[2,64,1280]{2,1,0:T(8,128)(2,1)S(1)} collective-permute-done((bf16[2,64,1280]{2,1,0:T(8,128)(2,1)S(1)}, bf16[2,64,1280]{2,1,0:T(8,128)(2,1)S(1)}, u32[]{:S(2)}, u32[]{:S(2)}) %collective-permute-start.22) | collective-permute-done | bytes 327712 | tf_op jit(solution)/shard_map/ppermute | solution.py:912
  350.9 1.2 pad_maximum_fusion
  354.2 1.3 collective-permute-done.24
  355.5 1.4 constant_dynamic-update-slice_fusion.terms_ref
  356.9 5.6 %triple_terms.1 = (f32[3,8,16,1152]{3,2,1,0:T(8,128)}, f32[3,8,16,288]{3,2,1,0:T(8,128)}) custom-call(bf16[16,64,1280]{2,1,0:T(8,128)(2,1)S(1)} %constant_dynamic-update-slice_fusion.terms_ref), custom_call_target="tpu_custom_call" | custom-call | flops 100000 | bytes 100000 | tf_op jit(solution)/shard_map/triple_terms/pallas_call | solution.py:836
  362.6 2.1 copy-done.7
  364.7 6.7 %block_terms.1 = (f32[8,16,1152]{2,1,0:T(8,128)}, f32[8,16,1152]{2,1,0:T(8,128)}, f32[8,16,1152]{2,1,0:T(8,128)}, f32[8,16,1076]{2,1,0:T(8,128)}, f32[8,16,1076]{2,1,0:T(8,128)}, /*index=5*/f32[8,16,1152]{2,1,0:T(8,128)S(1)}) custom-call(bf16[16,96,1280]{2,1,0:T(8,128)(2,1)S(1)} %copy-done.7), custom_call_target="tpu_custom_call" | custom-call | flops 100000 | bytes 100000 | tf_op jit(solution)/shard_map/block_terms/pallas_call | solution.py:836
  371.4 1.7 layer_result.1
  373.9 3.5 tokens_result.1
  (262 shorter events, 40.7 us)
Async XLA Ops:
  7.2 31.3 %copy-start = (bf16[3,8,1152,16]{2,3,1,0:T(8,128)(2,1)S(1)}, bf16[3,8,1152,16]{2,3,1,0:T(8,128)(2,1)}, u32[]{:S(2)}) copy-start(bf16[3,8,1152,16]{2,3,1,0:T(8,128)(2,1)} %param.32) | copy-start | bytes 2654212
  7.2 172.8 %all-gather.8.cloned.1.call-start = ((), (), s32[]{:S(2)}) async-start(), calls=%async_computation.4 | async-start | bytes 3649536 | tf_op jit(solution)/shard_map/all_gather | solution.py:986
  9.0 171.1 %all-gather.10.cloned.1.call-start = ((), (), s32[]{:S(2)}) async-start(), calls=%async_computation.5 | async-start | bytes 5640192 | tf_op jit(solution)/shard_map/all_gather | solution.py:1034
  12.4 17.3 %copy-start.67 = (bf16[1152]{0:T(1024)(128)(2,1)S(1)}, bf16[1152]{0:T(1024)(128)(2,1)}, u32[]{:S(2)}) copy-start(bf16[1152]{0:T(1024)(128)(2,1)} %param.28) | copy-start | bytes 6916
  12.4 17.3 %copy-start.68 = (bf16[1152]{0:T(1024)(128)(2,1)S(1)}, bf16[1152]{0:T(1024)(128)(2,1)}, u32[]{:S(2)}) copy-start(bf16[1152]{0:T(1024)(128)(2,1)} %param.29) | copy-start | bytes 6916
  12.4 17.3 %copy-start.69 = (bf16[1152]{0:T(1024)(128)(2,1)S(1)}, bf16[1152]{0:T(1024)(128)(2,1)}, u32[]{:S(2)}) copy-start(bf16[1152]{0:T(1024)(128)(2,1)} %param.35) | copy-start | bytes 6916
  12.4 17.3 %copy-start.70 = (bf16[1152]{0:T(1024)(128)(2,1)S(1)}, bf16[1152]{0:T(1024)(128)(2,1)}, u32[]{:S(2)}) copy-start(bf16[1152]{0:T(1024)(128)(2,1)} %param.38) | copy-start | bytes 6916
  12.4 17.4 %copy-start.71 = (bf16[1152]{0:T(1024)(128)(2,1)S(1)}, bf16[1152]{0:T(1024)(128)(2,1)}, u32[]{:S(2)}) copy-start(bf16[1152]{0:T(1024)(128)(2,1)} %param.39) | copy-start | bytes 6916
  12.4 17.4 %copy-start.72 = (bf16[1076]{0:T(1024)(128)(2,1)S(1)}, bf16[1076]{0:T(1024)(128)(2,1)}, u32[]{:S(2)}) copy-start(bf16[1076]{0:T(1024)(128)(2,1)} %param.41) | copy-start | bytes 6460
  12.4 17.4 %copy-start.73 = (bf16[1152]{0:T(1024)(128)(2,1)S(1)}, bf16[1152]{0:T(1024)(128)(2,1)}, u32[]{:S(2)}) copy-start(bf16[1152]{0:T(1024)(128)(2,1)} %param.45) | copy-start | bytes 6916
  19.8 31.9 %collective-permute-start.1 = (bf16[144,1152]{1,0:T(8,128)(2,1)}, bf16[144,1152]{1,0:T(8,128)(2,1)}, u32[]{:S(2)}, u32[]{:S(2)}) collective-permute-start(bf16[144,1152]{1,0:T(8,128)(2,1)} %fusion.7), channel_id=1, source_target_pairs={{0,2},{1,3},{2,0},{3,1},{4,6},{5,7},{6,4},{7,5},{8,10},{9,11},{10,... | collective-permute-start | bytes 995336 | tf_op jit(solution)/shard_map/ppermute | solution.py:898
  23.9 48.5 %collective-permute-start = (bf16[288,768]{1,0:T(8,128)(2,1)}, bf16[288,768]{1,0:T(8,128)(2,1)S(1)}, u32[]{:S(2)}, u32[]{:S(2)}) collective-permute-start(bf16[288,768]{1,0:T(8,128)(2,1)} %get-tuple-element.91), channel_id=1, source_target_pairs={{0,2},{1,3},{2,0},{3,1},{4,6},{5,7},{6,4},{7,5},{8,10},{9,11},{10,... | collective-permute-start | bytes 1327112 | tf_op jit(solution)/shard_map/ppermute | solution.py:898
  23.9 72.8 %collective-permute-start.5 = (bf16[288,768]{1,0:T(8,128)(2,1)}, bf16[288,768]{1,0:T(8,128)(2,1)S(1)}, u32[]{:S(2)}, u32[]{:S(2)}) collective-permute-start(bf16[288,768]{1,0:T(8,128)(2,1)} %get-tuple-element.99), channel_id=1, source_target_pairs={{0,1},{1,0},{2,3},{3,2},{4,5},{5,4},{6,7},{7,6},{8,9},{9,8},{10,11... | collective-permute-start | bytes 1327112 | tf_op jit(solution)/shard_map/ppermute | solution.py:898
  29.8 9.6 %copy-start.74 = (pred[768]{0:T(1024)(128)(4,1)S(1)}, pred[768]{0:T(1024)(128)(4,1)}, u32[]{:S(2)}) copy-start(pred[768]{0:T(1024)(128)(4,1)} %constant.145.clone.1) | copy-start | bytes 2308
  52.7 11.4 %copy-start.80 = (s32[2]{0:T(128)S(1)}, s32[2]{0:T(128)}, u32[]{:S(2)}) copy-start(s32[2]{0:T(128)} %param.27) | copy-start | bytes 28
  52.8 8.2 %collective-permute-start.6 = (bf16[1,112,1152]{2,1,0:T(8,128)(2,1)S(1)}, bf16[1,112,1152]{2,1,0:T(8,128)(2,1)S(1)}, u32[]{:S(2)}, u32[]{:S(2)}) collective-permute-start(bf16[1,112,1152]{2,1,0:T(8,128)(2,1)S(1)} %slice_bitcast_fusion), channel_id=1, source_target_pairs={{0,16},{4,20},{8,24},{12,28},{16,0},{20,4},{24,8},{28,12},{1,17},{... | collective-permute-start | bytes 774152 | tf_op jit(solution)/shard_map/ppermute | solution.py:912
  61.8 11.6 %collective-permute-start.7 = (bf16[2,112,1152]{2,1,0:T(8,128)(2,1)}, bf16[2,112,1152]{2,1,0:T(8,128)(2,1)}, u32[]{:S(2)}, u32[]{:S(2)}) collective-permute-start(bf16[2,112,1152]{2,1,0:T(8,128)(2,1)} %pad_maximum_fusion.5), channel_id=1, source_target_pairs={{0,8},{4,12},{8,0},{12,4},{16,24},{20,28},{24,16},{28,20},{1,9},{5... | collective-permute-start | bytes 1548296 | tf_op jit(solution)/shard_map/ppermute | solution.py:912
  63.2 60.9 %copy-start.46 = (bf16[2,304,768]{2,1,0:T(8,128)(2,1)}, bf16[2,304,768]{2,1,0:T(8,128)(2,1)S(1)}, u32[]{:S(2)}) copy-start(bf16[2,304,768]{2,1,0:T(8,128)(2,1)S(1)} %pad_maximum_fusion.3.own_cot) | copy-start | bytes 2801668
  64.8 31.9 %copy-start.21 = (bf16[64,1152]{1,0:T(8,128)(2,1)}, bf16[64,1152]{1,0:T(8,128)(2,1)S(1)}, u32[]{:S(2)}) copy-start(bf16[64,1152]{1,0:T(8,128)(2,1)S(1)} %pad.112.down_ref) | copy-start | bytes 442372
  71.3 56.2 %copy-start.39 = (s32[6]{0:T(128)}, s32[6]{0:T(128)S(1)}, u32[]{:S(2)}) copy-start(s32[6]{0:T(128)S(1)} %stack.123.sc) | copy-start | bytes 76
  72.3 24.4 %copy-start.15 = (f32[1152,8]{1,0:T(8,128)}, f32[1152,8]{1,0:T(8,128)S(1)}, u32[]{:S(2)}) copy-start(f32[1152,8]{1,0:T(8,128)S(1)} %pad_convert_fusion.norm_ref) | copy-start | bytes 110596
  72.4 20.0 %collective-permute-start.2 = (bf16[288,768]{1,0:T(8,128)(2,1)S(1)}, bf16[288,768]{1,0:T(8,128)(2,1)S(1)}, u32[]{:S(2)}, u32[]{:S(2)}) collective-permute-start(bf16[288,768]{1,0:T(8,128)(2,1)S(1)} %collective-permute-done.rest_1_), channel_id=1, source_target_pairs={{0,1},{1,0},{2,3},{3,2},{4,5},{5,4},{6,7},{7,6},{8,9},{9,8},{10,11... | collective-permute-start | bytes 1327112 | tf_op jit(solution)/shard_map/ppermute | solution.py:898
  74.7 22.0 %copy-start.5 = (bf16[4,112,1152]{2,1,0:T(8,128)(2,1)}, bf16[4,112,1152]{2,1,0:T(8,128)(2,1)S(1)}, u32[]{:S(2)}) copy-start(bf16[4,112,1152]{2,1,0:T(8,128)(2,1)S(1)} %pad_maximum_fusion.2.rest_3_.rest_0_) | copy-start | bytes 3096580
  74.7 22.0 %collective-permute-start.8 = (bf16[4,112,1152]{2,1,0:T(8,128)(2,1)S(1)}, bf16[4,112,1152]{2,1,0:T(8,128)(2,1)S(1)}, u32[]{:S(2)}, u32[]{:S(2)}) collective-permute-start(bf16[4,112,1152]{2,1,0:T(8,128)(2,1)S(1)} %pad_maximum_fusion.2.rest_3_.rest_0_), channel_id=1, source_target_pairs={{0,4},{4,0},{8,12},{12,8},{16,20},{20,16},{24,28},{28,24},{1,5},{5... | collective-permute-start | bytes 3096584 | tf_op jit(solution)/shard_map/ppermute | solution.py:912
  74.9 21.8 %copy-start.13 = (bf16[2,288,768]{2,1,0:T(8,128)(2,1)}, bf16[2,288,768]{2,1,0:T(8,128)(2,1)S(1)}, u32[]{:S(2)}) copy-start(bf16[2,288,768]{2,1,0:T(8,128)(2,1)S(1)} %pad_maximum_fusion.1.own_tok.img_ref) | copy-start | bytes 2654212
  92.3 30.0 %collective-permute-start.4 = (bf16[272,1152]{1,0:T(8,128)(2,1)S(1)}, bf16[272,1152]{1,0:T(8,128)(2,1)S(1)}, u32[]{:S(2)}, u32[]{:S(2)}) collective-permute-start(bf16[272,1152]{1,0:T(8,128)(2,1)S(1)} %dynamic-slice_select_fusion), channel_id=1, source_target_pairs={{0,2},{1,3},{2,0},{3,1},{4,6},{5,7},{6,4},{7,5},{8,10},{9,11},{10,... | collective-permute-start | bytes 1880072 | tf_op jit(solution)/shard_map/ppermute | solution.py:898
  96.7 15.8 %copy-start.23 = (bf16[4,112,1152]{2,1,0:T(8,128)(2,1)}, bf16[4,112,1152]{2,1,0:T(8,128)(2,1)S(1)}, u32[]{:S(2)}) copy-start(bf16[4,112,1152]{2,1,0:T(8,128)(2,1)S(1)} %collective-permute-done.8.rest_4_.rest_1_) | copy-start | bytes 3096580
  123.3 22.1 %collective-permute-start.3 = (bf16[304,768]{1,0:T(8,128)(2,1)S(1)}, bf16[304,768]{1,0:T(8,128)(2,1)S(1)}, u32[]{:S(2)}, u32[]{:S(2)}) collective-permute-start(bf16[304,768]{1,0:T(8,128)(2,1)S(1)} %dynamic-slice_bitcast_fusion.1), channel_id=1, source_target_pairs={{0,1},{1,0},{2,3},{3,2},{4,5},{5,4},{6,7},{7,6},{8,9},{9,8},{10,11... | collective-permute-start | bytes 1400840 | tf_op jit(solution)/shard_map/ppermute | solution.py:898
  124.1 41.6 %collective-permute-start.9 = (bf16[304,768]{1,0:T(8,128)(2,1)S(1)}, bf16[304,768]{1,0:T(8,128)(2,1)S(1)}, u32[]{:S(2)}, u32[]{:S(2)}) collective-permute-start(bf16[304,768]{1,0:T(8,128)(2,1)S(1)} %dynamic-slice_bitcast_fusion), channel_id=1, source_target_pairs={{0,2},{1,3},{2,0},{3,1},{4,6},{5,7},{6,4},{7,5},{8,10},{9,11},{10,... | collective-permute-start | bytes 1400840 | tf_op jit(solution)/shard_map/ppermute | solution.py:898
  129.4 15.2 %copy-start.63 = (bf16[48,1088]{1,0:T(8,128)(2,1)S(1)}, bf16[48,1088]{1,0:T(8,128)(2,1)}, u32[]{:S(2)}) copy-start(bf16[48,1088]{1,0:T(8,128)(2,1)} %get-tuple-element.103) | copy-start | bytes 313348
  129.4 40.3 %copy-start.59 = (bf16[48,1088]{1,0:T(8,128)(2,1)S(1)}, bf16[48,1088]{1,0:T(8,128)(2,1)}, u32[]{:S(2)}) copy-start(bf16[48,1088]{1,0:T(8,128)(2,1)} %get-tuple-element.108) | copy-start | bytes 313348
  144.5 35.5 %copy-start.43 = (bf16[2,288,768]{2,1,0:T(8,128)(2,1)}, bf16[2,288,768]{2,1,0:T(8,128)(2,1)S(1)}, u32[]{:S(2)}) copy-start(bf16[2,288,768]{2,1,0:T(8,128)(2,1)S(1)} %get-tuple-element.111.own_heads) | copy-start | bytes 2654212
  144.5 25.9 %collective-permute-start.12 = (bf16[2,288,768]{2,1,0:T(8,128)(2,1)S(1)}, bf16[2,288,768]{2,1,0:T(8,128)(2,1)S(1)}, u32[]{:S(2)}, u32[]{:S(2)}) collective-permute-start(bf16[2,288,768]{2,1,0:T(8,128)(2,1)S(1)} %get-tuple-element.111.own_heads), channel_id=1, source_target_pairs={{0,1},{1,0},{2,3},{3,2},{4,5},{5,4},{6,7},{7,6},{8,9},{9,8},{10,11... | collective-permute-start | bytes 2654216 | tf_op jit(solution)/shard_map/ppermute | solution.py:898
  144.5 21.2 %collective-permute-start.10 = (bf16[48,1088]{1,0:T(8,128)(2,1)S(1)}, bf16[48,1088]{1,0:T(8,128)(2,1)S(1)}, u32[]{:S(2)}, u32[]{:S(2)}) collective-permute-start(bf16[48,1088]{1,0:T(8,128)(2,1)S(1)} %copy-done.63), channel_id=1, source_target_pairs={{0,2},{1,3},{2,0},{3,1},{4,6},{5,7},{6,4},{7,5},{8,10},{9,11},{10,... | collective-permute-start | bytes 313352 | tf_op jit(solution)/shard_map/ppermute | solution.py:898
  145.4 25.1 %copy-start.77 = (bf16[304,768]{1,0:T(8,128)(2,1)}, bf16[304,768]{1,0:T(8,128)(2,1)S(1)}, u32[]{:S(2)}) copy-start(bf16[304,768]{1,0:T(8,128)(2,1)S(1)} %collective-permute-done.3.rest_0_) | copy-start | bytes 1400836
  165.7 14.3 %collective-permute-start.11 = (bf16[304,768]{1,0:T(8,128)(2,1)S(1)}, bf16[304,768]{1,0:T(8,128)(2,1)S(1)}, u32[]{:S(2)}, u32[]{:S(2)}) collective-permute-start(bf16[304,768]{1,0:T(8,128)(2,1)S(1)} %collective-permute-done.9.rest_1_), channel_id=1, source_target_pairs={{0,1},{1,0},{2,3},{3,2},{4,5},{5,4},{6,7},{7,6},{8,9},{9,8},{10,11... | collective-permute-start | bytes 1400840 | tf_op jit(solution)/shard_map/ppermute | solution.py:898
  204.5 30.8 %copy-start.40 = (s32[6]{0:T(128)S(1)}, s32[6]{0:T(128)}, u32[]{:S(2)}) copy-start(s32[6]{0:T(128)} %copy-done.39) | copy-start | bytes 76
  204.5 27.1 %collective-permute-start.13 = (bf16[384,1152]{1,0:T(8,128)(2,1)}, bf16[384,1152]{1,0:T(8,128)(2,1)S(1)}, u32[]{:S(2)}, u32[]{:S(2)}) collective-permute-start(bf16[384,1152]{1,0:T(8,128)(2,1)} %get-tuple-element.114), channel_id=1, source_target_pairs={{0,1},{1,0},{2,3},{3,2},{4,5},{5,4},{6,7},{7,6},{8,9},{9,8},{10,11... | collective-permute-start | bytes 2654216 | tf_op jit(solution)/shard_map/ppermute | solution.py:898
  231.6 24.7 %all-to-all-start = ((bf16[4,288,384]{2,1,0:T(8,128)(2,1)}), bf16[4,288,384]{2,1,0:T(8,128)(2,1)S(1)}, u32[]{:S(2)}, u32[]{:S(2)}) async-start(bf16[4,288,384]{2,1,0:T(8,128)(2,1)} %get-tuple-element.134), calls=%async_computation | async-start | bytes 1769472 | tf_op jit(solution)/shard_map/all_to_all | solution.py:901
  247.2 14.9 %collective-permute-start.14 = (bf16[2,288,384]{2,1,0:T(8,128)(2,1)S(1)}, bf16[2,288,384]{2,1,0:T(8,128)(2,1)S(1)}, u32[]{:S(2)}, u32[]{:S(2)}) collective-permute-start(bf16[2,288,384]{2,1,0:T(8,128)(2,1)S(1)} %dynamic-slice_bitcast_fusion.2), channel_id=1, source_target_pairs={{0,1},{1,0},{2,3},{3,2},{4,5},{5,4},{6,7},{7,6},{8,9},{9,8},{10,11... | collective-permute-start | bytes 1327112 | tf_op jit(solution)/shard_map/ppermute | solution.py:898
  256.3 27.9 %all-to-all-start.1 = ((bf16[4,288,384]{2,1,0:T(8,128)(2,1)}), bf16[4,288,384]{2,1,0:T(8,128)(2,1)S(1)}, u32[]{:S(2)}, u32[]{:S(2)}) async-start(bf16[4,288,384]{2,1,0:T(8,128)(2,1)} %get-tuple-element.143), calls=%async_computation.1 | async-start | bytes 1769472 | tf_op jit(solution)/shard_map/all_to_all | solution.py:901
  259.8 102.7 %all-gather.6.cloned.1.call-start = ((), (), s32[]{:S(2)}) async-start(), calls=%async_computation.3 | async-start | bytes 4423680 | tf_op jit(solution)/shard_map/all_gather | solution.py:1101
  266.5 10.6 %copy-start.38 = (bf16[32,1280]{1,0:T(8,128)(2,1)S(1)}, bf16[32,1280]{1,0:T(8,128)(2,1)}, u32[]{:S(2)}) copy-start(bf16[32,1280]{1,0:T(8,128)(2,1)} %copy-done.37) | copy-start | bytes 245764
  266.5 10.7 %copy-start.64 = (bf16[32,1280]{1,0:T(8,128)(2,1)S(1)}, bf16[32,1280]{1,0:T(8,128)(2,1)}, u32[]{:S(2)}) copy-start(bf16[32,1280]{1,0:T(8,128)(2,1)} %get-tuple-element.138) | copy-start | bytes 245764
  266.5 10.7 %copy-start.65 = (bf16[32,1280]{1,0:T(8,128)(2,1)S(1)}, bf16[32,1280]{1,0:T(8,128)(2,1)}, u32[]{:S(2)}) copy-start(bf16[32,1280]{1,0:T(8,128)(2,1)} %get-tuple-element.139) | copy-start | bytes 245764
  266.5 14.8 %copy-start.61 = (bf16[2,32,1280]{2,1,0:T(8,128)(2,1)S(1)}, bf16[2,32,1280]{2,1,0:T(8,128)(2,1)}, u32[]{:S(2)}) copy-start(bf16[2,32,1280]{2,1,0:T(8,128)(2,1)} %get-tuple-element.140) | copy-start | bytes 491524
  266.5 14.8 %copy-start.62 = (bf16[2,32,1280]{2,1,0:T(8,128)(2,1)S(1)}, bf16[2,32,1280]{2,1,0:T(8,128)(2,1)}, u32[]{:S(2)}) copy-start(bf16[2,32,1280]{2,1,0:T(8,128)(2,1)} %get-tuple-element.141) | copy-start | bytes 491524
  277.2 7.1 %copy-start.54 = (bf16[16,1280]{1,0:T(8,128)(2,1)}, bf16[16,1280]{1,0:T(8,128)(2,1)S(1)}, u32[]{:S(2)}) copy-start(bf16[16,1280]{1,0:T(8,128)(2,1)S(1)} %get-tuple-element.180) | copy-start | bytes 122884
  277.2 7.1 %copy-start.56 = (bf16[16,1280]{1,0:T(8,128)(2,1)}, bf16[16,1280]{1,0:T(8,128)(2,1)S(1)}, u32[]{:S(2)}) copy-start(bf16[16,1280]{1,0:T(8,128)(2,1)S(1)} %get-tuple-element.181) | copy-start | bytes 122884
  277.9 21.3 %collective-permute-start.15 = (bf16[64,1280]{1,0:T(8,128)(2,1)}, bf16[64,1280]{1,0:T(8,128)(2,1)}, u32[]{:S(2)}, u32[]{:S(2)}) collective-permute-start(bf16[64,1280]{1,0:T(8,128)(2,1)} %pad_maximum_fusion.10), channel_id=1, source_target_pairs={{0,1},{1,0},{2,3},{3,2},{4,5},{5,4},{6,7},{7,6},{8,9},{9,8},{10,11... | collective-permute-start | bytes 491528 | tf_op jit(solution)/shard_map/ppermute | solution.py:898
  277.9 22.4 %collective-permute-start.17 = (bf16[64,1280]{1,0:T(8,128)(2,1)}, bf16[64,1280]{1,0:T(8,128)(2,1)}, u32[]{:S(2)}, u32[]{:S(2)}) collective-permute-start(bf16[64,1280]{1,0:T(8,128)(2,1)} %pad_maximum_fusion.10), channel_id=1, source_target_pairs={{0,3},{1,2},{2,1},{3,0},{4,7},{5,6},{6,5},{7,4},{8,11},{9,10},{10,... | collective-permute-start | bytes 491528 | tf_op jit(solution)/shard_map/ppermute | solution.py:898
  285.2 15.2 %collective-permute-start.16 = (bf16[96,1280]{1,0:T(8,128)(2,1)}, bf16[96,1280]{1,0:T(8,128)(2,1)S(1)}, u32[]{:S(2)}, u32[]{:S(2)}) collective-permute-start(bf16[96,1280]{1,0:T(8,128)(2,1)} %pad_maximum_fusion.8), channel_id=1, source_target_pairs={{0,2},{1,3},{2,0},{3,1},{4,6},{5,7},{6,4},{7,5},{8,10},{9,11},{10,... | collective-permute-start | bytes 737288 | tf_op jit(solution)/shard_map/ppermute | solution.py:898
  288.7 10.5 %copy-start.50 = (bf16[32,1280]{1,0:T(8,128)(2,1)S(1)}, bf16[32,1280]{1,0:T(8,128)(2,1)}, u32[]{:S(2)}) copy-start(bf16[32,1280]{1,0:T(8,128)(2,1)} %copy-done.49) | copy-start | bytes 245764
  288.8 10.5 %copy-start.55 = (bf16[16,1280]{1,0:T(8,128)(2,1)S(1)}, bf16[16,1280]{1,0:T(8,128)(2,1)}, u32[]{:S(2)}) copy-start(bf16[16,1280]{1,0:T(8,128)(2,1)} %copy-done.54) | copy-start | bytes 122884
  288.8 10.5 %copy-start.57 = (bf16[16,1280]{1,0:T(8,128)(2,1)S(1)}, bf16[16,1280]{1,0:T(8,128)(2,1)}, u32[]{:S(2)}) copy-start(bf16[16,1280]{1,0:T(8,128)(2,1)} %copy-done.56) | copy-start | bytes 122884
  288.8 11.5 %copy-start.60 = (bf16[32,1280]{1,0:T(8,128)(2,1)S(1)}, bf16[32,1280]{1,0:T(8,128)(2,1)}, u32[]{:S(2)}) copy-start(bf16[32,1280]{1,0:T(8,128)(2,1)} %get-tuple-element.174) | copy-start | bytes 245764
  306.1 16.9 %collective-permute-start.20 = (bf16[48,1280]{1,0:T(8,128)(2,1)S(1)}, bf16[48,1280]{1,0:T(8,128)(2,1)S(1)}, u32[]{:S(2)}, u32[]{:S(2)}) collective-permute-start(bf16[48,1280]{1,0:T(8,128)(2,1)S(1)} %get-tuple-element.153), channel_id=1, source_target_pairs={{0,3},{1,2},{2,1},{3,0},{4,7},{5,6},{6,5},{7,4},{8,11},{9,10},{10,... | collective-permute-start | bytes 368648 | tf_op jit(solution)/shard_map/ppermute | solution.py:898
  308.0 14.8 %collective-permute-start.18 = (bf16[48,1280]{1,0:T(8,128)(2,1)S(1)}, bf16[48,1280]{1,0:T(8,128)(2,1)S(1)}, u32[]{:S(2)}, u32[]{:S(2)}) collective-permute-start(bf16[48,1280]{1,0:T(8,128)(2,1)S(1)} %get-tuple-element.153), channel_id=1, source_target_pairs={{0,1},{1,0},{2,3},{3,2},{4,5},{5,4},{6,7},{7,6},{8,9},{9,8},{10,11... | collective-permute-start | bytes 368648 | tf_op jit(solution)/shard_map/ppermute | solution.py:898
  309.6 13.3 %collective-permute-start.19 = (bf16[64,1280]{1,0:T(8,128)(2,1)S(1)}, bf16[64,1280]{1,0:T(8,128)(2,1)S(1)}, u32[]{:S(2)}, u32[]{:S(2)}) collective-permute-start(bf16[64,1280]{1,0:T(8,128)(2,1)S(1)} %pad_maximum_fusion.11), channel_id=1, source_target_pairs={{0,2},{1,3},{2,0},{3,1},{4,6},{5,7},{6,4},{7,5},{8,10},{9,11},{10,... | collective-permute-start | bytes 491528 | tf_op jit(solution)/shard_map/ppermute | solution.py:898
  323.1 50.9 %all-to-all-start.2 = ((bf16[4,304,768]{2,1,0:T(8,128)(2,1)}), bf16[4,304,768]{2,1,0:T(8,128)(2,1)}, u32[]{:S(2)}, u32[]{:S(2)}) async-start(bf16[4,304,768]{2,1,0:T(8,128)(2,1)} %norm_back.1), calls=%async_computation.2 | async-start | bytes 3735552 | tf_op jit(solution)/shard_map/all_to_all | solution.py:901
  327.8 17.7 %collective-permute-start.23 = (bf16[2,64,1280]{2,1,0:T(8,128)(2,1)S(1)}, bf16[2,64,1280]{2,1,0:T(8,128)(2,1)S(1)}, u32[]{:S(2)}, u32[]{:S(2)}) collective-permute-start(bf16[2,64,1280]{2,1,0:T(8,128)(2,1)S(1)} %pad_maximum_fusion.7), channel_id=1, source_target_pairs={{0,24},{4,28},{8,16},{12,20},{16,8},{20,12},{24,0},{28,4},{1,25},{... | collective-permute-start | bytes 983048 | tf_op jit(solution)/shard_map/ppermute | solution.py:912
  329.8 20.4 %collective-permute-start.22 = (bf16[2,64,1280]{2,1,0:T(8,128)(2,1)S(1)}, bf16[2,64,1280]{2,1,0:T(8,128)(2,1)S(1)}, u32[]{:S(2)}, u32[]{:S(2)}) collective-permute-start(bf16[2,64,1280]{2,1,0:T(8,128)(2,1)S(1)} %pad_maximum_fusion.7), channel_id=1, source_target_pairs={{0,16},{4,20},{8,24},{12,28},{16,0},{20,4},{24,8},{28,12},{1,17},{... | collective-permute-start | bytes 983048 | tf_op jit(solution)/shard_map/ppermute | solution.py:912
  330.3 19.9 %collective-permute-start.21 = (bf16[2,64,1280]{2,1,0:T(8,128)(2,1)S(1)}, bf16[2,64,1280]{2,1,0:T(8,128)(2,1)S(1)}, u32[]{:S(2)}, u32[]{:S(2)}) collective-permute-start(bf16[2,64,1280]{2,1,0:T(8,128)(2,1)S(1)} %pad_maximum_fusion.7), channel_id=1, source_target_pairs={{0,8},{4,12},{8,0},{12,4},{16,24},{20,28},{24,16},{28,20},{1,9},{5... | collective-permute-start | bytes 983048 | tf_op jit(solution)/shard_map/ppermute | solution.py:912
  352.1 3.4 collective-permute-start.24
  (48 other events, 129.1 us)
Sparse Core Ops, SparseCore 0:
  10.9 82.4 all-gather.7
  123.3 40.6 all-gather.9
  302.3 48.9 all-gather.5
